TPU v7x, 512 devices: a whole 4x8x8 slice. The times are simulated.
512 devices in a mesh: wide: 128 (over z, y, core), narrow: 4 (over x).
Axes of the slice: x: 4, y: 8, z: 8, core: 2. Of those that a mesh axis runs over, the one named last changes fastest.
Arguments:
- features: bfloat16 [32768, 512], P('wide', 'narrow'), may hold values from -6 to 6
- tile_blocks: bfloat16 [128, 4, 48, 128, 128], P('wide', 'narrow'), may hold values from -0.078125 to 0.078125
- tile_rows: int32 [128, 4, 48], P('wide', 'narrow'), may hold values from 0 to 1
- tile_cols: int32 [128, 4, 48], P('wide', 'narrow'), may hold values from 0 to 63, as said below
- tile_count: int32 [128, 4], P('wide', 'narrow'), may hold values from 12 to 48, as said below
- neighbor_weight: bfloat16 [512, 512], P('narrow'), may hold values from -0.25 to 0.25
- root_weight: bfloat16 [512, 512], P('narrow'), may hold values from -0.25 to 0.25
- output_weight: bfloat16 [512, 512], replicated, may hold values from -0.25 to 0.25
- cotangent: bfloat16 [32768, 512], P('wide'), may hold values from -0.078125 to 0.078125
Outputs:
- layer_output: bfloat16 [32768, 512], P('wide', 'narrow')
- neighbor_grad: float32 [512, 512], P('narrow')
- root_grad: float32 [512, 512], P('narrow')
- output_grad: float32 [512, 512], P(None, 'narrow')
Inputs may be any that keep to these rules, and one draw needn't show every extreme that they name: `tile_count`: slots at or past a device's count hold no tiles and are ignored; the largest count is 48 on some device in every draw, the smallest max(1, 12) on another. `tile_cols`: positions may repeat; repeated tiles add. Slot 0 of every device of row block b names the column tile that holds the nodes of row block b + 128 // 2 (counted round).
All inputs are finite; a program needn't handle non-finite values.
Results may differ from a plain program's by a relative error of at most 0.015.
Values may be sent and summed in bfloat16 or wider, within the bound.
No kernel may reach another device: no remote copies, remote signals or barrier semaphores. Data moves between devices by JAX's collectives and lax.ppermute only.
A program may use at most 64 MiB of HBM per device.

v0:
```python
import math

import jax
import jax.numpy as jnp
from jax import lax
from jax.sharding import PartitionSpec as P


def tile_sum(block_tiles, row_ids, col_ids, live_count, column_tiles, tile_rows_count):
    capacity = block_tiles.shape[0]
    block_size = math.gcd(capacity, 24)
    tile_side = block_tiles.shape[-1]
    feature_width = column_tiles.shape[-1]
    row_range = jnp.arange(tile_rows_count, dtype=jnp.int32)
    slot_range = jnp.arange(block_size, dtype=jnp.int32)

    def one_turn(turn_index, running):
        first_slot = turn_index * block_size
        some_tiles = lax.dynamic_slice_in_dim(block_tiles, first_slot, block_size, 0)
        some_rows = lax.dynamic_slice_in_dim(row_ids, first_slot, block_size, 0)
        some_cols = lax.dynamic_slice_in_dim(col_ids, first_slot, block_size, 0)
        picked = column_tiles[some_cols]
        product = jnp.einsum("tij,tjh->tih", some_tiles, picked, preferred_element_type=jnp.float32)
        alive = (first_slot + slot_range < live_count).astype(jnp.float32)
        placing = alive[:, None] * (some_rows[:, None] == row_range[None, :]).astype(jnp.float32)
        return running + jnp.einsum("tr,tih->rih", placing, product)

    block_turns = (live_count + block_size - 1) // block_size
    start_value = jnp.zeros((tile_rows_count, tile_side, feature_width), jnp.float32)
    summed = lax.fori_loop(0, block_turns, one_turn, start_value)
    return summed.reshape(tile_rows_count * tile_side, feature_width)


def per_device(
    features,
    tile_blocks,
    tile_rows,
    tile_cols,
    tile_count,
    neighbor_weight,
    root_weight,
    output_weight,
    cotangent,
):
    node_rows = features.shape[0]
    slice_width = features.shape[1]
    wide_count = lax.axis_size("wide")
    narrow_count = lax.axis_size("narrow")
    tile_side = tile_blocks.shape[-1]
    tile_rows_count = node_rows // tile_side
    group_rows = node_rows // narrow_count
    all_tiles, all_rows, all_cols, all_counts = (
        lax.all_gather(tile_blocks, "narrow", axis=1, tiled=True),
        lax.all_gather(tile_rows, "narrow", axis=1, tiled=True),
        lax.all_gather(tile_cols, "narrow", axis=1, tiled=True),
        lax.all_gather(tile_count, "narrow", axis=1, tiled=True),
    )
    columns = lax.all_gather(features, "wide", axis=0, tiled=True)
    groups = columns.reshape(wide_count, narrow_count, group_rows, slice_width).transpose(
        1, 0, 2, 3
    )
    groups = groups.reshape(narrow_count, -1, tile_side, slice_width)
    running = jnp.zeros((node_rows, slice_width), jnp.float32)
    for source in range(narrow_count):
        running = running + tile_sum(
            all_tiles[0, source],
            all_rows[0, source],
            all_cols[0, source],
            all_counts[0, source],
            groups[source],
            tile_rows_count,
        )
    agg = running.astype(jnp.bfloat16)
    partial_pre = jnp.dot(agg, neighbor_weight, preferred_element_type=jnp.float32) + jnp.dot(
        features, root_weight, preferred_element_type=jnp.float32
    )
    pre = lax.psum(partial_pre, "narrow")
    hidden = jax.nn.silu(pre).astype(jnp.bfloat16)
    narrow_index = lax.axis_index("narrow")
    out_columns = lax.dynamic_slice_in_dim(
        output_weight, narrow_index * slice_width, slice_width, 1
    )
    layer_output = (
        features.astype(jnp.float32)
        + jnp.dot(hidden, out_columns, preferred_element_type=jnp.float32)
    ).astype(jnp.bfloat16)
    hidden_grad = jnp.dot(cotangent, output_weight.T, preferred_element_type=jnp.float32)
    sigmoid_pre = jax.nn.sigmoid(pre)
    pre_grad = (hidden_grad * sigmoid_pre * (1.0 + pre * (1.0 - sigmoid_pre))).astype(jnp.bfloat16)
    cot_columns = lax.dynamic_slice_in_dim(cotangent, narrow_index * slice_width, slice_width, 1)
    neighbor_part = jnp.dot(agg.T, pre_grad, preferred_element_type=jnp.float32)
    root_part = jnp.dot(features.T, pre_grad, preferred_element_type=jnp.float32)
    output_part = jnp.dot(hidden.T, cot_columns, preferred_element_type=jnp.float32)
    neighbor_grad, root_grad, output_grad = lax.psum(
        (neighbor_part, root_part, output_part), "wide"
    )
    return (layer_output, neighbor_grad, root_grad, output_grad)


def solution(mesh):
    return jax.shard_map(
        per_device,
        mesh=mesh,
        in_specs=(
            P("wide", "narrow"),
            P("wide", "narrow", None, None, None),
            P("wide", "narrow", None),
            P("wide", "narrow", None),
            P("wide", "narrow"),
            P("narrow", None),
            P("narrow", None),
            P(),
            P("wide", None),
        ),
        out_specs=(P("wide", "narrow"), P("narrow", None), P("narrow", None), P(None, "narrow")),
        check_vma=False,
    )
```

profile of v0, /device:TPU:1, one launch (start us, length us, event | category | flops | bytes accessed | tf_op | source)
XLA Modules:
  0.0 500.8 jit_solution(12524197187598778538)
XLA Ops:
  9.4 1.3 dynamic-slice
  11.3 7.7 %all-reduce = s32[4]{0:T(128)S(1)} all-reduce(s32[4]{0:T(128)S(1)} %bitcast_dynamic-update-slice_fusion), channel_id=1, replica_groups=mesh['wide'=128,'narrow'=4] {'narrow'}, use_global_device_ids=true, to_apply=%add | all-reduce | flops 4 | bytes 32
  22.3 6.2 %all_gather.16 = s32[1,4,48]{2,0,1:T(1,128)S(1)} all-gather(s32[1,1,48]{2,0,1:T(1,128)} %bitcast.100), channel_id=1, replica_groups=mesh['wide'=128,'narrow'=4] {'narrow'}, dimensions={1}, use_global_device_ids=true | all-gather | bytes 960 | tf_op jit(solution)/shard_map/all_gather | solution.py:54
  28.5 5.9 %all_gather.18 = s32[1,4,48]{2,0,1:T(1,128)S(1)} all-gather(s32[1,1,48]{2,0,1:T(1,128)} %bitcast.101), channel_id=1, replica_groups=mesh['wide'=128,'narrow'=4] {'narrow'}, dimensions={1}, use_global_device_ids=true | all-gather | bytes 960 | tf_op jit(solution)/shard_map/all_gather | solution.py:55
  34.4 52.2 %all-gather.3.cloned.1.call-done = bf16[1,4,48,128,128]{4,3,2,0,1:T(8,128)(2,1)} async-done(((bf16[1,1,48,128,128]{4,3,2,0,1:T(8,128)(2,1)}), bf16[1,4,48,128,128]{4,3,2,0,1:T(8,128)(2,1)}) %all-gather.3.cloned.1.call-update) | async-done | bytes 6291472 | tf_op jit(solution)/shard_map/all_gather | solution.py:53
  86.6 6.2 %slice_bitcast_fusion.3 = (bf16[48,128,128]{2,1,0:T(8,128)(2,1)}, bf16[48,128,128]{2,1,0:T(8,128)(2,1)S(1)}, bf16[48,128,128]{2,1,0:T(8,128)(2,1)}, bf16[48,128,128]{2,1,0:T(8,128)(2,1)}) fusion(bf16[1,4,48,128,128]{4,3,2,0,1:T(8,128)(2,1)} %all-gather.3.cloned.1.call-done), kind=kLoop, calls=%fused_computation.84 | loop fusion | bytes 12582912 | tf_op jit(solution)/shard_map/squeeze | solution.py:66
  92.8 86.2 %all-gather.5.cloned.1.call-done = bf16[32768,128]{1,0:T(8,128)(2,1)} async-done(((bf16[256,128]{1,0:T(8,128)(2,1)}), bf16[32768,128]{1,0:T(8,128)(2,1)}) %all-gather.5.cloned.1.call-update) | async-done | bytes 8388624 | tf_op jit(solution)/shard_map/all_gather | solution.py:58
  179.1 9.4 %copy.61 = bf16[128,4,64,128]{3,2,0,1:T(8,128)(2,1)} copy(bf16[128,4,64,128]{3,2,1,0:T(8,128)(2,1)} %bitcast.95) | data formatting | bytes 16777216 | tf_op jit(solution)/shard_map/reshape | solution.py:59
  188.5 6.3 %fusion.85 = (bf16[1,128,64,128]{3,2,1,0:T(8,128)(2,1)}, bf16[1,128,64,128]{3,2,1,0:T(8,128)(2,1)}, bf16[1,128,64,128]{3,2,1,0:T(8,128)(2,1)}, bf16[1,128,64,128]{3,2,1,0:T(8,128)(2,1)}) fusion(bf16[4,128,64,128]{3,2,1,0:T(8,128)(2,1)} %bitcast.90), kind=kLoop, calls=%fused_computation.112 | loop fusion | bytes 16777216 | tf_op jit(solution)/shard_map/slice | solution.py:70
  194.8 5.5 %while.44 = (s32[]{:T(128)}, f32[2,128,128]{2,0,1:T(2,128)S(1)}, s32[]{:T(128)}, s32[48]{0:T(128)S(1)}, s32[]{:T(128)}, /*index=5*/bf16[48,128,128]{2,1,0:T(8,12...) while((s32[]{:T(128)}, f32[2,128,128]{2,0,1:T(2,128)S(1)}, ...), condition=%wide.region_1.2_spmd.clone, body=%wide.region_0.1_spmd.clone.sunk | while | flops 102270200 | bytes 4985783 | solution.py:30
  194.9 2.3 gather_fusion
  197.2 1.5 fusion.133
  200.3 10.9 %while.45 = (s32[]{:T(128)}, f32[2,128,128]{2,0,1:T(2,128)S(1)}, s32[]{:T(128)}, s32[48]{0:T(128)S(1)}, s32[]{:T(128)}, /*index=5*/bf16[48,128,128]{2,1,0:T(8,12...) while((s32[]{:T(128)}, f32[2,128,128]{2,0,1:T(2,128)S(1)}, ...), condition=%wide.region_3.4_spmd.clone, body=%wide.region_2.3_spmd.clone.sunk | while | flops 102270200 | bytes 4985783 | solution.py:30
  200.5 2.3 gather_fusion.1
  202.8 1.5 fusion.139
  205.9 2.3 gather_fusion.1
  208.2 1.5 fusion.139
  211.3 11.0 %while.46 = (s32[]{:T(128)}, f32[2,128,128]{2,0,1:T(2,128)S(1)}, s32[]{:T(128)}, s32[48]{0:T(128)S(1)}, s32[]{:T(128)}, /*index=5*/bf16[48,128,128]{2,1,0:T(8,12...) while((s32[]{:T(128)}, f32[2,128,128]{2,0,1:T(2,128)S(1)}, ...), condition=%wide.region_5.6_spmd.clone, body=%wide.region_4.5_spmd.clone.sunk | while | flops 102270200 | bytes 4985783 | solution.py:30
  211.4 2.3 gather_fusion.2
  213.7 1.5 fusion.145
  216.9 2.3 gather_fusion.2
  219.2 1.5 fusion.145
  222.4 8.7 %while.47 = (s32[]{:T(128)}, f32[2,128,128]{2,0,1:T(2,128)S(1)}, s32[]{:T(128)}, s32[48]{0:T(128)S(1)}, s32[]{:T(128)}, /*index=5*/bf16[48,128,128]{2,1,0:T(8,12...) while((s32[]{:T(128)}, f32[2,128,128]{2,0,1:T(2,128)S(1)}, ...), condition=%wide.region_7.8_spmd.clone, body=%wide.region_6.7_spmd.clone.sunk | while | flops 102270200 | bytes 4985783 | solution.py:30
  222.5 2.3 gather_fusion.3
  226.8 2.3 gather_fusion.3
  232.3 1.9 convolution_add_fusion
  234.3 53.1 %all-reduce.5.cloned.1.call-done = f32[256,512]{1,0:T(8,128)} async-done(((f32[256,512]{1,0:T(8,128)}), f32[256,512]{1,0:T(8,128)}) %all-reduce.5.cloned.1.call-update) | async-done | bytes 524304 | tf_op jit(solution)/shard_map/psum | solution.py:77
  287.4 1.5 fusion.77
  292.8 196.4 %all-reduce.7.cloned.1.call-done = (f32[128,512]{1,0:T(8,128)}, f32[128,512]{0,1:T(8,128)}, f32[512,128]{1,0:T(8,128)}) async-done(((f32[128,512]{1,0:T(8,128)}, f32[128,512]{0,1:T(8,128)}, f32[512,128]{1,0:T(8,128)}), (f32[128,512]{1,0:T(8,128)}, f32[128,512]{0,1:T(8,128)}, f32[512,128]{1,0:T(8,128)})) %all-reduce.7.cloned.1.call-update) | async-done | bytes 786448 | tf_op jit(solution)/shard_map/psum | solution.py:94
  489.2 1.8 copy.33
  491.0 1.7 copy.100
  492.6 1.7 copy.101
  (69 shorter events, 20.3 us)
Async XLA Ops:
  7.2 280.2 %copy-start = (bf16[512,512]{1,0:T(8,128)(2,1)S(1)}, bf16[512,512]{1,0:T(8,128)(2,1)}, u32[]{:S(2)}) copy-start(bf16[512,512]{1,0:T(8,128)(2,1)} %param.24) | copy-start | bytes 1572868
  7.2 79.5 %all-gather.3.cloned.1.call-start = ((), (), s32[]{:S(2)}) async-start(), calls=%async_computation | async-start | bytes 7864320 | tf_op jit(solution)/shard_map/all_gather | solution.py:53
  7.9 171.2 %all-gather.5.cloned.1.call-start = ((), (), s32[]{:S(2)}) async-start(), calls=%async_computation.1 | async-start | bytes 8454144 | tf_op jit(solution)/shard_map/all_gather | solution.py:58
  8.7 278.7 %all-reduce.5.cloned.1.call-start = ((), (), s32[]{:S(2)}) async-start(), calls=%async_computation.2 | async-start | bytes 1048576 | tf_op jit(solution)/shard_map/psum | solution.py:77
  222.3 9.9 %copy-start.1 = (bf16[256,128]{1,0:T(8,128)(2,1)S(1)}, bf16[256,128]{1,0:T(8,128)(2,1)}, u32[]{:S(2)}) copy-start(bf16[256,128]{1,0:T(8,128)(2,1)} %param.17) | copy-start | bytes 196612
  231.1 56.3 %copy-start.3 = (bf16[256,512]{1,0:T(8,128)(2,1)S(1)}, bf16[256,512]{1,0:T(8,128)(2,1)}, u32[]{:S(2)}) copy-start(bf16[256,512]{1,0:T(8,128)(2,1)} %param.25) | copy-start | bytes 786436
  234.2 255.0 %all-reduce.7.cloned.1.call-start = ((), (), s32[]{:S(2)}) async-start(), calls=%async_computation.3 | async-start | bytes 1572864 | tf_op jit(solution)/shard_map/psum | solution.py:94
  287.4 3.4 copy-start.2
Sparse Core Ops, SparseCore 0:
  10.1 76.4 all-gather.2
  89.8 89.2 all-gather.4
  234.3 52.9 all-reduce.4
  292.1 197.0 all-reduce.6
where the time goes:
time: 503 us; the launch traced here: 501 us
  waiting for transfers between devices  389 us (77%)
  local copies, waits for them, and re-layouts  46.3 us (9%)
  matrix products  22.3 us (4%)
  blocking collectives  19.9 us (4%)
  between operations  17.2 us (3%)
  other arithmetic  5.29 us (1%)
    psum x1, waiting for transfers between devices, per_device(): lax.psum((neighbor_part, root_part, output_part), 'wide')  196 us
    all_gather x1, waiting for transfers between devices, per_device(): columns = lax.all_gather(features, 'wide', axis=0, tiled=True)  86.2 us
    psum x1, waiting for transfers between devices, per_device(): pre = lax.psum(partial_pre, 'narrow')  53.1 us
    all_gather x1, waiting for transfers between devices, per_device(): lax.all_gather(tile_blocks, 'narrow', axis=1, tiled=True)  52.2 us
    gather x7, local copies, waits for them, and re-layouts, one_turn(): picked = column_tiles[some_cols]  16 us
  transfers between devices with their start and end apart: 4, of which 4 were waited for; matrix products, arithmetic and copies ran while one was open for 2% of the time, Pallas kernels for 0%

commit v1 on v0

v1 whole, which is shorter than its diff:
```python
import functools

import jax
import jax.numpy as jnp
from jax import lax
from jax.experimental import pallas as pl
from jax.experimental.pallas import tpu as pltpu
from jax.sharding import PartitionSpec as P

AXES = ("wide", "narrow")
NZ, NY, NC, NN = 8, 8, 2, 4
VMEM = pl.BlockSpec(memory_space=pltpu.VMEM)
SMEM = pl.BlockSpec(memory_space=pltpu.SMEM)
BIG = pltpu.CompilerParams(vmem_limit_bytes=48 * 1024 * 1024)
F32, BF16 = jnp.float32, jnp.bfloat16


def places():
    for z in range(NZ):
        for y in range(NY):
            for c in range(NC):
                for n in range(NN):
                    yield z, y, c, n


def device(z, y, c, n):
    return ((z * NY + y) * NC + c) * NN + n


def groups(key):
    found = {}
    for place in places():
        found.setdefault(key(*place), []).append(device(*place))
    return list(found.values())


FIRST = groups(lambda z, y, c, n: (0, y) if c == 0 else (1, z))
SECOND = groups(lambda z, y, c, n: (c, z, n) if c == 0 else (c, y, n))
OVER_X = groups(lambda z, y, c, n: (z, y, c))
OVER_ZC = groups(lambda z, y, c, n: (y, n))
OVER_Y = groups(lambda z, y, c, n: (z, c, n))
OTHER_CORE = [(device(z, y, c, n), device(z, y, 1 - c, n)) for z, y, c, n in places()]


def exchange(pieces, groups_):
    return lax.all_to_all(pieces, AXES, 0, 0, axis_index_groups=groups_, tiled=True)


def share(piece, count, groups_):
    return exchange(jnp.broadcast_to(piece[None], (count, *piece.shape)), groups_)


def swap_cores(value):
    return lax.ppermute(value, AXES, OTHER_CORE)


def place_kernel(s_ref, own_ref, other_ref, lo_ref, lt_ref):
    slots = own_ref.shape[0]
    core = s_ref[4 * slots + 2]
    first = core == 0
    low = lax.broadcasted_iota(jnp.int32, own_ref.shape[1:], 1) < own_ref.shape[2] // 2
    half = own_ref.shape[2] // 2
    for block, (t_ref, l_ref) in enumerate(((own_ref, lo_ref), (other_ref, lt_ref))):
        base = 2 * slots * block
        count = s_ref[4 * slots + block]

        def one_pair(p, carry, t_ref=t_ref, l_ref=l_ref, base=base, count=count):
            a = t_ref[2 * p].astype(F32)
            b = t_ref[2 * p + 1].astype(F32)
            moved = pltpu.roll(jnp.where(first, b, a), half, 1)
            both = jnp.where(low, jnp.where(first, a, moved), jnp.where(first, moved, b))
            row_a, row_b = s_ref[base + 2 * p], s_ref[base + 2 * p + 1]
            row_a = jnp.where(2 * p < count, row_a, -1)
            row_b = jnp.where(2 * p + 1 < count, row_b, -1)
            rows = jnp.where(low, row_a, row_b)
            side = both.shape[0]
            for r in range(2):
                l_ref[p, r * side:(r + 1) * side, :] = jnp.where(rows == r, both, 0.0).astype(BF16)
            return carry

        lax.fori_loop(0, slots // 2, one_pair, 0)


def sum_kernel(s_ref, lo_ref, lt_ref, g_ref, po_ref, pt_ref, acc):
    slots = 2 * lo_ref.shape[0]
    step = 8
    for block, (l_ref, p_ref) in enumerate(((lo_ref, po_ref), (lt_ref, pt_ref))):
        base = 2 * slots * block + slots
        count = s_ref[4 * slots + block]
        acc[...] = jnp.zeros_like(acc)

        def one_turn(i, carry, l_ref=l_ref, base=base):
            left = jnp.concatenate([l_ref[i * (step // 2) + k] for k in range(step // 2)], axis=1)
            spots = [s_ref[base + i * step + k] * NN for k in range(step)]
            right = jnp.concatenate(
                [jnp.concatenate([g_ref[spot + n] for spot in spots], axis=0) for n in range(NN)],
                axis=1,
            )
            acc[...] += jnp.dot(left, right, preferred_element_type=F32)
            return carry

        lax.fori_loop(0, (count + step - 1) // step, one_turn, 0)
        p_ref[...] = acc[...].astype(p_ref.dtype)


def early_kernel(w_ref, cot_ref, ow_ref, root_ref, hg_ref):
    width = w_ref.shape[2]
    side = width // NN
    quarter = w_ref.shape[1] - 2 * side
    root_weight = jnp.concatenate([w_ref[j, side:2 * side, :] for j in range(NN)], axis=0)
    for q in range(NN):
        rows = jnp.concatenate(
            [w_ref[j, 2 * side:, q * side:(q + 1) * side] for j in range(NN)], axis=1
        )
        root_ref[q * quarter:(q + 1) * quarter, :] = jnp.dot(
            rows, root_weight, preferred_element_type=F32
        )
    hg_ref[...] = lax.dot_general(
        cot_ref[...], ow_ref[...], (((1,), (1,)), ((), ())), preferred_element_type=F32
    )


def dense_kernel(n_ref, a_ref, w_ref, root_ref, hg_ref, f_ref, cot_ref, ow_ref, out_ref, g_ref, agg_ref):
    side = f_ref.shape[1]
    mine = pl.ds(pl.multiple_of(n_ref[0] * side, side), side)
    agg = a_ref[0].astype(F32)
    for j in range(1, NN):
        agg = agg + a_ref[j].astype(F32)
    agg = agg.astype(BF16)
    agg_ref[...] = agg
    weight = jnp.concatenate([w_ref[j, :side, :] for j in range(NN)], axis=0)
    pre = jnp.dot(agg, weight, preferred_element_type=F32) + root_ref[...]
    s = jax.nn.sigmoid(pre)
    hidden = (pre * s).astype(BF16)
    pre_grad = (hg_ref[...] * s * (1.0 + pre * (1.0 - s))).astype(BF16)
    over_rows = (((0,), (0,)), ((), ()))
    parts = (
        lax.dot_general(agg_ref[:, mine], pre_grad, over_rows, preferred_element_type=F32),
        lax.dot_general(f_ref[...], pre_grad, over_rows, preferred_element_type=F32),
    )
    for k, part in enumerate(parts):
        for j in range(NN):
            g_ref[k * NN + j] = part[:, j * side:(j + 1) * side].astype(BF16)
    part = lax.dot_general(hidden, cot_ref[:, mine], over_rows, preferred_element_type=F32)
    for j in range(NN):
        g_ref[2 * NN + j] = part[j * side:(j + 1) * side, :].astype(BF16)
    out_ref[...] = (
        f_ref[...].astype(F32) + jnp.dot(hidden, ow_ref[:, mine], preferred_element_type=F32)
    ).astype(BF16)


def total(pieces):
    return jnp.sum(pieces.astype(F32), axis=0).astype(BF16)


def per_device(
    features,
    tile_blocks,
    tile_rows,
    tile_cols,
    tile_count,
    neighbor_weight,
    root_weight,
    output_weight,
    cotangent,
):
    rows, side = features.shape
    quarter = rows // NN
    slots = tile_rows.shape[-1]
    core = lax.rem(lax.axis_index("wide"), NC)
    narrow = lax.axis_index("narrow")

    pieces = jnp.broadcast_to(
        features.reshape(1, NN, quarter, side), (NZ, NN, quarter, side)
    ).reshape(NZ * NN, quarter, side)
    line = exchange(pieces, FIRST)
    weights = jnp.concatenate(
        [
            neighbor_weight,
            root_weight,
            features.reshape(NN, quarter, side).swapaxes(0, 1).reshape(quarter, NN * side),
        ],
        axis=0,
    )
    tiles = tile_blocks[0, 0]
    numbers = jnp.concatenate([tile_rows[0, 0], tile_cols[0, 0], tile_count[0]])
    line, weights, tiles, numbers = lax.optimization_barrier((line, weights, tiles, numbers))
    plane = lax.all_gather(line, AXES, axis_index_groups=SECOND, axis=0, tiled=True)

    other_tiles = swap_cores(tiles)
    other_numbers = swap_cores(numbers)
    all_weights = share(weights, NN, OVER_X)

    def spot(cols):
        return jnp.where(core == 0, (cols % NY) * NZ + cols // NY, cols)

    scalars = jnp.concatenate(
        [
            numbers[:slots],
            spot(numbers[slots:2 * slots]),
            other_numbers[:slots],
            spot(other_numbers[slots:2 * slots]),
            numbers[2 * slots:],
            other_numbers[2 * slots:],
            core[None],
        ]
    ).astype(jnp.int32)
    placed = jax.ShapeDtypeStruct((slots // 2, rows, tiles.shape[-1]), BF16)
    left_own, left_other = pl.pallas_call(
        place_kernel,
        out_shape=(placed, placed),
        in_specs=[SMEM, VMEM, VMEM],
        out_specs=(VMEM, VMEM),
        compiler_params=BIG,
        cost_estimate=pl.CostEstimate(flops=10**6, bytes_accessed=6 * 10**6, transcendentals=0),
        name="place",
    )(scalars, tiles, other_tiles)
    width = NN * side
    whole = jax.ShapeDtypeStruct((rows, width), F32)
    root_part, hidden_grad = pl.pallas_call(
        early_kernel,
        out_shape=(whole, whole),
        in_specs=[VMEM, VMEM, VMEM],
        out_specs=(VMEM, VMEM),
        compiler_params=BIG,
        cost_estimate=pl.CostEstimate(
            flops=4 * rows * width * width, bytes_accessed=4 * 10**6, transcendentals=0
        ),
        name="early",
    )(all_weights.reshape(NN, *weights.shape), cotangent, output_weight)

    part_own, part_other = pl.pallas_call(
        sum_kernel,
        out_shape=(whole, jax.ShapeDtypeStruct((rows, width), BF16)),
        in_specs=[SMEM, VMEM, VMEM, VMEM],
        out_specs=(VMEM, VMEM),
        scratch_shapes=[pltpu.VMEM((rows, width), F32)],
        compiler_params=BIG,
        cost_estimate=pl.CostEstimate(
            flops=2 * slots * rows * quarter * width * 2, bytes_accessed=8 * 10**6, transcendentals=0
        ),
        name="sum",
    )(scalars, left_own, left_other, plane)
    block_part = (part_own + swap_cores(part_other).astype(F32)).astype(BF16)
    parts = share(block_part, NN, OVER_X)

    layer_output, grads = pl.pallas_call(
        dense_kernel,
        out_shape=(
            jax.ShapeDtypeStruct((rows, side), BF16),
            jax.ShapeDtypeStruct((3 * NN, side, side), BF16),
        ),
        in_specs=[SMEM] + [VMEM] * 7,
        out_specs=(VMEM, VMEM),
        scratch_shapes=[pltpu.VMEM((rows, width), BF16)],
        compiler_params=BIG,
        cost_estimate=pl.CostEstimate(
            flops=4 * rows * width * width, bytes_accessed=5 * 10**6, transcendentals=rows * width
        ),
        name="dense",
    )(
        narrow[None],
        parts.reshape(NN, rows, width),
        all_weights.reshape(NN, *weights.shape),
        root_part,
        hidden_grad,
        features,
        cotangent,
        output_weight,
    )

    chunk = 3 * NN * side // (NZ * NC)
    summed = total(exchange(grads.reshape(NZ * NC, chunk, side), OVER_ZC))
    summed = total(share(summed, NY, OVER_Y))
    full = share(summed, NZ * NC, OVER_ZC).reshape(3, NN, side, side).astype(F32)
    neighbor_grad, root_grad = (
        full[k].transpose(1, 0, 2).reshape(side, width) for k in range(2)
    )
    output_grad = full[2].reshape(width, side)
    return layer_output, neighbor_grad, root_grad, output_grad


def solution(mesh):
    return jax.shard_map(
        per_device,
        mesh=mesh,
        in_specs=(
            P("wide", "narrow"),
            P("wide", "narrow", None, None, None),
            P("wide", "narrow", None),
            P("wide", "narrow", None),
            P("wide", "narrow"),
            P("narrow", None),
            P("narrow", None),
            P(),
            P("wide", None),
        ),
        out_specs=(P("wide", "narrow"), P("narrow", None), P("narrow", None), P(None, "narrow")),
        check_vma=False,
    )
```

time: 503 us -> 178 us (0.35)
  waiting for transfers between devices: 389 us -> 43.1 us
  blocking collectives: 19.9 us -> 55.6 us
  starting transfers between devices: 0.16 us -> 33.1 us
  local copies, waits for them, and re-layouts: 46.3 us -> 18.2 us
  matrix products: 22.3 us -> 0 us
  Pallas kernels: 0 us -> 11.7 us
    psum x2 -> x0, waiting for transfers between devices: 249 us -> none  [the longest x1 196 us: per_device(): lax.psum((neighbor_part, root_part, output_part), 'wide')]
    all_gather x2 -> x1, waiting for transfers between devices: 138 us -> 17.9 us  [per_device(): lax.all_gather(line, AXES, axis_index_groups=SECOND, axis=0, tiled=True)]
    all_to_all x0 -> x3, blocking collectives: none -> 55.6 us  [exchange(): lax.all_to_all(pieces, AXES, 0, 0, axis_index_groups=groups_, tiled=True)]
    all_to_all x0 -> x3, waiting for transfers between devices: none -> 24.1 us  [exchange(): lax.all_to_all(pieces, AXES, 0, 0, axis_index_groups=groups_, tiled=True)]
    dot_general x21 -> x0, matrix products: 22.3 us -> none  [the longest x7 8.21 us: one_turn(): jnp.einsum('tij,tjh->tih', some_tiles, picked, preferred_element_type=jnp...]
    all_to_all x0 -> x3, starting transfers between devices: none -> 18.6 us  [exchange(): lax.all_to_all(pieces, AXES, 0, 0, axis_index_groups=groups_, tiled=True)]
    gather x7 -> x0, local copies, waits for them, and re-layouts: 16 us -> none  [one_turn(): picked = column_tiles[some_cols]]
    ppermute x0 -> x3, starting transfers between devices: none -> 14.4 us  [swap_cores(): return lax.ppermute(value, AXES, OTHER_CORE)]
  transfers between devices with their start and end apart: 4 -> 7, of which waited for: 4 -> 4; matrix products, arithmetic and copies ran while one was open for 2% -> 2% of each run, Pallas kernels for 0% -> 6%
where the time goes in v1:
time: 178 us; the launch traced here: 177 us
  blocking collectives  55.6 us (31%)
  waiting for transfers between devices  43.1 us (24%)
  starting transfers between devices  33.1 us (19%)
  local copies, waits for them, and re-layouts  18.2 us (10%)
  between operations  14.9 us (8%)
  Pallas kernels  11.7 us (7%)
    all_to_all x3, blocking collectives, exchange(): lax.all_to_all(pieces, AXES, 0, 0, axis_index_groups=groups_, tiled=True)  55.6 us
    all_to_all x3, waiting for transfers between devices, exchange(): lax.all_to_all(pieces, AXES, 0, 0, axis_index_groups=groups_, tiled=True)  24.1 us
    all_to_all x3, starting transfers between devices, exchange(): lax.all_to_all(pieces, AXES, 0, 0, axis_index_groups=groups_, tiled=True)  18.6 us
    all_gather x1, waiting for transfers between devices, per_device(): lax.all_gather(line, AXES, axis_index_groups=SECOND, axis=0, tiled=True)  17.9 us
    ppermute x3, starting transfers between devices, swap_cores(): return lax.ppermute(value, AXES, OTHER_CORE)  14.4 us
    unnamed x36, local copies, waits for them, and re-layouts  9.71 us
    pallas_call x1, Pallas kernels, per_device(): pl.pallas_call(place_kernel, out_shape=(placed, placed), in_specs=[SMEM,...  5.66 us
    pallas_call x1, Pallas kernels, per_device(): pl.pallas_call(sum_kernel, out_shape=(whole, jax.ShapeDtypeStruct((rows,...  3.86 us
  transfers between devices with their start and end apart: 7, of which 4 were waited for; matrix products, arithmetic and copies ran while one was open for 2% of the time, Pallas kernels for 6%

profile of v1, /device:TPU:1, one launch (start us, length us, event | category | flops | bytes accessed | tf_op | source)
XLA Modules:
  0.0 177.1 jit_solution(8133832482802641566)
XLA Ops:
  7.2 1.9 %broadcast_in_dim.18 = bf16[8,4,64,128]{3,2,1,0:T(8,128)(2,1)} broadcast(bf16[4,64,128]{2,1,0:T(8,128)(2,1)} %bitcast.34), dimensions={1,2,3} | broadcast | bytes 589824 | tf_op jit(solution)/shard_map/broadcast_in_dim | solution.py:173
  9.1 10.5 %all-to-all-start = ((bf16[32,64,128]{2,1,0:T(8,128)(2,1)}), bf16[32,64,128]{2,1,0:T(8,128)(2,1)S(1)}, u32[]{:S(2)}, u32[]{:S(2)}) async-start(bf16[32,64,128]{2,1,0:T(8,128)(2,1)} %bitcast.2), calls=%async_computation | async-start | bytes 1048576 | tf_op jit(solution)/shard_map/all_to_all | solution.py:46
  20.6 11.9 %all-to-all-done = bf16[32,64,128]{2,1,0:T(8,128)(2,1)S(1)} async-done(((bf16[32,64,128]{2,1,0:T(8,128)(2,1)}), bf16[32,64,128]{2,1,0:T(8,128)(2,1)S(1)}, u32[]{:S(2)}, u32[]{:S(2)}) %all-to-all-start) | async-done | bytes 524320 | tf_op jit(solution)/shard_map/all_to_all | solution.py:46
  32.5 0.8 copy-done.12
  33.3 7.1 %collective-permute-start.1 = (bf16[48,128,128]{2,1,0:T(8,128)(2,1)S(1)}, bf16[48,128,128]{2,1,0:T(8,128)(2,1)}, u32[]{:S(2)}, u32[]{:S(2)}) collective-permute-start(bf16[48,128,128]{2,1,0:T(8,128)(2,1)S(1)} %bitcast.32), channel_id=1, source_target_pairs={{0,4},{1,5},{2,6},{3,7},{4,0},{5,1},{6,2},{7,3},{8,12},{9,13},{10,... | collective-permute-start | bytes 4718600 | tf_op jit(solution)/shard_map/ppermute | solution.py:54
  40.4 1.9 %collective-permute-start = (s32[97]{0:T(128)S(1)}, s32[97]{0:T(128)S(1)}, u32[]{:S(2)}, u32[]{:S(2)}) collective-permute-start(s32[97]{0:T(128)S(1)} %pad_add_fusion), channel_id=1, source_target_pairs={{0,4},{1,5},{2,6},{3,7},{4,0},{5,1},{6,2},{7,3},{8,12},{9,13},{10,... | collective-permute-start | bytes 1172 | tf_op jit(solution)/shard_map/ppermute | solution.py:54
  42.3 1.3 broadcast_in_dim.42
  43.6 3.5 %all-to-all-start.2 = ((bf16[4,320,512]{2,1,0:T(8,128)(2,1)}), bf16[4,320,512]{2,1,0:T(8,128)(2,1)S(1)}, u32[]{:S(2)}, u32[]{:S(2)}) async-start(bf16[4,320,512]{2,1,0:T(8,128)(2,1)} %broadcast_in_dim.42), calls=%async_computation.2 | async-start | bytes 2621440 | tf_op jit(solution)/shard_map/all_to_all | solution.py:46
  48.5 1.4 concatenate.11.s_ref
  49.9 5.7 %place.1 = (bf16[24,256,128]{2,1,0:T(8,128)(2,1)S(1)}, bf16[24,256,128]{2,1,0:T(8,128)(2,1)S(1)}) custom-call(s32[195]{0:T(256)S(1)} %concatenate.11.s_ref, bf16[48,128,128]{2,1,0:T(8,128)(2,1)S(1)} %bitcast.33, bf16[48,128,128]{2,1,0:T(8,128)(2,1)} %collective-permute-done.1.other_ref), custom_call_target="tpu_custom_call" | custom-call | flops 1000000 | bytes 6000000 | tf_op jit(solution)/shard_map/place/pallas_call | solution.py:209
  55.6 1.2 copy-done.2
  56.7 1.1 copy-done.4
  57.9 17.9 %all-gather.2.cloned.1.call-done.g_ref = bf16[256,64,128]{2,1,0:T(8,128)(2,1)} async-done(((bf16[32,64,128]{2,1,0:T(8,128)(2,1)}), bf16[256,64,128]{2,1,0:T(8,128)(2,1)}) %all-gather.2.cloned.1.call-update) | async-done | bytes 4194320 | tf_op jit(solution)/shard_map/all_gather | solution.py:188
  75.7 1.4 copy-done.3
  77.1 1.4 copy-done.5
  78.5 3.9 %sum.1 = (f32[256,512]{1,0:T(8,128)S(1)}, bf16[256,512]{1,0:T(8,128)(2,1)S(1)}) custom-call(s32[195]{0:T(256)S(1)} %concatenate.11.s_ref, bf16[24,256,128]{2,1,0:T(8,128)(2,1)S(1)} %copy-done.3, bf16[24,256,128]{2,1,0:T(8,128)(2,1)S(1)} %copy-done.5, bf16[256,64,128]{2,1,0:T(8,128)(2,1)} %all-gather.2.cloned.1.call-done.g_ref), custom_call_target="tpu_custom_call" | custom-call | flops 1610612736 | bytes 8000000 | tf_op jit(solution)/shard_map/sum/pallas_call | solution.py:232
  82.4 5.4 %collective-permute-start.2 = (bf16[256,512]{1,0:T(8,128)(2,1)S(1)}, bf16[256,512]{1,0:T(8,128)(2,1)S(1)}, u32[]{:S(2)}, u32[]{:S(2)}) collective-permute-start(bf16[256,512]{1,0:T(8,128)(2,1)S(1)} %get-tuple-element.22), channel_id=1, source_target_pairs={{0,4},{1,5},{2,6},{3,7},{4,0},{5,1},{6,2},{7,3},{8,12},{9,13},{10,... | collective-permute-start | bytes 786440 | tf_op jit(solution)/shard_map/ppermute | solution.py:54
  87.8 1.1 collective-permute-done.2
  89.1 1.1 broadcast_in_dim.20
  90.2 4.6 %all-to-all-start.1 = ((bf16[4,256,512]{2,1,0:T(8,128)(2,1)}), bf16[4,256,512]{2,1,0:T(8,128)(2,1)S(1)}, u32[]{:S(2)}, u32[]{:S(2)}) async-start(bf16[4,256,512]{2,1,0:T(8,128)(2,1)} %broadcast_in_dim.20), calls=%async_computation.1 | async-start | bytes 2097152 | tf_op jit(solution)/shard_map/all_to_all | solution.py:46
  94.8 0.7 early.1
  95.5 0.8 copy-done.8
  96.3 0.8 copy-done.10
  97.1 12.2 %all-to-all-done.1.a_ref = bf16[4,256,512]{2,1,0:T(8,128)(2,1)S(1)} async-done(((bf16[4,256,512]{2,1,0:T(8,128)(2,1)}), bf16[4,256,512]{2,1,0:T(8,128)(2,1)S(1)}, u32[]{:S(2)}, u32[]{:S(2)}) %all-to-all-start.1) | async-done | bytes 1048608 | tf_op jit(solution)/shard_map/all_to_all | solution.py:46
  109.3 1.0 copy-done.9
  110.3 1.0 copy-done.11
  111.4 1.4 dense.1
  112.8 24.1 %all_to_all.30 = bf16[16,96,128]{2,1,0:T(8,128)(2,1)S(1)} all-to-all(bf16[16,96,128]{2,1,0:T(8,128)(2,1)S(1)} %bitcast.36), channel_id=1, replica_groups={{0,4,64,68,128,132,192,196,256,260,320,324,384,388,448,452},{1,5,65,69,..., dimensions={0} | all-to-all | bytes 786432 | tf_op jit(solution)/shard_map/all_to_all | solution.py:46
  137.0 14.1 %all_to_all.31 = bf16[8,96,128]{2,1,0:T(8,128)(2,1)S(1)} all-to-all(bf16[8,96,128]{2,1,0:T(8,128)(2,1)S(1)} %broadcast_in_dim.43), channel_id=1, replica_groups={{0,8,16,24,32,40,48,56},{1,9,17,25,33,41,49,57},{2,10,18,26,34,42,50,58..., dimensions={0} | all-to-all | bytes 393216 | tf_op jit(solution)/shard_map/all_to_all | solution.py:46
  151.2 17.4 %all_to_all.32 = bf16[16,96,128]{2,1,0:T(8,128)(2,1)S(1)} all-to-all(bf16[16,96,128]{2,1,0:T(8,128)(2,1)S(1)} %broadcast_in_dim.44), channel_id=1, replica_groups={{0,4,64,68,128,132,192,196,256,260,320,324,384,388,448,452},{1,5,65,69,..., dimensions={0} | all-to-all | bytes 786432 | tf_op jit(solution)/shard_map/all_to_all | solution.py:46
  168.7 0.7 slice.38
  169.4 0.9 copy_bitcast_fusion
  (45 shorter events, 2.0 us)
Async XLA Ops:
  7.2 12.5 %copy-start.7 = (bf16[256,128]{1,0:T(8,128)(2,1)S(1)}, bf16[256,128]{1,0:T(8,128)(2,1)}, u32[]{:S(2)}) copy-start(bf16[256,128]{1,0:T(8,128)(2,1)} %f_ref.1) | copy-start | bytes 196612
  7.2 13.3 %copy-start.16 = (s32[1,1,48]{2,1,0:T(1,128)S(1)}, s32[1,1,48]{2,1,0:T(1,128)}, u32[]{:S(2)}) copy-start(s32[1,1,48]{2,1,0:T(1,128)} %param.11) | copy-start | bytes 580
  7.2 13.3 %copy-start.15 = (s32[1,1,48]{2,1,0:T(1,128)S(1)}, s32[1,1,48]{2,1,0:T(1,128)}, u32[]{:S(2)}) copy-start(s32[1,1,48]{2,1,0:T(1,128)} %param.12) | copy-start | bytes 580
  7.2 13.3 %copy-start.14 = (bf16[128,512]{1,0:T(8,128)(2,1)S(1)}, bf16[128,512]{1,0:T(8,128)(2,1)}, u32[]{:S(2)}) copy-start(bf16[128,512]{1,0:T(8,128)(2,1)} %param.14) | copy-start | bytes 393220
  7.2 13.3 %copy-start.13 = (bf16[128,512]{1,0:T(8,128)(2,1)S(1)}, bf16[128,512]{1,0:T(8,128)(2,1)}, u32[]{:S(2)}) copy-start(bf16[128,512]{1,0:T(8,128)(2,1)} %param.15) | copy-start | bytes 393220
  7.2 26.1 %copy-start.1 = (bf16[1,1,48,128,128]{4,3,2,1,0:T(8,128)(2,1)S(1)}, bf16[1,1,48,128,128]{4,3,2,1,0:T(8,128)(2,1)}, u32[]{:S(2)}) copy-start(bf16[1,1,48,128,128]{4,3,2,1,0:T(8,128)(2,1)} %param.10) | copy-start | bytes 4718596
  9.1 23.3 %all-to-all-start = ((bf16[32,64,128]{2,1,0:T(8,128)(2,1)}), bf16[32,64,128]{2,1,0:T(8,128)(2,1)S(1)}, u32[]{:S(2)}, u32[]{:S(2)}) async-start(bf16[32,64,128]{2,1,0:T(8,128)(2,1)} %bitcast.2), calls=%async_computation | async-start | bytes 1048576 | tf_op jit(solution)/shard_map/all_to_all | solution.py:46
  19.6 56.1 %all-gather.2.cloned.1.call-start = ((), (), s32[]{:S(2)}) async-start(), calls=%async_computation.6 | async-start | bytes 4718592 | tf_op jit(solution)/shard_map/all_gather | solution.py:188
  32.5 0.8 copy-start.12
  33.3 16.6 %collective-permute-start.1 = (bf16[48,128,128]{2,1,0:T(8,128)(2,1)S(1)}, bf16[48,128,128]{2,1,0:T(8,128)(2,1)}, u32[]{:S(2)}, u32[]{:S(2)}) collective-permute-start(bf16[48,128,128]{2,1,0:T(8,128)(2,1)S(1)} %bitcast.32), channel_id=1, source_target_pairs={{0,4},{1,5},{2,6},{3,7},{4,0},{5,1},{6,2},{7,3},{8,12},{9,13},{10,... | collective-permute-start | bytes 4718600 | tf_op jit(solution)/shard_map/ppermute | solution.py:54
  40.4 7.4 %collective-permute-start = (s32[97]{0:T(128)S(1)}, s32[97]{0:T(128)S(1)}, u32[]{:S(2)}, u32[]{:S(2)}) collective-permute-start(s32[97]{0:T(128)S(1)} %pad_add_fusion), channel_id=1, source_target_pairs={{0,4},{1,5},{2,6},{3,7},{4,0},{5,1},{6,2},{7,3},{8,12},{9,13},{10,... | collective-permute-start | bytes 1172 | tf_op jit(solution)/shard_map/ppermute | solution.py:54
  43.6 45.5 %all-to-all-start.2 = ((bf16[4,320,512]{2,1,0:T(8,128)(2,1)}), bf16[4,320,512]{2,1,0:T(8,128)(2,1)S(1)}, u32[]{:S(2)}, u32[]{:S(2)}) async-start(bf16[4,320,512]{2,1,0:T(8,128)(2,1)} %broadcast_in_dim.42), calls=%async_computation.2 | async-start | bytes 2621440 | tf_op jit(solution)/shard_map/all_to_all | solution.py:46
  55.5 1.2 copy-start.2
  56.7 1.1 copy-start.4
  75.7 1.4 copy-start.3
  77.1 1.4 copy-start.5
  82.4 6.6 %collective-permute-start.2 = (bf16[256,512]{1,0:T(8,128)(2,1)S(1)}, bf16[256,512]{1,0:T(8,128)(2,1)S(1)}, u32[]{:S(2)}, u32[]{:S(2)}) collective-permute-start(bf16[256,512]{1,0:T(8,128)(2,1)S(1)} %get-tuple-element.22), channel_id=1, source_target_pairs={{0,4},{1,5},{2,6},{3,7},{4,0},{5,1},{6,2},{7,3},{8,12},{9,13},{10,... | collective-permute-start | bytes 786440 | tf_op jit(solution)/shard_map/ppermute | solution.py:54
  89.1 5.7 %copy-start = (bf16[512,512]{1,0:T(8,128)(2,1)S(1)}, bf16[512,512]{1,0:T(8,128)(2,1)}, u32[]{:S(2)}) copy-start(bf16[512,512]{1,0:T(8,128)(2,1)} %ow_ref.3) | copy-start | bytes 1572868
  89.1 5.7 %copy-start.6 = (bf16[256,512]{1,0:T(8,128)(2,1)S(1)}, bf16[256,512]{1,0:T(8,128)(2,1)}, u32[]{:S(2)}) copy-start(bf16[256,512]{1,0:T(8,128)(2,1)} %cot_ref.3) | copy-start | bytes 786436
  90.2 19.1 %all-to-all-start.1 = ((bf16[4,256,512]{2,1,0:T(8,128)(2,1)}), bf16[4,256,512]{2,1,0:T(8,128)(2,1)S(1)}, u32[]{:S(2)}, u32[]{:S(2)}) async-start(bf16[4,256,512]{2,1,0:T(8,128)(2,1)} %broadcast_in_dim.20), calls=%async_computation.1 | async-start | bytes 2097152 | tf_op jit(solution)/shard_map/all_to_all | solution.py:46
  95.5 0.8 copy-start.8
  96.3 0.8 copy-start.10
  109.3 1.0 copy-start.9
  110.3 1.0 copy-start.11
Sparse Core Ops, SparseCore 0:
  33.4 42.2 all-gather.1

commit v2 on v1

v2 whole, which is shorter than its diff:
```python
import jax
import jax.numpy as jnp
from jax import lax
from jax.experimental import pallas as pl
from jax.experimental.pallas import tpu as pltpu
from jax.sharding import PartitionSpec as P

AXES = ("wide", "narrow")
NZ, NY, NC, NN = 8, 8, 2, 4
STEP = 8
VMEM = pl.BlockSpec(memory_space=pltpu.VMEM)
SMEM = pl.BlockSpec(memory_space=pltpu.SMEM)
ANY = pl.BlockSpec(memory_space=pl.ANY)
F32, BF16, I32 = jnp.float32, jnp.bfloat16, jnp.int32
NEAR = (0, 7, 1, 6, 2)
FAR = (5, 3, 4)


def places():
    for z in range(NZ):
        for y in range(NY):
            for c in range(NC):
                for n in range(NN):
                    yield z, y, c, n


def device(z, y, c, n):
    return ((z * NY + y) * NC + c) * NN + n


def groups(key):
    found = {}
    for place in places():
        found.setdefault(key(*place), []).append(device(*place))
    return list(found.values())


FIRST = groups(lambda z, y, c, n: (0, y) if c == 0 else (1, z))
OVER_X = groups(lambda z, y, c, n: (z, y, c))
OVER_ZC = groups(lambda z, y, c, n: (y, n))
OVER_Y = groups(lambda z, y, c, n: (z, c, n))
OTHER_CORE = [(device(z, y, c, n), device(z, y, 1 - c, n)) for z, y, c, n in places()]


def exchange(pieces, groups_):
    return lax.all_to_all(pieces, AXES, 0, 0, axis_index_groups=groups_, tiled=True)


def swap_cores(value):
    return lax.ppermute(value, AXES, OTHER_CORE)


def pass_on(value, hops):
    pairs = []
    for z, y, c, n in places():
        to = (z, (y + hops) % NY, c, n) if c == 0 else ((z + hops) % NZ, y, c, n)
        pairs.append((device(z, y, c, n), device(*to)))
    return lax.ppermute(value, AXES, pairs)


def call(kernel, name, out_shape, in_specs, out_specs, scratch, vmem, flops, size, *args):
    return pl.pallas_call(
        kernel,
        out_shape=out_shape,
        in_specs=in_specs,
        out_specs=out_specs,
        scratch_shapes=scratch,
        compiler_params=pltpu.CompilerParams(vmem_limit_bytes=vmem << 20),
        cost_estimate=pl.CostEstimate(flops=flops, bytes_accessed=size, transcendentals=0),
        name=name,
    )(*args)


def place_kernel(where_ref, own_n_ref, other_n_ref, own_ref, other_ref, lo_ref, lt_ref, meta_ref, order):
    slots, half = own_ref.shape[0], own_ref.shape[2] // 2
    side = own_ref.shape[1]
    room = meta_ref.shape[1] - 2
    first = where_ref[0] == 0
    here = where_ref[1]
    low = lax.broadcasted_iota(I32, own_ref.shape[1:], 1) < half
    for block, (n_ref, t_ref, l_ref) in enumerate(
        ((own_n_ref, own_ref, lo_ref), (other_n_ref, other_ref, lt_ref))
    ):
        count = n_ref[2 * slots]

        def clear(k, carry, block=block):
            order[k] = -1
            meta_ref[block, k] = 0
            return carry

        lax.fori_loop(0, room, clear, 0)

        def looked_up(s, n_ref=n_ref):
            col = n_ref[slots + s]
            z, y = lax.shift_right_logical(col, 3), lax.bitwise_and(col, 7)
            ring = jnp.where(first, y, z)
            inner = jnp.where(first, z, y)
            away = lax.bitwise_and(ring - here + 8, 7)
            return away, inner

        def tally(s, near):
            away, _ = looked_up(s)
            return near + jnp.where((away >= 3) & (away <= 5), 0, 1)

        near = lax.fori_loop(0, count, tally, 0)
        near_turns = lax.shift_right_logical(near + STEP - 1, 3)
        far_turns = lax.shift_right_logical(count - near + STEP - 1, 3)
        meta_ref[block, room] = near_turns
        meta_ref[block, room + 1] = near_turns + far_turns

        def assign(s, carry, block=block):
            near_at, far_at = carry
            away, inner = looked_up(s)
            far = (away >= 3) & (away <= 5)
            base = jnp.int32(0)
            for among in (NEAR, FAR):
                for k, distance in enumerate(among):
                    base = jnp.where(away == distance, k, base)
            at = jnp.where(far, far_at, near_at)
            order[at] = s
            meta_ref[block, at] = base * (NZ * NN) + inner * NN
            step = jnp.where(far, 1, 0)
            return near_at + 1 - step, far_at + step

        lax.fori_loop(0, count, assign, (0, near_turns * STEP))

        def one_pair(p, carry, n_ref=n_ref, t_ref=t_ref, l_ref=l_ref):
            slot_a, slot_b = order[2 * p], order[2 * p + 1]
            at_a, at_b = jnp.maximum(slot_a, 0), jnp.maximum(slot_b, 0)
            a, b = t_ref[at_a].astype(F32), t_ref[at_b].astype(F32)
            moved = pltpu.roll(jnp.where(first, b, a), half, 1)
            both = jnp.where(low, jnp.where(first, a, moved), jnp.where(first, moved, b))
            row_a = jnp.where(slot_a >= 0, n_ref[at_a], -1)
            row_b = jnp.where(slot_b >= 0, n_ref[at_b], -1)
            rows = jnp.where(low, row_a, row_b)
            for r in range(2):
                l_ref[p, r * side:(r + 1) * side, :] = jnp.where(rows == r, both, 0.0).astype(BF16)
            return carry

        lax.fori_loop(0, (near_turns + far_turns) * (STEP // 2), one_pair, 0)


def add_turns(meta_ref, block, first_turn, last_turn, l_ref, blocks, acc):
    def one_turn(i, carry):
        left = jnp.concatenate([l_ref[i * (STEP // 2) + k] for k in range(STEP // 2)], axis=1)
        spots = [meta_ref[block, i * STEP + k] for k in range(STEP)]
        right = jnp.concatenate(
            [jnp.concatenate([blocks[spot + n] for spot in spots], axis=0) for n in range(NN)],
            axis=1,
        )
        acc[...] += jnp.dot(left, right, preferred_element_type=F32)
        return carry

    lax.fori_loop(first_turn, last_turn, one_turn, 0)


def bring(refs, blocks, sems):
    copies, at = [], 0
    for k, ref in enumerate(refs):
        copies.append(
            pltpu.make_async_copy(ref, blocks.at[pl.ds(at, ref.shape[0])], sems.at[k])
        )
        at += ref.shape[0]
    for copy in copies:
        copy.start()
    return copies


def near_kernel(meta_ref, lo_ref, lt_ref, *refs):
    *given, po_ref, pt_ref, blocks, sems = refs
    room = meta_ref.shape[1] - 2
    copies = bring(given, blocks, sems)
    po_ref[...] = jnp.zeros_like(po_ref)
    pt_ref[...] = jnp.zeros_like(pt_ref)
    for copy in copies:
        copy.wait()
    add_turns(meta_ref, 1, 0, meta_ref[1, room], lt_ref, blocks, pt_ref)
    add_turns(meta_ref, 0, 0, meta_ref[0, room], lo_ref, blocks, po_ref)


def far_kernel(meta_ref, lo_ref, lt_ref, no_ref, nt_ref, *refs):
    *given, po_ref, pt_ref, acc, blocks, sems = refs
    room = meta_ref.shape[1] - 2
    copies = bring(given, blocks, sems)
    acc[...] = nt_ref[...]
    po_ref[...] = no_ref[...]
    for copy in copies:
        copy.wait()
    add_turns(meta_ref, 1, meta_ref[1, room], meta_ref[1, room + 1], lt_ref, blocks, acc)
    pt_ref[...] = acc[...].astype(BF16)
    add_turns(meta_ref, 0, meta_ref[0, room], meta_ref[0, room + 1], lo_ref, blocks, po_ref)


def join_kernel(own_ref, came_ref, out_ref):
    joined = (own_ref[...] + came_ref[...].astype(F32)).astype(BF16)
    for j in range(out_ref.shape[0]):
        out_ref[j] = joined


def total_kernel(in_ref, out_ref):
    summed = in_ref[0].astype(F32)
    for j in range(1, in_ref.shape[0]):
        summed = summed + in_ref[j].astype(F32)
    summed = summed.astype(BF16)
    for j in range(out_ref.shape[0]):
        out_ref[j] = summed


def last_kernel(in_ref, neighbor_ref, root_ref, output_ref):
    side = in_ref.shape[1]
    for j in range(NN):
        neighbor_ref[:, j * side:(j + 1) * side] = in_ref[j].astype(F32)
        root_ref[:, j * side:(j + 1) * side] = in_ref[NN + j].astype(F32)
        output_ref[j * side:(j + 1) * side, :] = in_ref[2 * NN + j].astype(F32)


def dense_kernel(n_ref, a_ref, w_ref, f_ref, cot_ref, ow_ref, out_ref, g_ref, agg_ref):
    side = f_ref.shape[1]
    quarter = w_ref.shape[1] - 2 * side
    mine = pl.ds(pl.multiple_of(n_ref[0] * side, side), side)
    root_weight = jnp.concatenate([w_ref[j, side:2 * side, :] for j in range(NN)], axis=0)
    neighbor_weight = jnp.concatenate([w_ref[j, :side, :] for j in range(NN)], axis=0)
    rows = jnp.concatenate(
        [
            jnp.concatenate(
                [w_ref[j, 2 * side:, q * side:(q + 1) * side] for j in range(NN)], axis=1
            )
            for q in range(NN)
        ],
        axis=0,
    )
    hidden_grad = lax.dot_general(
        cot_ref[...], ow_ref[...], (((1,), (1,)), ((), ())), preferred_element_type=F32
    )
    agg = a_ref[0].astype(F32)
    for j in range(1, NN):
        agg = agg + a_ref[j].astype(F32)
    agg = agg.astype(BF16)
    agg_ref[...] = agg
    pre = jnp.dot(agg, neighbor_weight, preferred_element_type=F32) + jnp.dot(
        rows, root_weight, preferred_element_type=F32
    )
    s = jax.nn.sigmoid(pre)
    hidden = (pre * s).astype(BF16)
    pre_grad = (hidden_grad * s * (1.0 + pre * (1.0 - s))).astype(BF16)
    over_rows = (((0,), (0,)), ((), ()))
    parts = (
        lax.dot_general(agg_ref[:, mine], pre_grad, over_rows, preferred_element_type=F32),
        lax.dot_general(f_ref[...], pre_grad, over_rows, preferred_element_type=F32),
    )
    for k, part in enumerate(parts):
        for j in range(NN):
            g_ref[k * NN + j] = part[:, j * side:(j + 1) * side].astype(BF16)
    part = lax.dot_general(hidden, cot_ref[:, mine], over_rows, preferred_element_type=F32)
    for j in range(NN):
        g_ref[2 * NN + j] = part[j * side:(j + 1) * side, :].astype(BF16)
    out_ref[...] = (
        f_ref[...].astype(F32) + jnp.dot(hidden, ow_ref[:, mine], preferred_element_type=F32)
    ).astype(BF16)


def per_device(
    features,
    tile_blocks,
    tile_rows,
    tile_cols,
    tile_count,
    neighbor_weight,
    root_weight,
    output_weight,
    cotangent,
):
    rows, side = features.shape
    width = NN * side
    quarter = rows // NN
    slots = tile_rows.shape[-1]
    wide = lax.axis_index("wide")
    narrow = lax.axis_index("narrow").astype(I32)
    core = wide % NC
    here = jnp.where(core == 0, (wide // NC) % NY, wide // (NC * NY))

    tiles = tile_blocks[0, 0]
    numbers = jnp.concatenate([tile_rows[0, 0], tile_cols[0, 0], tile_count[0]])
    other_tiles = swap_cores(tiles)
    other_numbers = swap_cores(numbers)

    pieces = jnp.broadcast_to(
        features.reshape(1, NN, quarter, side), (NZ, NN, quarter, side)
    ).reshape(NZ * NN, quarter, side)
    line = exchange(pieces, FIRST)

    turns = (slots + 2 * STEP - 2) // STEP
    placed = jax.ShapeDtypeStruct((turns * STEP // 2, rows, side), BF16)
    left_own, left_other, meta = call(
        place_kernel,
        "place",
        (placed, placed, jax.ShapeDtypeStruct((2, turns * STEP + 2), I32)),
        [SMEM, SMEM, SMEM, VMEM, VMEM],
        (VMEM, VMEM, SMEM),
        [pltpu.SMEM((turns * STEP,), I32)],
        10,
        10**7,
        7 * 10**6,
        jnp.stack([core, here]).astype(I32),
        numbers,
        other_numbers,
        tiles,
        other_tiles,
    )

    weights = jnp.concatenate(
        [
            neighbor_weight,
            root_weight,
            features.reshape(NN, quarter, side).swapaxes(0, 1).reshape(quarter, width),
        ],
        axis=0,
    )
    line, weights = lax.optimization_barrier((line, weights))
    all_weights = exchange(jnp.broadcast_to(weights[None], (NN, *weights.shape)), OVER_X)

    by_distance = {0: line}
    for hops in (1, -1, 2, -2):
        by_distance[-hops % NY] = pass_on(line, hops)
    for hops in (1, -1):
        by_distance[-3 * hops % NY] = pass_on(by_distance[-2 * hops % NY], hops)
    middle = NZ * NN // 2
    far_low = pass_on(by_distance[6][:middle], 2)
    far_high = pass_on(by_distance[2][middle:], -2)

    whole = jax.ShapeDtypeStruct((rows, width), F32)
    flops = 2 * slots * rows * quarter * width
    line_size = NZ * NN
    near_own, near_other = call(
        near_kernel,
        "near",
        (whole, whole),
        [SMEM, VMEM, VMEM] + [ANY] * len(NEAR),
        (VMEM, VMEM),
        [
            pltpu.VMEM((len(NEAR) * line_size, quarter, side), BF16),
            pltpu.SemaphoreType.DMA((len(NEAR),)),
        ],
        20,
        flops,
        8 * 10**6,
        meta,
        left_own,
        left_other,
        *[by_distance[d] for d in NEAR],
    )
    part_own, part_other = call(
        far_kernel,
        "far",
        (whole, jax.ShapeDtypeStruct((rows, width), BF16)),
        [SMEM, VMEM, VMEM, VMEM, VMEM] + [ANY] * (len(FAR) + 1),
        (VMEM, VMEM),
        [
            pltpu.VMEM((rows, width), F32),
            pltpu.VMEM((len(FAR) * line_size, quarter, side), BF16),
            pltpu.SemaphoreType.DMA((len(FAR) + 1,)),
        ],
        20,
        flops // 2,
        6 * 10**6,
        meta,
        left_own,
        left_other,
        near_own,
        near_other,
        by_distance[FAR[0]],
        by_distance[FAR[1]],
        far_low,
        far_high,
    )
    copies = call(
        join_kernel,
        "join",
        jax.ShapeDtypeStruct((NN, rows, width), BF16),
        [VMEM, VMEM],
        VMEM,
        [],
        8,
        10**6,
        2 * 10**6,
        part_own,
        swap_cores(part_other),
    )
    parts = exchange(copies, OVER_X)

    layer_output, grads = call(
        dense_kernel,
        "dense",
        (
            jax.ShapeDtypeStruct((rows, side), BF16),
            jax.ShapeDtypeStruct((3 * NN, side, side), BF16),
        ),
        [SMEM] + [VMEM] * 5,
        (VMEM, VMEM),
        [pltpu.VMEM((rows, width), BF16)],
        16,
        12 * rows * width * width,
        5 * 10**6,
        narrow[None],
        parts,
        all_weights,
        features,
        cotangent,
        output_weight,
    )

    chunk = 3 * NN * side // (NZ * NC)

    def total(pieces, count):
        return call(
            total_kernel,
            "total",
            jax.ShapeDtypeStruct((count, chunk, side), BF16),
            [VMEM],
            VMEM,
            [],
            4,
            10**6,
            10**6,
            pieces,
        )

    summed = total(exchange(grads.reshape(NZ * NC, chunk, side), OVER_ZC), NY)
    summed = total(exchange(summed, OVER_Y), NZ * NC)
    full = exchange(summed, OVER_ZC).reshape(3 * NN, side, side)
    return layer_output, *call(
        last_kernel,
        "last",
        (
            jax.ShapeDtypeStruct((side, width), F32),
            jax.ShapeDtypeStruct((side, width), F32),
            jax.ShapeDtypeStruct((width, side), F32),
        ),
        [VMEM],
        (VMEM, VMEM, VMEM),
        [],
        4,
        10**6,
        10**6,
        full,
    )


def solution(mesh):
    return jax.shard_map(
        per_device,
        mesh=mesh,
        in_specs=(
            P("wide", "narrow"),
            P("wide", "narrow", None, None, None),
            P("wide", "narrow", None),
            P("wide", "narrow", None),
            P("wide", "narrow"),
            P("narrow", None),
            P("narrow", None),
            P(),
            P("wide", None),
        ),
        out_specs=(P("wide", "narrow"), P("narrow", None), P("narrow", None), P(None, "narrow")),
        check_vma=False,
    )
```

time: 178 us -> 172 us (0.966)
  starting transfers between devices: 33.1 us -> 63.8 us
  waiting for transfers between devices: 43.1 us -> 23.1 us
  between operations: 14.9 us -> 1.63 us
  local copies, waits for them, and re-layouts: 18.2 us -> 7.45 us
  Pallas kernels: 11.7 us -> 19.3 us
    ppermute x0 -> x8, starting transfers between devices: none -> 32 us  [pass_on(): return lax.ppermute(value, AXES, pairs)]
    all_gather x1 -> x0, waiting for transfers between devices: 17.9 us -> none  [per_device(): lax.all_gather(line, AXES, axis_index_groups=SECOND, axis=0, tiled=True)]
    unnamed x36 -> x17, local copies, waits for them, and re-layouts: 9.71 us -> 0.99 us
    pallas_call x4 -> x8, Pallas kernels: 11.7 us -> 19.3 us  [call(): pl.pallas_call(kernel, out_shape=out_shape, in_specs=in_specs, out_specs=...]
    all_to_all x3, waiting for transfers between devices: 24.1 us -> 21.1 us  [exchange(): lax.all_to_all(pieces, AXES, 0, 0, axis_index_groups=groups_, tiled=True)]
  transfers between devices with their start and end apart: 7 -> 14, of which waited for: 4 -> 4; matrix products, arithmetic and copies ran while one was open for 2% -> 3% of each run, Pallas kernels for 6% -> 10%
where the time goes in v2:
time: 172 us; the launch traced here: 171 us
  starting transfers between devices  63.8 us (37%)
  blocking collectives  55.4 us (32%)
  waiting for transfers between devices  23.1 us (13%)
  Pallas kernels  19.3 us (11%)
  local copies, waits for them, and re-layouts  7.45 us (4%)
    all_to_all x3, blocking collectives, exchange(): lax.all_to_all(pieces, AXES, 0, 0, axis_index_groups=groups_, tiled=True)  55.4 us
    ppermute x8, starting transfers between devices, pass_on(): return lax.ppermute(value, AXES, pairs)  32 us
    all_to_all x3, waiting for transfers between devices, exchange(): lax.all_to_all(pieces, AXES, 0, 0, axis_index_groups=groups_, tiled=True)  21.1 us
    pallas_call x8, Pallas kernels, call(): pl.pallas_call(kernel, out_shape=out_shape, in_specs=in_specs, out_specs=...  19.3 us
    all_to_all x3, starting transfers between devices, exchange(): lax.all_to_all(pieces, AXES, 0, 0, axis_index_groups=groups_, tiled=True)  18.4 us
    ppermute x3, starting transfers between devices, swap_cores(): return lax.ppermute(value, AXES, OTHER_CORE)  13.4 us
  transfers between devices with their start and end apart: 14, of which 4 were waited for; matrix products, arithmetic and copies ran while one was open for 3% of the time, Pallas kernels for 10%

profile of v2, /device:TPU:1, one launch (start us, length us, event | category | flops | bytes accessed | tf_op | source)
XLA Modules:
  0.0 170.9 jit_solution(8320338309062486070)
XLA Ops:
  0.7 1.9 %broadcast_in_dim.18 = bf16[8,4,64,128]{3,2,1,0:T(8,128)(2,1)} broadcast(bf16[4,64,128]{2,1,0:T(8,128)(2,1)} %bitcast.20), dimensions={1,2,3} | broadcast | bytes 589824 | tf_op jit(solution)/shard_map/broadcast_in_dim | solution.py:287
  2.6 10.5 %all-to-all-start = ((bf16[32,64,128]{2,1,0:T(8,128)(2,1)}), bf16[32,64,128]{2,1,0:T(8,128)(2,1)S(1)}, u32[]{:S(2)}, u32[]{:S(2)}) async-start(bf16[32,64,128]{2,1,0:T(8,128)(2,1)} %bitcast.8), calls=%async_computation | async-start | bytes 1048576 | tf_op jit(solution)/shard_map/all_to_all | solution.py:46
  13.1 6.1 %collective-permute-start.1 = (bf16[48,128,128]{2,1,0:T(8,128)(2,1)S(1)}, bf16[48,128,128]{2,1,0:T(8,128)(2,1)}, u32[]{:S(2)}, u32[]{:S(2)}) collective-permute-start(bf16[48,128,128]{2,1,0:T(8,128)(2,1)S(1)} %bitcast.17), channel_id=1, source_target_pairs={{0,4},{1,5},{2,6},{3,7},{4,0},{5,1},{6,2},{7,3},{8,12},{9,13},{10,... | collective-permute-start | bytes 4718600 | tf_op jit(solution)/shard_map/ppermute | solution.py:50
  19.3 6.6 %all-to-all-done.refs_0_ = bf16[32,64,128]{2,1,0:T(8,128)(2,1)S(1)} async-done(((bf16[32,64,128]{2,1,0:T(8,128)(2,1)}), bf16[32,64,128]{2,1,0:T(8,128)(2,1)S(1)}, u32[]{:S(2)}, u32[]{:S(2)}) %all-to-all-start) | async-done | bytes 524320 | tf_op jit(solution)/shard_map/all_to_all | solution.py:46
  25.9 5.7 %collective-permute-start.4 = (bf16[32,64,128]{2,1,0:T(8,128)(2,1)S(1)}, bf16[32,64,128]{2,1,0:T(8,128)(2,1)}, u32[]{:S(2)}, u32[]{:S(2)}) collective-permute-start(bf16[32,64,128]{2,1,0:T(8,128)(2,1)S(1)} %all-to-all-done.refs_0_), channel_id=1, source_target_pairs={{0,16},{1,17},{2,18},{3,19},{4,132},{5,133},{6,134},{7,135},{8,24}... | collective-permute-start | bytes 1572872 | tf_op jit(solution)/shard_map/ppermute | solution.py:58
  31.6 6.8 %collective-permute-start.5 = (bf16[32,64,128]{2,1,0:T(8,128)(2,1)S(1)}, bf16[32,64,128]{2,1,0:T(8,128)(2,1)}, u32[]{:S(2)}, u32[]{:S(2)}) collective-permute-start(bf16[32,64,128]{2,1,0:T(8,128)(2,1)S(1)} %all-to-all-done.refs_0_), channel_id=1, source_target_pairs={{0,48},{1,49},{2,50},{3,51},{4,388},{5,389},{6,390},{7,391},{8,56}... | collective-permute-start | bytes 1572872 | tf_op jit(solution)/shard_map/ppermute | solution.py:58
  38.3 3.1 %collective-permute-start.2 = (bf16[32,64,128]{2,1,0:T(8,128)(2,1)S(1)}, bf16[32,64,128]{2,1,0:T(8,128)(2,1)}, u32[]{:S(2)}, u32[]{:S(2)}) collective-permute-start(bf16[32,64,128]{2,1,0:T(8,128)(2,1)S(1)} %all-to-all-done.refs_0_), channel_id=1, source_target_pairs={{0,8},{1,9},{2,10},{3,11},{4,68},{5,69},{6,70},{7,71},{8,16},{9,17... | collective-permute-start | bytes 1572872 | tf_op jit(solution)/shard_map/ppermute | solution.py:58
  42.1 1.2 broadcast_in_dim.19
  43.3 3.7 %all-to-all-start.2 = ((bf16[4,320,512]{2,1,0:T(8,128)(2,1)}), bf16[4,320,512]{2,1,0:T(8,128)(2,1)S(1)}, u32[]{:S(2)}, u32[]{:S(2)}) async-start(bf16[4,320,512]{2,1,0:T(8,128)(2,1)} %broadcast_in_dim.19), calls=%async_computation.2 | async-start | bytes 2621440 | tf_op jit(solution)/shard_map/all_to_all | solution.py:46
  47.0 3.0 %collective-permute-start = (s32[97]{0:T(128)S(1)}, s32[97]{0:T(128)S(1)}, u32[]{:S(2)}, u32[]{:S(2)}) collective-permute-start(s32[97]{0:T(128)S(1)} %pad_add_fusion.1.own_n_ref), channel_id=1, source_target_pairs={{0,4},{1,5},{2,6},{3,7},{4,0},{5,1},{6,2},{7,3},{8,12},{9,13},{10,... | collective-permute-start | bytes 1172 | tf_op jit(solution)/shard_map/ppermute | solution.py:50
  50.0 0.8 collective-permute-done.other_n_ref
  50.8 2.6 %collective-permute-start.3 = (bf16[32,64,128]{2,1,0:T(8,128)(2,1)S(1)}, bf16[32,64,128]{2,1,0:T(8,128)(2,1)}, u32[]{:S(2)}, u32[]{:S(2)}) collective-permute-start(bf16[32,64,128]{2,1,0:T(8,128)(2,1)S(1)} %all-to-all-done.refs_0_), channel_id=1, source_target_pairs={{0,56},{1,57},{2,58},{3,59},{4,452},{5,453},{6,454},{7,455},{8,0},... | collective-permute-start | bytes 1572872 | tf_op jit(solution)/shard_map/ppermute | solution.py:58
  53.5 2.7 %collective-permute-start.6 = (bf16[32,64,128]{2,1,0:T(8,128)(2,1)}, bf16[32,64,128]{2,1,0:T(8,128)(2,1)}, u32[]{:S(2)}, u32[]{:S(2)}) collective-permute-start(bf16[32,64,128]{2,1,0:T(8,128)(2,1)} %collective-permute-done.4.refs_3_), channel_id=1, source_target_pairs={{0,8},{1,9},{2,10},{3,11},{4,68},{5,69},{6,70},{7,71},{8,16},{9,17... | collective-permute-start | bytes 1572872 | tf_op jit(solution)/shard_map/ppermute | solution.py:58
  56.1 3.8 %collective-permute-start.7 = (bf16[32,64,128]{2,1,0:T(8,128)(2,1)}, bf16[32,64,128]{2,1,0:T(8,128)(2,1)}, u32[]{:S(2)}, u32[]{:S(2)}) collective-permute-start(bf16[32,64,128]{2,1,0:T(8,128)(2,1)} %collective-permute-done.5.refs_4_), channel_id=1, source_target_pairs={{0,56},{1,57},{2,58},{3,59},{4,452},{5,453},{6,454},{7,455},{8,0},... | collective-permute-start | bytes 1572872 | tf_op jit(solution)/shard_map/ppermute | solution.py:58
  60.0 1.7 slice.8
  61.6 1.7 slice.9
  63.3 1.9 %collective-permute-start.8 = (bf16[16,64,128]{2,1,0:T(8,128)(2,1)}, bf16[16,64,128]{2,1,0:T(8,128)(2,1)}, u32[]{:S(2)}, u32[]{:S(2)}) collective-permute-start(bf16[16,64,128]{2,1,0:T(8,128)(2,1)} %slice.8), channel_id=1, source_target_pairs={{0,16},{1,17},{2,18},{3,19},{4,132},{5,133},{6,134},{7,135},{8,24}... | collective-permute-start | bytes 786440 | tf_op jit(solution)/shard_map/ppermute | solution.py:58
  65.3 5.5 %collective-permute-start.9 = (bf16[16,64,128]{2,1,0:T(8,128)(2,1)}, bf16[16,64,128]{2,1,0:T(8,128)(2,1)}, u32[]{:S(2)}, u32[]{:S(2)}) collective-permute-start(bf16[16,64,128]{2,1,0:T(8,128)(2,1)} %slice.9), channel_id=1, source_target_pairs={{0,48},{1,49},{2,50},{3,51},{4,388},{5,389},{6,390},{7,391},{8,56}... | collective-permute-start | bytes 786440 | tf_op jit(solution)/shard_map/ppermute | solution.py:58
  70.9 8.4 %place.1 = (bf16[28,256,128]{2,1,0:T(8,128)(2,1)S(1)}, bf16[28,256,128]{2,1,0:T(8,128)(2,1)S(1)}, s32[2,58]{1,0:T(2,128)S(1)}) custom-call(s32[2]{0:T(128)S(1)} %pad_add_fusion.where_ref, s32[97]{0:T(128)S(1)} %pad_add_fusion.1.own_n_ref, s32[97]{0:T(128)S(1)} %collective-permute-done.other_n_ref, bf16[48,128,128]{2,1,0:T(8,128)(2,1)S(1)} %bitcast.18, ...), custom_call_target="tpu_custom_call" | custom-call | flops 10000000 | bytes 7000000 | tf_op jit(solution)/shard_map/place/pallas_call | solution.py:62
  79.2 4.0 %near.1 = (f32[256,512]{1,0:T(8,128)S(1)}, f32[256,512]{1,0:T(8,128)S(1)}) custom-call(s32[2,58]{1,0:T(2,128)S(1)} %get-tuple-element.18.meta_ref, bf16[28,256,128]{2,1,0:T(8,128)(2,1)S(1)} %get-tuple-element.19.lo_ref, bf16[28,256,128]{2,1,0:T(8,128)(2,1)S(1)} %get-tuple-element.20.lt_ref, bf16[32,64,128]{2,1,0:T(8,128)(2,1)S(1)} %all-to-all-done.refs_0_, ...), custom_call_target="tpu_custom_call" | custom-call | flops 805306368 | bytes 8000000 | tf_op jit(solution)/shard_map/near/pallas_call | solution.py:62
  83.3 3.2 %far.1 = (f32[256,512]{1,0:T(8,128)S(1)}, bf16[256,512]{1,0:T(8,128)(2,1)S(1)}) custom-call(s32[2,58]{1,0:T(2,128)S(1)} %get-tuple-element.18.meta_ref, bf16[28,256,128]{2,1,0:T(8,128)(2,1)S(1)} %get-tuple-element.19.lo_ref, bf16[28,256,128]{2,1,0:T(8,128)(2,1)S(1)} %get-tuple-element.20.lt_ref, f32[256,512]{1,0:T(8,128)S(1)} %get-tuple-element.22.no_ref, ...), custom_call_target="tpu_custom_call" | custom-call | flops 402653184 | bytes 6000000 | tf_op jit(solution)/shard_map/far/pallas_call | solution.py:62
  86.5 4.4 %collective-permute-start.10 = (bf16[256,512]{1,0:T(8,128)(2,1)S(1)}, bf16[256,512]{1,0:T(8,128)(2,1)S(1)}, u32[]{:S(2)}, u32[]{:S(2)}) collective-permute-start(bf16[256,512]{1,0:T(8,128)(2,1)S(1)} %get-tuple-element.25), channel_id=1, source_target_pairs={{0,4},{1,5},{2,6},{3,7},{4,0},{5,1},{6,2},{7,3},{8,12},{9,13},{10,... | collective-permute-start | bytes 786440 | tf_op jit(solution)/shard_map/ppermute | solution.py:50
  90.8 1.1 collective-permute-done.10.came_ref
  92.0 1.1 join.1
  93.0 4.2 %all-to-all-start.1 = ((bf16[4,256,512]{2,1,0:T(8,128)(2,1)}), bf16[4,256,512]{2,1,0:T(8,128)(2,1)S(1)}, u32[]{:S(2)}, u32[]{:S(2)}) async-start(bf16[4,256,512]{2,1,0:T(8,128)(2,1)} %join.1), calls=%async_computation.1 | async-start | bytes 2097152 | tf_op jit(solution)/shard_map/all_to_all | solution.py:46
  97.3 14.5 %all-to-all-done.1.a_ref = bf16[4,256,512]{2,1,0:T(8,128)(2,1)S(1)} async-done(((bf16[4,256,512]{2,1,0:T(8,128)(2,1)}), bf16[4,256,512]{2,1,0:T(8,128)(2,1)S(1)}, u32[]{:S(2)}, u32[]{:S(2)}) %all-to-all-start.1) | async-done | bytes 1048608 | tf_op jit(solution)/shard_map/all_to_all | solution.py:46
  111.8 0.9 copy-done.3
  112.7 1.7 dense.1
  114.4 20.6 %all_to_all.30.in_ref = bf16[16,96,128]{2,1,0:T(8,128)(2,1)S(1)} all-to-all(bf16[16,96,128]{2,1,0:T(8,128)(2,1)S(1)} %bitcast.22), channel_id=1, replica_groups={{0,4,64,68,128,132,192,196,256,260,320,324,384,388,448,452},{1,5,65,69,..., dimensions={0} | all-to-all | bytes 786432 | tf_op jit(solution)/shard_map/all_to_all | solution.py:46
  135.1 17.5 %all_to_all.31.in_ref = bf16[8,96,128]{2,1,0:T(8,128)(2,1)S(1)} all-to-all(bf16[8,96,128]{2,1,0:T(8,128)(2,1)S(1)} %total.2), channel_id=1, replica_groups={{0,8,16,24,32,40,48,56},{1,9,17,25,33,41,49,57},{2,10,18,26,34,42,50,58..., dimensions={0} | all-to-all | bytes 393216 | tf_op jit(solution)/shard_map/all_to_all | solution.py:46
  152.6 17.4 %all_to_all.32 = bf16[16,96,128]{2,1,0:T(8,128)(2,1)S(1)} all-to-all(bf16[16,96,128]{2,1,0:T(8,128)(2,1)S(1)} %total.3), channel_id=1, replica_groups={{0,4,64,68,128,132,192,196,256,260,320,324,384,388,448,452},{1,5,65,69,..., dimensions={0} | all-to-all | bytes 786432 | tf_op jit(solution)/shard_map/all_to_all | solution.py:46
  169.9 0.9 last.1
  (32 shorter events, 0.4 us)
Async XLA Ops:
  0.6 18.5 %copy-start.1 = (bf16[256,128]{1,0:T(8,128)(2,1)S(1)}, bf16[256,128]{1,0:T(8,128)(2,1)}, u32[]{:S(2)}) copy-start(bf16[256,128]{1,0:T(8,128)(2,1)} %f_ref.1) | copy-start | bytes 196612
  0.6 12.4 %copy-start = (bf16[1,1,48,128,128]{4,3,2,1,0:T(8,128)(2,1)S(1)}, bf16[1,1,48,128,128]{4,3,2,1,0:T(8,128)(2,1)}, u32[]{:S(2)}) copy-start(bf16[1,1,48,128,128]{4,3,2,1,0:T(8,128)(2,1)} %param.10) | copy-start | bytes 4718596
  0.7 18.6 %copy-start.5 = (bf16[128,512]{1,0:T(8,128)(2,1)S(1)}, bf16[128,512]{1,0:T(8,128)(2,1)}, u32[]{:S(2)}) copy-start(bf16[128,512]{1,0:T(8,128)(2,1)} %param.14) | copy-start | bytes 393220
  0.7 18.6 %copy-start.4 = (bf16[128,512]{1,0:T(8,128)(2,1)S(1)}, bf16[128,512]{1,0:T(8,128)(2,1)}, u32[]{:S(2)}) copy-start(bf16[128,512]{1,0:T(8,128)(2,1)} %param.15) | copy-start | bytes 393220
  2.6 23.3 %all-to-all-start = ((bf16[32,64,128]{2,1,0:T(8,128)(2,1)}), bf16[32,64,128]{2,1,0:T(8,128)(2,1)S(1)}, u32[]{:S(2)}, u32[]{:S(2)}) async-start(bf16[32,64,128]{2,1,0:T(8,128)(2,1)} %bitcast.8), calls=%async_computation | async-start | bytes 1048576 | tf_op jit(solution)/shard_map/all_to_all | solution.py:46
  13.1 52.2 %collective-permute-start.1 = (bf16[48,128,128]{2,1,0:T(8,128)(2,1)S(1)}, bf16[48,128,128]{2,1,0:T(8,128)(2,1)}, u32[]{:S(2)}, u32[]{:S(2)}) collective-permute-start(bf16[48,128,128]{2,1,0:T(8,128)(2,1)S(1)} %bitcast.17), channel_id=1, source_target_pairs={{0,4},{1,5},{2,6},{3,7},{4,0},{5,1},{6,2},{7,3},{8,12},{9,13},{10,... | collective-permute-start | bytes 4718600 | tf_op jit(solution)/shard_map/ppermute | solution.py:50
  25.9 27.6 %collective-permute-start.4 = (bf16[32,64,128]{2,1,0:T(8,128)(2,1)S(1)}, bf16[32,64,128]{2,1,0:T(8,128)(2,1)}, u32[]{:S(2)}, u32[]{:S(2)}) collective-permute-start(bf16[32,64,128]{2,1,0:T(8,128)(2,1)S(1)} %all-to-all-done.refs_0_), channel_id=1, source_target_pairs={{0,16},{1,17},{2,18},{3,19},{4,132},{5,133},{6,134},{7,135},{8,24}... | collective-permute-start | bytes 1572872 | tf_op jit(solution)/shard_map/ppermute | solution.py:58
  31.6 24.6 %collective-permute-start.5 = (bf16[32,64,128]{2,1,0:T(8,128)(2,1)S(1)}, bf16[32,64,128]{2,1,0:T(8,128)(2,1)}, u32[]{:S(2)}, u32[]{:S(2)}) collective-permute-start(bf16[32,64,128]{2,1,0:T(8,128)(2,1)S(1)} %all-to-all-done.refs_0_), channel_id=1, source_target_pairs={{0,48},{1,49},{2,50},{3,51},{4,388},{5,389},{6,390},{7,391},{8,56}... | collective-permute-start | bytes 1572872 | tf_op jit(solution)/shard_map/ppermute | solution.py:58
  38.3 25.0 %collective-permute-start.2 = (bf16[32,64,128]{2,1,0:T(8,128)(2,1)S(1)}, bf16[32,64,128]{2,1,0:T(8,128)(2,1)}, u32[]{:S(2)}, u32[]{:S(2)}) collective-permute-start(bf16[32,64,128]{2,1,0:T(8,128)(2,1)S(1)} %all-to-all-done.refs_0_), channel_id=1, source_target_pairs={{0,8},{1,9},{2,10},{3,11},{4,68},{5,69},{6,70},{7,71},{8,16},{9,17... | collective-permute-start | bytes 1572872 | tf_op jit(solution)/shard_map/ppermute | solution.py:58
  43.3 3.7 %copy-start.6 = (s32[1,1,48]{2,1,0:T(1,128)S(1)}, s32[1,1,48]{2,1,0:T(1,128)}, u32[]{:S(2)}) copy-start(s32[1,1,48]{2,1,0:T(1,128)} %param.12) | copy-start | bytes 580
  43.3 3.7 %copy-start.7 = (s32[1,1,48]{2,1,0:T(1,128)S(1)}, s32[1,1,48]{2,1,0:T(1,128)}, u32[]{:S(2)}) copy-start(s32[1,1,48]{2,1,0:T(1,128)} %param.11) | copy-start | bytes 580
  43.3 49.8 %all-to-all-start.2 = ((bf16[4,320,512]{2,1,0:T(8,128)(2,1)}), bf16[4,320,512]{2,1,0:T(8,128)(2,1)S(1)}, u32[]{:S(2)}, u32[]{:S(2)}) async-start(bf16[4,320,512]{2,1,0:T(8,128)(2,1)} %broadcast_in_dim.19), calls=%async_computation.2 | async-start | bytes 2621440 | tf_op jit(solution)/shard_map/all_to_all | solution.py:46
  47.0 3.8 %collective-permute-start = (s32[97]{0:T(128)S(1)}, s32[97]{0:T(128)S(1)}, u32[]{:S(2)}, u32[]{:S(2)}) collective-permute-start(s32[97]{0:T(128)S(1)} %pad_add_fusion.1.own_n_ref), channel_id=1, source_target_pairs={{0,4},{1,5},{2,6},{3,7},{4,0},{5,1},{6,2},{7,3},{8,12},{9,13},{10,... | collective-permute-start | bytes 1172 | tf_op jit(solution)/shard_map/ppermute | solution.py:50
  50.8 28.4 %collective-permute-start.3 = (bf16[32,64,128]{2,1,0:T(8,128)(2,1)S(1)}, bf16[32,64,128]{2,1,0:T(8,128)(2,1)}, u32[]{:S(2)}, u32[]{:S(2)}) collective-permute-start(bf16[32,64,128]{2,1,0:T(8,128)(2,1)S(1)} %all-to-all-done.refs_0_), channel_id=1, source_target_pairs={{0,56},{1,57},{2,58},{3,59},{4,452},{5,453},{6,454},{7,455},{8,0},... | collective-permute-start | bytes 1572872 | tf_op jit(solution)/shard_map/ppermute | solution.py:58
  53.5 29.8 %collective-permute-start.6 = (bf16[32,64,128]{2,1,0:T(8,128)(2,1)}, bf16[32,64,128]{2,1,0:T(8,128)(2,1)}, u32[]{:S(2)}, u32[]{:S(2)}) collective-permute-start(bf16[32,64,128]{2,1,0:T(8,128)(2,1)} %collective-permute-done.4.refs_3_), channel_id=1, source_target_pairs={{0,8},{1,9},{2,10},{3,11},{4,68},{5,69},{6,70},{7,71},{8,16},{9,17... | collective-permute-start | bytes 1572872 | tf_op jit(solution)/shard_map/ppermute | solution.py:58
  56.1 27.1 %collective-permute-start.7 = (bf16[32,64,128]{2,1,0:T(8,128)(2,1)}, bf16[32,64,128]{2,1,0:T(8,128)(2,1)}, u32[]{:S(2)}, u32[]{:S(2)}) collective-permute-start(bf16[32,64,128]{2,1,0:T(8,128)(2,1)} %collective-permute-done.5.refs_4_), channel_id=1, source_target_pairs={{0,56},{1,57},{2,58},{3,59},{4,452},{5,453},{6,454},{7,455},{8,0},... | collective-permute-start | bytes 1572872 | tf_op jit(solution)/shard_map/ppermute | solution.py:58
  63.3 19.9 %collective-permute-start.8 = (bf16[16,64,128]{2,1,0:T(8,128)(2,1)}, bf16[16,64,128]{2,1,0:T(8,128)(2,1)}, u32[]{:S(2)}, u32[]{:S(2)}) collective-permute-start(bf16[16,64,128]{2,1,0:T(8,128)(2,1)} %slice.8), channel_id=1, source_target_pairs={{0,16},{1,17},{2,18},{3,19},{4,132},{5,133},{6,134},{7,135},{8,24}... | collective-permute-start | bytes 786440 | tf_op jit(solution)/shard_map/ppermute | solution.py:58
  65.3 18.0 %collective-permute-start.9 = (bf16[16,64,128]{2,1,0:T(8,128)(2,1)}, bf16[16,64,128]{2,1,0:T(8,128)(2,1)}, u32[]{:S(2)}, u32[]{:S(2)}) collective-permute-start(bf16[16,64,128]{2,1,0:T(8,128)(2,1)} %slice.9), channel_id=1, source_target_pairs={{0,48},{1,49},{2,50},{3,51},{4,388},{5,389},{6,390},{7,391},{8,56}... | collective-permute-start | bytes 786440 | tf_op jit(solution)/shard_map/ppermute | solution.py:58
  86.5 5.5 %collective-permute-start.10 = (bf16[256,512]{1,0:T(8,128)(2,1)S(1)}, bf16[256,512]{1,0:T(8,128)(2,1)S(1)}, u32[]{:S(2)}, u32[]{:S(2)}) collective-permute-start(bf16[256,512]{1,0:T(8,128)(2,1)S(1)} %get-tuple-element.25), channel_id=1, source_target_pairs={{0,4},{1,5},{2,6},{3,7},{4,0},{5,1},{6,2},{7,3},{8,12},{9,13},{10,... | collective-permute-start | bytes 786440 | tf_op jit(solution)/shard_map/ppermute | solution.py:50
  92.0 19.8 %copy-start.2 = (bf16[512,512]{1,0:T(8,128)(2,1)S(1)}, bf16[512,512]{1,0:T(8,128)(2,1)}, u32[]{:S(2)}) copy-start(bf16[512,512]{1,0:T(8,128)(2,1)} %ow_ref.1) | copy-start | bytes 1572868
  93.0 18.7 %all-to-all-start.1 = ((bf16[4,256,512]{2,1,0:T(8,128)(2,1)}), bf16[4,256,512]{2,1,0:T(8,128)(2,1)S(1)}, u32[]{:S(2)}, u32[]{:S(2)}) async-start(bf16[4,256,512]{2,1,0:T(8,128)(2,1)} %join.1), calls=%async_computation.1 | async-start | bytes 2097152 | tf_op jit(solution)/shard_map/all_to_all | solution.py:46
  111.8 1.0 copy-start.3

commit v3 on v2

--- a/solution.py
+++ b/solution.py
@@ -14,6 +14,7 @@
 F32, BF16, I32 = jnp.float32, jnp.bfloat16, jnp.int32
 NEAR = (0, 7, 1, 6, 2)
 FAR = (5, 3, 4)
+RING = [(FAR if d in FAR else NEAR).index(d) * NZ * NN for d in range(NY)] + [int(d in FAR) for d in range(NY)]
 
 
 def places():
@@ -37,8 +38,9 @@
 
 FIRST = groups(lambda z, y, c, n: (0, y) if c == 0 else (1, z))
 OVER_X = groups(lambda z, y, c, n: (z, y, c))
-OVER_ZC = groups(lambda z, y, c, n: (y, n))
-OVER_Y = groups(lambda z, y, c, n: (z, c, n))
+NEARBY = groups(lambda z, y, c, n: (z // 2, y // 2, n))
+ALONG_Y = groups(lambda z, y, c, n: (z, y % 2, c, n))
+ALONG_Z = groups(lambda z, y, c, n: (z % 2, y, c, n))
 OTHER_CORE = [(device(z, y, c, n), device(z, y, 1 - c, n)) for z, y, c, n in places()]
 
 
@@ -71,63 +73,47 @@
     )(*args)
 
 
-def place_kernel(where_ref, own_n_ref, other_n_ref, own_ref, other_ref, lo_ref, lt_ref, meta_ref, order):
+def place_kernel(where_ref, own_n_ref, other_n_ref, own_ref, other_ref, lo_ref, lt_ref, meta_ref, order, tiles, sems):
     slots, half = own_ref.shape[0], own_ref.shape[2] // 2
     side = own_ref.shape[1]
+    copies = [
+        pltpu.make_async_copy(ref, tiles.at[k], sems.at[k]) for k, ref in enumerate((own_ref, other_ref))
+    ]
+    for copy in copies:
+        copy.start()
     room = meta_ref.shape[1] - 2
     first = where_ref[0] == 0
     here = where_ref[1]
     low = lax.broadcasted_iota(I32, own_ref.shape[1:], 1) < half
-    for block, (n_ref, t_ref, l_ref) in enumerate(
-        ((own_n_ref, own_ref, lo_ref), (other_n_ref, other_ref, lt_ref))
-    ):
+    for block, (n_ref, l_ref) in enumerate(((own_n_ref, lo_ref), (other_n_ref, lt_ref))):
         count = n_ref[2 * slots]
-
-        def clear(k, carry, block=block):
+        for k in range(room):
             order[k] = -1
             meta_ref[block, k] = 0
-            return carry
-
-        lax.fori_loop(0, room, clear, 0)
-
-        def looked_up(s, n_ref=n_ref):
+
+        def assign(s, carry, block=block, n_ref=n_ref):
+            near, far = carry
             col = n_ref[slots + s]
             z, y = lax.shift_right_logical(col, 3), lax.bitwise_and(col, 7)
             ring = jnp.where(first, y, z)
             inner = jnp.where(first, z, y)
-            away = lax.bitwise_and(ring - here + 8, 7)
-            return away, inner
-
-        def tally(s, near):
-            away, _ = looked_up(s)
-            return near + jnp.where((away >= 3) & (away <= 5), 0, 1)
-
-        near = lax.fori_loop(0, count, tally, 0)
+            away = lax.bitwise_and(ring - here + NY, NY - 1)
+            is_far = where_ref[2 + NY + away]
+            at = jnp.where(is_far == 1, room - 1 - far, near)
+            order[at] = s
+            meta_ref[block, at] = where_ref[2 + away] + inner * NN
+            return near + 1 - is_far, far + is_far
+
+        near, far = lax.fori_loop(0, count, assign, (jnp.int32(0), jnp.int32(0)))
         near_turns = lax.shift_right_logical(near + STEP - 1, 3)
-        far_turns = lax.shift_right_logical(count - near + STEP - 1, 3)
+        far_turns = lax.shift_right_logical(far + STEP - 1, 3)
         meta_ref[block, room] = near_turns
-        meta_ref[block, room + 1] = near_turns + far_turns
-
-        def assign(s, carry, block=block):
-            near_at, far_at = carry
-            away, inner = looked_up(s)
-            far = (away >= 3) & (away <= 5)
-            base = jnp.int32(0)
-            for among in (NEAR, FAR):
-                for k, distance in enumerate(among):
-                    base = jnp.where(away == distance, k, base)
-            at = jnp.where(far, far_at, near_at)
-            order[at] = s
-            meta_ref[block, at] = base * (NZ * NN) + inner * NN
-            step = jnp.where(far, 1, 0)
-            return near_at + 1 - step, far_at + step
-
-        lax.fori_loop(0, count, assign, (0, near_turns * STEP))
-
-        def one_pair(p, carry, n_ref=n_ref, t_ref=t_ref, l_ref=l_ref):
+        meta_ref[block, room + 1] = room // STEP - far_turns
+
+        def one_pair(p, carry, block=block, n_ref=n_ref, l_ref=l_ref):
             slot_a, slot_b = order[2 * p], order[2 * p + 1]
             at_a, at_b = jnp.maximum(slot_a, 0), jnp.maximum(slot_b, 0)
-            a, b = t_ref[at_a].astype(F32), t_ref[at_b].astype(F32)
+            a, b = tiles[block, at_a].astype(F32), tiles[block, at_b].astype(F32)
             moved = pltpu.roll(jnp.where(first, b, a), half, 1)
             both = jnp.where(low, jnp.where(first, a, moved), jnp.where(first, moved, b))
             row_a = jnp.where(slot_a >= 0, n_ref[at_a], -1)
@@ -137,7 +123,9 @@
                 l_ref[p, r * side:(r + 1) * side, :] = jnp.where(rows == r, both, 0.0).astype(BF16)
             return carry
 
-        lax.fori_loop(0, (near_turns + far_turns) * (STEP // 2), one_pair, 0)
+        copies[block].wait()
+        lax.fori_loop(0, near_turns * (STEP // 2), one_pair, 0)
+        lax.fori_loop((room // STEP - far_turns) * (STEP // 2), room // 2, one_pair, 0)
 
 
 def add_turns(meta_ref, block, first_turn, last_turn, l_ref, blocks, acc):
@@ -166,6 +154,22 @@
     return copies
 
 
+def spread_kernel(f_ref, out_ref):
+    quarter = out_ref.shape[1]
+    for j in range(out_ref.shape[0]):
+        out_ref[j] = f_ref[j % NN * quarter:(j % NN + 1) * quarter, :]
+
+
+def pack_kernel(nw_ref, rw_ref, f_ref, w_ref):
+    side = nw_ref.shape[0]
+    quarter = f_ref.shape[0] // NN
+    for j in range(NN):
+        w_ref[j, :side, :] = nw_ref[...]
+        w_ref[j, side:2 * side, :] = rw_ref[...]
+        for q in range(NN):
+            w_ref[j, 2 * side:, q * side:(q + 1) * side] = f_ref[q * quarter:(q + 1) * quarter, :]
+
+
 def near_kernel(meta_ref, lo_ref, lt_ref, *refs):
     *given, po_ref, pt_ref, blocks, sems = refs
     room = meta_ref.shape[1] - 2
@@ -186,9 +190,9 @@
     po_ref[...] = no_ref[...]
     for copy in copies:
         copy.wait()
-    add_turns(meta_ref, 1, meta_ref[1, room], meta_ref[1, room + 1], lt_ref, blocks, acc)
+    add_turns(meta_ref, 1, meta_ref[1, room + 1], room // STEP, lt_ref, blocks, acc)
     pt_ref[...] = acc[...].astype(BF16)
-    add_turns(meta_ref, 0, meta_ref[0, room], meta_ref[0, room + 1], lo_ref, blocks, po_ref)
+    add_turns(meta_ref, 0, meta_ref[0, room + 1], room // STEP, lo_ref, blocks, po_ref)
 
 
 def join_kernel(own_ref, came_ref, out_ref):
@@ -284,9 +288,18 @@
     other_tiles = swap_cores(tiles)
     other_numbers = swap_cores(numbers)
 
-    pieces = jnp.broadcast_to(
-        features.reshape(1, NN, quarter, side), (NZ, NN, quarter, side)
-    ).reshape(NZ * NN, quarter, side)
+    pieces = call(
+        spread_kernel,
+        "spread",
+        jax.ShapeDtypeStruct((NZ * NN, quarter, side), BF16),
+        [VMEM],
+        VMEM,
+        [],
+        4,
+        10**5,
+        10**6,
+        features,
+    )
     line = exchange(pieces, FIRST)
 
     turns = (slots + 2 * STEP - 2) // STEP
@@ -295,39 +308,47 @@
         place_kernel,
         "place",
         (placed, placed, jax.ShapeDtypeStruct((2, turns * STEP + 2), I32)),
-        [SMEM, SMEM, SMEM, VMEM, VMEM],
+        [SMEM, SMEM, SMEM, ANY, ANY],
         (VMEM, VMEM, SMEM),
-        [pltpu.SMEM((turns * STEP,), I32)],
+        [
+            pltpu.SMEM((turns * STEP,), I32),
+            pltpu.VMEM((2, *tiles.shape), BF16),
+            pltpu.SemaphoreType.DMA((2,)),
+        ],
         10,
         10**7,
         7 * 10**6,
-        jnp.stack([core, here]).astype(I32),
+        jnp.concatenate([jnp.stack([core, here]).astype(I32), jnp.array(RING, I32)]),
         numbers,
         other_numbers,
         tiles,
         other_tiles,
     )
 
-    weights = jnp.concatenate(
-        [
-            neighbor_weight,
-            root_weight,
-            features.reshape(NN, quarter, side).swapaxes(0, 1).reshape(quarter, width),
-        ],
-        axis=0,
-    )
-    line, weights = lax.optimization_barrier((line, weights))
-    all_weights = exchange(jnp.broadcast_to(weights[None], (NN, *weights.shape)), OVER_X)
-
+    weights = call(
+        pack_kernel,
+        "pack",
+        jax.ShapeDtypeStruct((NN, 2 * side + quarter, width), BF16),
+        [VMEM, VMEM, VMEM],
+        VMEM,
+        [],
+        4,
+        10**5,
+        2 * 10**6,
+        neighbor_weight,
+        root_weight,
+        features,
+    )
+    line, meta, weights = lax.optimization_barrier((line, meta, weights))
+    all_weights = exchange(weights, OVER_X)
     by_distance = {0: line}
     for hops in (1, -1, 2, -2):
         by_distance[-hops % NY] = pass_on(line, hops)
+    arrived = lax.optimization_barrier([by_distance[d] for d in NEAR[1:]])
+    by_distance.update(zip(NEAR[1:], arrived))
+    by_distance[4] = pass_on(by_distance[6], 2)
     for hops in (1, -1):
         by_distance[-3 * hops % NY] = pass_on(by_distance[-2 * hops % NY], hops)
-    middle = NZ * NN // 2
-    far_low = pass_on(by_distance[6][:middle], 2)
-    far_high = pass_on(by_distance[2][middle:], -2)
-
     whole = jax.ShapeDtypeStruct((rows, width), F32)
     flops = 2 * slots * rows * quarter * width
     line_size = NZ * NN
@@ -353,12 +374,12 @@
         far_kernel,
         "far",
         (whole, jax.ShapeDtypeStruct((rows, width), BF16)),
-        [SMEM, VMEM, VMEM, VMEM, VMEM] + [ANY] * (len(FAR) + 1),
+        [SMEM, VMEM, VMEM, VMEM, VMEM] + [ANY] * len(FAR),
         (VMEM, VMEM),
         [
             pltpu.VMEM((rows, width), F32),
             pltpu.VMEM((len(FAR) * line_size, quarter, side), BF16),
-            pltpu.SemaphoreType.DMA((len(FAR) + 1,)),
+            pltpu.SemaphoreType.DMA((len(FAR),)),
         ],
         20,
         flops // 2,
@@ -368,10 +389,7 @@
         left_other,
         near_own,
         near_other,
-        by_distance[FAR[0]],
-        by_distance[FAR[1]],
-        far_low,
-        far_high,
+        *[by_distance[d] for d in FAR],
     )
     copies = call(
         join_kernel,
@@ -409,7 +427,8 @@
         output_weight,
     )
 
-    chunk = 3 * NN * side // (NZ * NC)
+    nearby = len(NEARBY[0])
+    chunk = 3 * NN * side // nearby
 
     def total(pieces, count):
         return call(
@@ -425,9 +444,10 @@
             pieces,
         )
 
-    summed = total(exchange(grads.reshape(NZ * NC, chunk, side), OVER_ZC), NY)
-    summed = total(exchange(summed, OVER_Y), NZ * NC)
-    full = exchange(summed, OVER_ZC).reshape(3 * NN, side, side)
+    summed = total(exchange(grads.reshape(nearby, chunk, side), NEARBY), NY // 2)
+    summed = total(exchange(summed, ALONG_Y), NZ // 2)
+    summed = total(exchange(summed, ALONG_Z), nearby)
+    full = exchange(summed, NEARBY).reshape(3 * NN, side, side)
     return layer_output, *call(
         last_kernel,
         "last",

time: 172 us -> 173 us (level)
  waiting for transfers between devices: 23.1 us -> 40.8 us
  starting transfers between devices: 63.8 us -> 53.8 us
  Pallas kernels: 19.3 us -> 14.2 us
  blocking collectives: 55.4 us -> 53.3 us
    ppermute x8 -> x7, waiting for transfers between devices: 0.02 us -> 24.9 us  [pass_on(): return lax.ppermute(value, AXES, pairs)]
    unnamed x17 -> x28, local copies, waits for them, and re-layouts: 0.99 us -> 8.01 us
    all_to_all x3, starting transfers between devices: 18.4 us -> 11.7 us  [exchange(): lax.all_to_all(pieces, AXES, 0, 0, axis_index_groups=groups_, tiled=True)]
    ppermute x8 -> x7, starting transfers between devices: 32 us -> 25.6 us  [pass_on(): return lax.ppermute(value, AXES, pairs)]
    all_to_all x3, waiting for transfers between devices: 21.1 us -> 14.8 us  [exchange(): lax.all_to_all(pieces, AXES, 0, 0, axis_index_groups=groups_, tiled=True)]
    pallas_call x8 -> x11, Pallas kernels: 19.3 us -> 14.2 us  [call(): pl.pallas_call(kernel, out_shape=out_shape, in_specs=in_specs, out_specs=...]
    slice x2 -> x0, local copies, waits for them, and re-layouts: 3.34 us -> none  [the longest x1 1.67 us: per_device(): far_low = pass_on(by_distance[6][:middle], 2)]
    broadcast_in_dim x3 -> x0, local copies, waits for them, and re-layouts: 3.12 us -> none  [the longest x2 1.95 us: per_device(): jnp.broadcast_to(features.reshape(1, NN, quarter, side), (NZ, NN, quarter...]
  transfers between devices with their start and end apart: 14 -> 13, of which waited for: 4 -> 7; matrix products, arithmetic and copies ran while one was open for 3% -> 0% of each run, Pallas kernels for 10% -> 7%
where the time goes in v3:
time: 173 us; the launch traced here: 172 us
  starting transfers between devices  53.8 us (31%)
  blocking collectives  53.3 us (31%)
  waiting for transfers between devices  40.8 us (24%)
  Pallas kernels  14.2 us (8%)
  local copies, waits for them, and re-layouts  8.01 us (5%)
    all_to_all x4, blocking collectives, exchange(): lax.all_to_all(pieces, AXES, 0, 0, axis_index_groups=groups_, tiled=True)  53.3 us
    ppermute x7, starting transfers between devices, pass_on(): return lax.ppermute(value, AXES, pairs)  25.6 us
    ppermute x7, waiting for transfers between devices, pass_on(): return lax.ppermute(value, AXES, pairs)  24.9 us
    ppermute x3, starting transfers between devices, swap_cores(): return lax.ppermute(value, AXES, OTHER_CORE)  16.4 us
    all_to_all x3, waiting for transfers between devices, exchange(): lax.all_to_all(pieces, AXES, 0, 0, axis_index_groups=groups_, tiled=True)  14.8 us
    pallas_call x11, Pallas kernels, call(): pl.pallas_call(kernel, out_shape=out_shape, in_specs=in_specs, out_specs=...  14.2 us
    all_to_all x3, starting transfers between devices, exchange(): lax.all_to_all(pieces, AXES, 0, 0, axis_index_groups=groups_, tiled=True)  11.7 us
    unnamed x28, local copies, waits for them, and re-layouts  8.01 us
  transfers between devices with their start and end apart: 13, of which 7 were waited for; matrix products, arithmetic and copies ran while one was open for 0% of the time, Pallas kernels for 7%

profile of v3, /device:TPU:1, one launch (start us, length us, event | category | flops | bytes accessed | tf_op | source)
XLA Modules:
  0.0 171.9 jit_solution(6800131102774379223)
XLA Ops:
  0.7 8.9 %collective-permute-start.1 = (bf16[48,128,128]{2,1,0:T(8,128)(2,1)}, bf16[48,128,128]{2,1,0:T(8,128)(2,1)S(1)}, u32[]{:S(2)}, u32[]{:S(2)}) collective-permute-start(bf16[48,128,128]{2,1,0:T(8,128)(2,1)} %bitcast.10), channel_id=1, source_target_pairs={{0,4},{1,5},{2,6},{3,7},{4,0},{5,1},{6,2},{7,3},{8,12},{9,13},{10,... | collective-permute-start | bytes 4718600 | tf_op jit(solution)/shard_map/ppermute | solution.py:52
  11.3 4.6 %all-to-all-start = ((bf16[32,64,128]{2,1,0:T(8,128)(2,1)}), bf16[32,64,128]{2,1,0:T(8,128)(2,1)}, u32[]{:S(2)}, u32[]{:S(2)}) async-start(bf16[32,64,128]{2,1,0:T(8,128)(2,1)} %spread.1), calls=%async_computation | async-start | bytes 1048576 | tf_op jit(solution)/shard_map/all_to_all | solution.py:48
  16.7 5.2 %collective-permute-start = (s32[97]{0:T(128)S(1)}, s32[97]{0:T(128)S(1)}, u32[]{:S(2)}, u32[]{:S(2)}) collective-permute-start(s32[97]{0:T(128)S(1)} %pad_add_fusion.1.own_n_ref), channel_id=1, source_target_pairs={{0,4},{1,5},{2,6},{3,7},{4,0},{5,1},{6,2},{7,3},{8,12},{9,13},{10,... | collective-permute-start | bytes 1172 | tf_op jit(solution)/shard_map/ppermute | solution.py:52
  23.8 1.2 pack.1
  25.0 1.2 copy-done.3
  26.2 1.4 copy-done.4
  27.6 3.8 %place.1 = (bf16[28,256,128]{2,1,0:T(8,128)(2,1)S(1)}, bf16[28,256,128]{2,1,0:T(8,128)(2,1)S(1)}, s32[2,58]{1,0:T(2,128)S(1)}) custom-call(s32[18]{0:T(128)S(1)} %pad_add_fusion.where_ref, s32[97]{0:T(128)S(1)} %pad_add_fusion.1.own_n_ref, s32[97]{0:T(128)S(1)} %collective-permute-done.other_n_ref, bf16[48,128,128]{2,1,0:T(8,128)(2,1)S(1)} %bitcast.11, ...), custom_call_target="tpu_custom_call" | custom-call | flops 10000000 | bytes 7000000 | tf_op jit(solution)/shard_map/place/pallas_call | solution.py:64
  31.5 1.3 copy-done
  32.7 9.2 %collective-permute-start.5 = (bf16[32,64,128]{2,1,0:T(8,128)(2,1)}, bf16[32,64,128]{2,1,0:T(8,128)(2,1)}, u32[]{:S(2)}, u32[]{:S(2)}) collective-permute-start(bf16[32,64,128]{2,1,0:T(8,128)(2,1)} %all-to-all-done.refs_0_), channel_id=1, source_target_pairs={{0,48},{1,49},{2,50},{3,51},{4,388},{5,389},{6,390},{7,391},{8,56}... | collective-permute-start | bytes 1572872 | tf_op jit(solution)/shard_map/ppermute | solution.py:60
  41.9 1.9 %collective-permute-start.4 = (bf16[32,64,128]{2,1,0:T(8,128)(2,1)}, bf16[32,64,128]{2,1,0:T(8,128)(2,1)}, u32[]{:S(2)}, u32[]{:S(2)}) collective-permute-start(bf16[32,64,128]{2,1,0:T(8,128)(2,1)} %all-to-all-done.refs_0_), channel_id=1, source_target_pairs={{0,16},{1,17},{2,18},{3,19},{4,132},{5,133},{6,134},{7,135},{8,24}... | collective-permute-start | bytes 1572872 | tf_op jit(solution)/shard_map/ppermute | solution.py:60
  43.8 5.4 %collective-permute-start.3 = (bf16[32,64,128]{2,1,0:T(8,128)(2,1)}, bf16[32,64,128]{2,1,0:T(8,128)(2,1)}, u32[]{:S(2)}, u32[]{:S(2)}) collective-permute-start(bf16[32,64,128]{2,1,0:T(8,128)(2,1)} %all-to-all-done.refs_0_), channel_id=1, source_target_pairs={{0,56},{1,57},{2,58},{3,59},{4,452},{5,453},{6,454},{7,455},{8,0},... | collective-permute-start | bytes 1572872 | tf_op jit(solution)/shard_map/ppermute | solution.py:60
  49.3 1.9 %collective-permute-start.2 = (bf16[32,64,128]{2,1,0:T(8,128)(2,1)}, bf16[32,64,128]{2,1,0:T(8,128)(2,1)}, u32[]{:S(2)}, u32[]{:S(2)}) collective-permute-start(bf16[32,64,128]{2,1,0:T(8,128)(2,1)} %all-to-all-done.refs_0_), channel_id=1, source_target_pairs={{0,8},{1,9},{2,10},{3,11},{4,68},{5,69},{6,70},{7,71},{8,16},{9,17... | collective-permute-start | bytes 1572872 | tf_op jit(solution)/shard_map/ppermute | solution.py:60
  51.2 3.6 %all-to-all-start.2 = ((bf16[4,320,512]{2,1,0:T(8,128)(2,1)}), bf16[4,320,512]{2,1,0:T(8,128)(2,1)S(1)}, u32[]{:S(2)}, u32[]{:S(2)}) async-start(bf16[4,320,512]{2,1,0:T(8,128)(2,1)} %pack.1), calls=%async_computation.2 | async-start | bytes 2621440 | tf_op jit(solution)/shard_map/all_to_all | solution.py:48
  54.8 5.2 %collective-permute-done.4.refs_3_ = bf16[32,64,128]{2,1,0:T(8,128)(2,1)} collective-permute-done((bf16[32,64,128]{2,1,0:T(8,128)(2,1)}, bf16[32,64,128]{2,1,0:T(8,128)(2,1)}, u32[]{:S(2)}, u32[]{:S(2)}) %collective-permute-start.4) | collective-permute-done | bytes 524320 | tf_op jit(solution)/shard_map/ppermute | solution.py:60
  60.1 5.5 %collective-permute-done.2.refs_1_ = bf16[32,64,128]{2,1,0:T(8,128)(2,1)} collective-permute-done((bf16[32,64,128]{2,1,0:T(8,128)(2,1)}, bf16[32,64,128]{2,1,0:T(8,128)(2,1)}, u32[]{:S(2)}, u32[]{:S(2)}) %collective-permute-start.2) | collective-permute-done | bytes 524320 | tf_op jit(solution)/shard_map/ppermute | solution.py:60
  65.6 2.3 %collective-permute-start.7 = (bf16[32,64,128]{2,1,0:T(8,128)(2,1)}, bf16[32,64,128]{2,1,0:T(8,128)(2,1)S(1)}, u32[]{:S(2)}, u32[]{:S(2)}) collective-permute-start(bf16[32,64,128]{2,1,0:T(8,128)(2,1)} %collective-permute-done.5.refs_4_), channel_id=1, source_target_pairs={{0,56},{1,57},{2,58},{3,59},{4,452},{5,453},{6,454},{7,455},{8,0},... | collective-permute-start | bytes 1572872 | tf_op jit(solution)/shard_map/ppermute | solution.py:60
  67.9 2.3 %collective-permute-start.8 = (bf16[32,64,128]{2,1,0:T(8,128)(2,1)}, bf16[32,64,128]{2,1,0:T(8,128)(2,1)S(1)}, u32[]{:S(2)}, u32[]{:S(2)}) collective-permute-start(bf16[32,64,128]{2,1,0:T(8,128)(2,1)} %collective-permute-done.4.refs_3_), channel_id=1, source_target_pairs={{0,16},{1,17},{2,18},{3,19},{4,132},{5,133},{6,134},{7,135},{8,24}... | collective-permute-start | bytes 1572872 | tf_op jit(solution)/shard_map/ppermute | solution.py:60
  70.3 2.6 %collective-permute-start.6 = (bf16[32,64,128]{2,1,0:T(8,128)(2,1)}, bf16[32,64,128]{2,1,0:T(8,128)(2,1)S(1)}, u32[]{:S(2)}, u32[]{:S(2)}) collective-permute-start(bf16[32,64,128]{2,1,0:T(8,128)(2,1)} %collective-permute-done.4.refs_3_), channel_id=1, source_target_pairs={{0,8},{1,9},{2,10},{3,11},{4,68},{5,69},{6,70},{7,71},{8,16},{9,17... | collective-permute-start | bytes 1572872 | tf_op jit(solution)/shard_map/ppermute | solution.py:60
  72.8 1.5 copy-done.1
  74.3 3.2 %near.1 = (f32[256,512]{1,0:T(8,128)S(1)}, f32[256,512]{1,0:T(8,128)S(1)}) custom-call(s32[2,58]{1,0:T(2,128)S(1)} %get-tuple-element.24.meta_ref, bf16[28,256,128]{2,1,0:T(8,128)(2,1)S(1)} %get-tuple-element.25.lo_ref, bf16[28,256,128]{2,1,0:T(8,128)(2,1)S(1)} %copy-done.1, bf16[32,64,128]{2,1,0:T(8,128)(2,1)} %all-to-all-done.refs_0_, ...), custom_call_target="tpu_custom_call" | custom-call | flops 805306368 | bytes 8000000 | tf_op jit(solution)/shard_map/near/pallas_call | solution.py:64
  77.5 8.5 %collective-permute-done.8.refs_2_ = bf16[32,64,128]{2,1,0:T(8,128)(2,1)S(1)} collective-permute-done((bf16[32,64,128]{2,1,0:T(8,128)(2,1)}, bf16[32,64,128]{2,1,0:T(8,128)(2,1)S(1)}, u32[]{:S(2)}, u32[]{:S(2)}) %collective-permute-start.8) | collective-permute-done | bytes 524320 | tf_op jit(solution)/shard_map/ppermute | solution.py:60
  86.1 5.5 %collective-permute-done.6.refs_0_ = bf16[32,64,128]{2,1,0:T(8,128)(2,1)S(1)} collective-permute-done((bf16[32,64,128]{2,1,0:T(8,128)(2,1)}, bf16[32,64,128]{2,1,0:T(8,128)(2,1)S(1)}, u32[]{:S(2)}, u32[]{:S(2)}) %collective-permute-start.6) | collective-permute-done | bytes 524320 | tf_op jit(solution)/shard_map/ppermute | solution.py:60
  91.5 1.4 far.1
  93.0 2.3 %collective-permute-start.9 = (bf16[256,512]{1,0:T(8,128)(2,1)S(1)}, bf16[256,512]{1,0:T(8,128)(2,1)S(1)}, u32[]{:S(2)}, u32[]{:S(2)}) collective-permute-start(bf16[256,512]{1,0:T(8,128)(2,1)S(1)} %get-tuple-element.35), channel_id=1, source_target_pairs={{0,4},{1,5},{2,6},{3,7},{4,0},{5,1},{6,2},{7,3},{8,12},{9,13},{10,... | collective-permute-start | bytes 786440 | tf_op jit(solution)/shard_map/ppermute | solution.py:52
  95.3 1.1 collective-permute-done.9.came_ref
  97.5 3.5 %all-to-all-start.1 = ((bf16[4,256,512]{2,1,0:T(8,128)(2,1)}), bf16[4,256,512]{2,1,0:T(8,128)(2,1)S(1)}, u32[]{:S(2)}, u32[]{:S(2)}) async-start(bf16[4,256,512]{2,1,0:T(8,128)(2,1)} %join.1), calls=%async_computation.1 | async-start | bytes 2097152 | tf_op jit(solution)/shard_map/all_to_all | solution.py:48
  101.0 14.8 %all-to-all-done.1.a_ref = bf16[4,256,512]{2,1,0:T(8,128)(2,1)S(1)} async-done(((bf16[4,256,512]{2,1,0:T(8,128)(2,1)}), bf16[4,256,512]{2,1,0:T(8,128)(2,1)S(1)}, u32[]{:S(2)}, u32[]{:S(2)}) %all-to-all-start.1) | async-done | bytes 1048608 | tf_op jit(solution)/shard_map/all_to_all | solution.py:48
  115.8 1.7 dense.1
  117.5 12.4 %all_to_all.35.in_ref = bf16[8,192,128]{2,1,0:T(8,128)(2,1)S(1)} all-to-all(bf16[8,192,128]{2,1,0:T(8,128)(2,1)S(1)} %bitcast.13), channel_id=1, replica_groups={{0,4,8,12,64,68,72,76},{1,5,9,13,65,69,73,77},{2,6,10,14,66,70,74,78},{..., dimensions={0} | all-to-all | bytes 786432 | tf_op jit(solution)/shard_map/all_to_all | solution.py:48
  130.0 13.1 %all_to_all.36.in_ref = bf16[4,192,128]{2,1,0:T(8,128)(2,1)S(1)} all-to-all(bf16[4,192,128]{2,1,0:T(8,128)(2,1)S(1)} %total.3), channel_id=1, replica_groups={{0,16,32,48},{1,17,33,49},{2,18,34,50},{3,19,35,51},{4,20,36,52},{5,21,..., dimensions={0} | all-to-all | bytes 393216 | tf_op jit(solution)/shard_map/all_to_all | solution.py:48
  143.1 13.7 %all_to_all.37.in_ref = bf16[4,192,128]{2,1,0:T(8,128)(2,1)S(1)} all-to-all(bf16[4,192,128]{2,1,0:T(8,128)(2,1)S(1)} %total.4), channel_id=1, replica_groups={{0,128,256,384},{1,129,257,385},{2,130,258,386},{3,131,259,387},{4,132,..., dimensions={0} | all-to-all | bytes 393216 | tf_op jit(solution)/shard_map/all_to_all | solution.py:48
  156.8 14.1 %all_to_all.38 = bf16[8,192,128]{2,1,0:T(8,128)(2,1)S(1)} all-to-all(bf16[8,192,128]{2,1,0:T(8,128)(2,1)S(1)} %total.5), channel_id=1, replica_groups={{0,4,8,12,64,68,72,76},{1,5,9,13,65,69,73,77},{2,6,10,14,66,70,74,78},{..., dimensions={0} | all-to-all | bytes 786432 | tf_op jit(solution)/shard_map/all_to_all | solution.py:48
  (39 shorter events, 6.0 us)
Async XLA Ops:
  0.6 21.3 %copy-start.13 = (s32[16]{0:T(128)S(1)}, s32[16]{0:T(128)}, u32[]{:S(2)}) copy-start(s32[16]{0:T(128)} %constant.57.clone) | copy-start | bytes 196
  0.6 15.9 %copy-start.11 = (s32[1,1,48]{2,1,0:T(1,128)S(1)}, s32[1,1,48]{2,1,0:T(1,128)}, u32[]{:S(2)}) copy-start(s32[1,1,48]{2,1,0:T(1,128)} %param.13) | copy-start | bytes 580
  0.7 15.9 %copy-start.12 = (s32[1,1,48]{2,1,0:T(1,128)S(1)}, s32[1,1,48]{2,1,0:T(1,128)}, u32[]{:S(2)}) copy-start(s32[1,1,48]{2,1,0:T(1,128)} %param.12) | copy-start | bytes 580
  0.7 25.5 %copy-start.2 = (bf16[1,1,48,128,128]{4,3,2,1,0:T(8,128)(2,1)S(1)}, bf16[1,1,48,128,128]{4,3,2,1,0:T(8,128)(2,1)}, u32[]{:S(2)}) copy-start(bf16[1,1,48,128,128]{4,3,2,1,0:T(8,128)(2,1)} %param.11) | copy-start | bytes 4718596
  0.7 24.3 %collective-permute-start.1 = (bf16[48,128,128]{2,1,0:T(8,128)(2,1)}, bf16[48,128,128]{2,1,0:T(8,128)(2,1)S(1)}, u32[]{:S(2)}, u32[]{:S(2)}) collective-permute-start(bf16[48,128,128]{2,1,0:T(8,128)(2,1)} %bitcast.10), channel_id=1, source_target_pairs={{0,4},{1,5},{2,6},{3,7},{4,0},{5,1},{6,2},{7,3},{8,12},{9,13},{10,... | collective-permute-start | bytes 4718600 | tf_op jit(solution)/shard_map/ppermute | solution.py:52
  9.6 0.8 copy-start.5
  10.4 11.6 %copy-start.6 = (bf16[256,128]{1,0:T(8,128)(2,1)S(1)}, bf16[256,128]{1,0:T(8,128)(2,1)}, u32[]{:S(2)}) copy-start(bf16[256,128]{1,0:T(8,128)(2,1)} %f_ref.5) | copy-start | bytes 196612
  11.3 21.4 %all-to-all-start = ((bf16[32,64,128]{2,1,0:T(8,128)(2,1)}), bf16[32,64,128]{2,1,0:T(8,128)(2,1)}, u32[]{:S(2)}, u32[]{:S(2)}) async-start(bf16[32,64,128]{2,1,0:T(8,128)(2,1)} %spread.1), calls=%async_computation | async-start | bytes 1048576 | tf_op jit(solution)/shard_map/all_to_all | solution.py:48
  16.7 8.3 %collective-permute-start = (s32[97]{0:T(128)S(1)}, s32[97]{0:T(128)S(1)}, u32[]{:S(2)}, u32[]{:S(2)}) collective-permute-start(s32[97]{0:T(128)S(1)} %pad_add_fusion.1.own_n_ref), channel_id=1, source_target_pairs={{0,4},{1,5},{2,6},{3,7},{4,0},{5,1},{6,2},{7,3},{8,12},{9,13},{10,... | collective-permute-start | bytes 1172 | tf_op jit(solution)/shard_map/ppermute | solution.py:52
  22.0 0.9 copy-start.9
  22.9 0.9 copy-start.10
  25.0 1.2 copy-start.3
  26.2 1.4 copy-start.4
  31.4 1.3 copy-start
  32.7 22.0 %collective-permute-start.5 = (bf16[32,64,128]{2,1,0:T(8,128)(2,1)}, bf16[32,64,128]{2,1,0:T(8,128)(2,1)}, u32[]{:S(2)}, u32[]{:S(2)}) collective-permute-start(bf16[32,64,128]{2,1,0:T(8,128)(2,1)} %all-to-all-done.refs_0_), channel_id=1, source_target_pairs={{0,48},{1,49},{2,50},{3,51},{4,388},{5,389},{6,390},{7,391},{8,56}... | collective-permute-start | bytes 1572872 | tf_op jit(solution)/shard_map/ppermute | solution.py:60
  41.9 18.1 %collective-permute-start.4 = (bf16[32,64,128]{2,1,0:T(8,128)(2,1)}, bf16[32,64,128]{2,1,0:T(8,128)(2,1)}, u32[]{:S(2)}, u32[]{:S(2)}) collective-permute-start(bf16[32,64,128]{2,1,0:T(8,128)(2,1)} %all-to-all-done.refs_0_), channel_id=1, source_target_pairs={{0,16},{1,17},{2,18},{3,19},{4,132},{5,133},{6,134},{7,135},{8,24}... | collective-permute-start | bytes 1572872 | tf_op jit(solution)/shard_map/ppermute | solution.py:60
  43.8 16.3 %collective-permute-start.3 = (bf16[32,64,128]{2,1,0:T(8,128)(2,1)}, bf16[32,64,128]{2,1,0:T(8,128)(2,1)}, u32[]{:S(2)}, u32[]{:S(2)}) collective-permute-start(bf16[32,64,128]{2,1,0:T(8,128)(2,1)} %all-to-all-done.refs_0_), channel_id=1, source_target_pairs={{0,56},{1,57},{2,58},{3,59},{4,452},{5,453},{6,454},{7,455},{8,0},... | collective-permute-start | bytes 1572872 | tf_op jit(solution)/shard_map/ppermute | solution.py:60
  49.3 16.4 %collective-permute-start.2 = (bf16[32,64,128]{2,1,0:T(8,128)(2,1)}, bf16[32,64,128]{2,1,0:T(8,128)(2,1)}, u32[]{:S(2)}, u32[]{:S(2)}) collective-permute-start(bf16[32,64,128]{2,1,0:T(8,128)(2,1)} %all-to-all-done.refs_0_), channel_id=1, source_target_pairs={{0,8},{1,9},{2,10},{3,11},{4,68},{5,69},{6,70},{7,71},{8,16},{9,17... | collective-permute-start | bytes 1572872 | tf_op jit(solution)/shard_map/ppermute | solution.py:60
  51.2 46.3 %all-to-all-start.2 = ((bf16[4,320,512]{2,1,0:T(8,128)(2,1)}), bf16[4,320,512]{2,1,0:T(8,128)(2,1)S(1)}, u32[]{:S(2)}, u32[]{:S(2)}) async-start(bf16[4,320,512]{2,1,0:T(8,128)(2,1)} %pack.1), calls=%async_computation.2 | async-start | bytes 2621440 | tf_op jit(solution)/shard_map/all_to_all | solution.py:48
  65.6 11.9 %collective-permute-start.7 = (bf16[32,64,128]{2,1,0:T(8,128)(2,1)}, bf16[32,64,128]{2,1,0:T(8,128)(2,1)S(1)}, u32[]{:S(2)}, u32[]{:S(2)}) collective-permute-start(bf16[32,64,128]{2,1,0:T(8,128)(2,1)} %collective-permute-done.5.refs_4_), channel_id=1, source_target_pairs={{0,56},{1,57},{2,58},{3,59},{4,452},{5,453},{6,454},{7,455},{8,0},... | collective-permute-start | bytes 1572872 | tf_op jit(solution)/shard_map/ppermute | solution.py:60
  67.9 18.1 %collective-permute-start.8 = (bf16[32,64,128]{2,1,0:T(8,128)(2,1)}, bf16[32,64,128]{2,1,0:T(8,128)(2,1)S(1)}, u32[]{:S(2)}, u32[]{:S(2)}) collective-permute-start(bf16[32,64,128]{2,1,0:T(8,128)(2,1)} %collective-permute-done.4.refs_3_), channel_id=1, source_target_pairs={{0,16},{1,17},{2,18},{3,19},{4,132},{5,133},{6,134},{7,135},{8,24}... | collective-permute-start | bytes 1572872 | tf_op jit(solution)/shard_map/ppermute | solution.py:60
  70.3 21.3 %collective-permute-start.6 = (bf16[32,64,128]{2,1,0:T(8,128)(2,1)}, bf16[32,64,128]{2,1,0:T(8,128)(2,1)S(1)}, u32[]{:S(2)}, u32[]{:S(2)}) collective-permute-start(bf16[32,64,128]{2,1,0:T(8,128)(2,1)} %collective-permute-done.4.refs_3_), channel_id=1, source_target_pairs={{0,8},{1,9},{2,10},{3,11},{4,68},{5,69},{6,70},{7,71},{8,16},{9,17... | collective-permute-start | bytes 1572872 | tf_op jit(solution)/shard_map/ppermute | solution.py:60
  72.8 1.5 copy-start.1
  93.0 3.5 %collective-permute-start.9 = (bf16[256,512]{1,0:T(8,128)(2,1)S(1)}, bf16[256,512]{1,0:T(8,128)(2,1)S(1)}, u32[]{:S(2)}, u32[]{:S(2)}) collective-permute-start(bf16[256,512]{1,0:T(8,128)(2,1)S(1)} %get-tuple-element.35), channel_id=1, source_target_pairs={{0,4},{1,5},{2,6},{3,7},{4,0},{5,1},{6,2},{7,3},{8,12},{9,13},{10,... | collective-permute-start | bytes 786440 | tf_op jit(solution)/shard_map/ppermute | solution.py:52
  96.4 19.4 %copy-start.7 = (bf16[512,512]{1,0:T(8,128)(2,1)S(1)}, bf16[512,512]{1,0:T(8,128)(2,1)}, u32[]{:S(2)}) copy-start(bf16[512,512]{1,0:T(8,128)(2,1)} %ow_ref.1) | copy-start | bytes 1572868
  96.4 19.4 %copy-start.8 = (bf16[256,512]{1,0:T(8,128)(2,1)S(1)}, bf16[256,512]{1,0:T(8,128)(2,1)}, u32[]{:S(2)}) copy-start(bf16[256,512]{1,0:T(8,128)(2,1)} %cot_ref.1) | copy-start | bytes 786436
  97.5 18.3 %all-to-all-start.1 = ((bf16[4,256,512]{2,1,0:T(8,128)(2,1)}), bf16[4,256,512]{2,1,0:T(8,128)(2,1)S(1)}, u32[]{:S(2)}, u32[]{:S(2)}) async-start(bf16[4,256,512]{2,1,0:T(8,128)(2,1)} %join.1), calls=%async_computation.1 | async-start | bytes 2097152 | tf_op jit(solution)/shard_map/all_to_all | solution.py:48

commit v4 on v3

--- a/solution.py
+++ b/solution.py
@@ -12,8 +12,8 @@
 SMEM = pl.BlockSpec(memory_space=pltpu.SMEM)
 ANY = pl.BlockSpec(memory_space=pl.ANY)
 F32, BF16, I32 = jnp.float32, jnp.bfloat16, jnp.int32
-NEAR = (0, 7, 1, 6, 2)
-FAR = (5, 3, 4)
+NEAR = (0, 6, 2, 7, 1)
+FAR = (4, 5, 3)
 RING = [(FAR if d in FAR else NEAR).index(d) * NZ * NN for d in range(NY)] + [int(d in FAR) for d in range(NY)]
 
 
@@ -195,10 +195,12 @@
     add_turns(meta_ref, 0, meta_ref[0, room + 1], room // STEP, lo_ref, blocks, po_ref)
 
 
-def join_kernel(own_ref, came_ref, out_ref):
+def join_kernel(own_ref, came_ref, *out_refs):
     joined = (own_ref[...] + came_ref[...].astype(F32)).astype(BF16)
-    for j in range(out_ref.shape[0]):
-        out_ref[j] = joined
+    part = joined.shape[1] // len(out_refs)
+    for k, out_ref in enumerate(out_refs):
+        for j in range(out_ref.shape[0]):
+            out_ref[j] = joined[:, k * part:(k + 1) * part]
 
 
 def total_kernel(in_ref, out_ref):
@@ -218,7 +220,7 @@
         output_ref[j * side:(j + 1) * side, :] = in_ref[2 * NN + j].astype(F32)
 
 
-def dense_kernel(n_ref, a_ref, w_ref, f_ref, cot_ref, ow_ref, out_ref, g_ref, agg_ref):
+def dense_kernel(n_ref, a_ref, b_ref, w_ref, f_ref, cot_ref, ow_ref, out_ref, g_ref, agg_ref):
     side = f_ref.shape[1]
     quarter = w_ref.shape[1] - 2 * side
     mine = pl.ds(pl.multiple_of(n_ref[0] * side, side), side)
@@ -236,10 +238,13 @@
     hidden_grad = lax.dot_general(
         cot_ref[...], ow_ref[...], (((1,), (1,)), ((), ())), preferred_element_type=F32
     )
-    agg = a_ref[0].astype(F32)
-    for j in range(1, NN):
-        agg = agg + a_ref[j].astype(F32)
-    agg = agg.astype(BF16)
+    halves = []
+    for half_ref in (a_ref, b_ref):
+        half = half_ref[0].astype(F32)
+        for j in range(1, NN):
+            half = half + half_ref[j].astype(F32)
+        halves.append(half.astype(BF16))
+    agg = jnp.concatenate(halves, axis=1)
     agg_ref[...] = agg
     pre = jnp.dot(agg, neighbor_weight, preferred_element_type=F32) + jnp.dot(
         rows, root_weight, preferred_element_type=F32
@@ -302,6 +307,30 @@
     )
     line = exchange(pieces, FIRST)
 
+    weights = call(
+        pack_kernel,
+        "pack",
+        jax.ShapeDtypeStruct((NN, 2 * side + quarter, width), BF16),
+        [VMEM, VMEM, VMEM],
+        VMEM,
+        [],
+        4,
+        10**5,
+        2 * 10**6,
+        neighbor_weight,
+        root_weight,
+        features,
+    )
+    line, weights, other_numbers = lax.optimization_barrier((line, weights, other_numbers))
+    all_weights = exchange(weights, OVER_X)
+    by_distance = {0: line}
+    for hops in (2, -2, 1, -1):
+        by_distance[-hops % NY] = pass_on(line, hops)
+    arrived = lax.optimization_barrier([by_distance[d] for d in NEAR[1:]])
+    by_distance.update(zip(NEAR[1:], arrived))
+    for hops in (1, -1):
+        by_distance[-3 * hops % NY] = pass_on(by_distance[-2 * hops % NY], hops)
+    by_distance[4] = pass_on(by_distance[6], 2)
     turns = (slots + 2 * STEP - 2) // STEP
     placed = jax.ShapeDtypeStruct((turns * STEP // 2, rows, side), BF16)
     left_own, left_other, meta = call(
@@ -325,30 +354,6 @@
         other_tiles,
     )
 
-    weights = call(
-        pack_kernel,
-        "pack",
-        jax.ShapeDtypeStruct((NN, 2 * side + quarter, width), BF16),
-        [VMEM, VMEM, VMEM],
-        VMEM,
-        [],
-        4,
-        10**5,
-        2 * 10**6,
-        neighbor_weight,
-        root_weight,
-        features,
-    )
-    line, meta, weights = lax.optimization_barrier((line, meta, weights))
-    all_weights = exchange(weights, OVER_X)
-    by_distance = {0: line}
-    for hops in (1, -1, 2, -2):
-        by_distance[-hops % NY] = pass_on(line, hops)
-    arrived = lax.optimization_barrier([by_distance[d] for d in NEAR[1:]])
-    by_distance.update(zip(NEAR[1:], arrived))
-    by_distance[4] = pass_on(by_distance[6], 2)
-    for hops in (1, -1):
-        by_distance[-3 * hops % NY] = pass_on(by_distance[-2 * hops % NY], hops)
     whole = jax.ShapeDtypeStruct((rows, width), F32)
     flops = 2 * slots * rows * quarter * width
     line_size = NZ * NN
@@ -394,9 +399,9 @@
     copies = call(
         join_kernel,
         "join",
-        jax.ShapeDtypeStruct((NN, rows, width), BF16),
+        (jax.ShapeDtypeStruct((NN, rows, width // 2), BF16),) * 2,
         [VMEM, VMEM],
-        VMEM,
+        (VMEM, VMEM),
         [],
         8,
         10**6,
@@ -404,7 +409,7 @@
         part_own,
         swap_cores(part_other),
     )
-    parts = exchange(copies, OVER_X)
+    parts = [exchange(copy, OVER_X) for copy in copies]
 
     layer_output, grads = call(
         dense_kernel,
@@ -413,14 +418,14 @@
             jax.ShapeDtypeStruct((rows, side), BF16),
             jax.ShapeDtypeStruct((3 * NN, side, side), BF16),
         ),
-        [SMEM] + [VMEM] * 5,
+        [SMEM] + [VMEM] * 6,
         (VMEM, VMEM),
         [pltpu.VMEM((rows, width), BF16)],
         16,
         12 * rows * width * width,
         5 * 10**6,
         narrow[None],
-        parts,
+        *parts,
         all_weights,
         features,
         cotangent,

time: 173 us -> 168 us (0.971)
  waiting for transfers between devices: 40.8 us -> 25.1 us
  blocking collectives: 53.3 us -> 62 us
  starting transfers between devices: 53.8 us -> 59.9 us
  local copies, waits for them, and re-layouts: 8.01 us -> 3.73 us
    ppermute x7, waiting for transfers between devices: 24.9 us -> 15.5 us  [pass_on(): return lax.ppermute(value, AXES, pairs)]
    all_to_all x4 -> x5, blocking collectives: 53.3 us -> 62 us  [exchange(): lax.all_to_all(pieces, AXES, 0, 0, axis_index_groups=groups_, tiled=True)]
    all_to_all x3, waiting for transfers between devices: 14.8 us -> 8.43 us  [exchange(): lax.all_to_all(pieces, AXES, 0, 0, axis_index_groups=groups_, tiled=True)]
    all_to_all x3, starting transfers between devices: 11.7 us -> 17.5 us  [exchange(): lax.all_to_all(pieces, AXES, 0, 0, axis_index_groups=groups_, tiled=True)]
    unnamed x28 -> x20, local copies, waits for them, and re-layouts: 8.01 us -> 3.73 us
    ppermute x7, starting transfers between devices: 25.6 us -> 28.5 us  [pass_on(): return lax.ppermute(value, AXES, pairs)]
    ppermute x3, starting transfers between devices: 16.4 us -> 13.9 us  [swap_cores(): return lax.ppermute(value, AXES, OTHER_CORE)]
  transfers between devices with their start and end apart: 13 -> 13, of which waited for: 7 -> 8; matrix products, arithmetic and copies ran while one was open for 0% -> 0% of each run, Pallas kernels for 7% -> 6%
where the time goes in v4:
time: 168 us; the launch traced here: 167 us
  blocking collectives  62 us (37%)
  starting transfers between devices  59.9 us (36%)
  waiting for transfers between devices  25.1 us (15%)
  Pallas kernels  14.4 us (9%)
  local copies, waits for them, and re-layouts  3.73 us (2%)
    all_to_all x5, blocking collectives, exchange(): lax.all_to_all(pieces, AXES, 0, 0, axis_index_groups=groups_, tiled=True)  62 us
    ppermute x7, starting transfers between devices, pass_on(): return lax.ppermute(value, AXES, pairs)  28.5 us
    all_to_all x3, starting transfers between devices, exchange(): lax.all_to_all(pieces, AXES, 0, 0, axis_index_groups=groups_, tiled=True)  17.5 us
    ppermute x7, waiting for transfers between devices, pass_on(): return lax.ppermute(value, AXES, pairs)  15.5 us
    pallas_call x11, Pallas kernels, call(): pl.pallas_call(kernel, out_shape=out_shape, in_specs=in_specs, out_specs=...  14.4 us
    ppermute x3, starting transfers between devices, swap_cores(): return lax.ppermute(value, AXES, OTHER_CORE)  13.9 us
    all_to_all x3, waiting for transfers between devices, exchange(): lax.all_to_all(pieces, AXES, 0, 0, axis_index_groups=groups_, tiled=True)  8.43 us
    unnamed x20, local copies, waits for them, and re-layouts  3.73 us
  transfers between devices with their start and end apart: 13, of which 8 were waited for; matrix products, arithmetic and copies ran while one was open for 0% of the time, Pallas kernels for 6%

profile of v4, /device:TPU:1, one launch (start us, length us, event | category | flops | bytes accessed | tf_op | source)
XLA Modules:
  0.0 166.8 jit_solution(17669451729187802637)
XLA Ops:
  2.5 10.5 %all-to-all-start = ((bf16[32,64,128]{2,1,0:T(8,128)(2,1)}), bf16[32,64,128]{2,1,0:T(8,128)(2,1)S(1)}, u32[]{:S(2)}, u32[]{:S(2)}) async-start(bf16[32,64,128]{2,1,0:T(8,128)(2,1)} %spread.1), calls=%async_computation | async-start | bytes 1048576 | tf_op jit(solution)/shard_map/all_to_all | solution.py:48
  13.0 6.1 %collective-permute-start.1 = (bf16[48,128,128]{2,1,0:T(8,128)(2,1)S(1)}, bf16[48,128,128]{2,1,0:T(8,128)(2,1)}, u32[]{:S(2)}, u32[]{:S(2)}) collective-permute-start(bf16[48,128,128]{2,1,0:T(8,128)(2,1)S(1)} %bitcast.10), channel_id=1, source_target_pairs={{0,4},{1,5},{2,6},{3,7},{4,0},{5,1},{6,2},{7,3},{8,12},{9,13},{10,... | collective-permute-start | bytes 4718600 | tf_op jit(solution)/shard_map/ppermute | solution.py:52
  19.8 1.9 %collective-permute-start = (s32[97]{0:T(128)S(1)}, s32[97]{0:T(128)S(1)}, u32[]{:S(2)}, u32[]{:S(2)}) collective-permute-start(s32[97]{0:T(128)S(1)} %pad_add_fusion.1.own_n_ref), channel_id=1, source_target_pairs={{0,4},{1,5},{2,6},{3,7},{4,0},{5,1},{6,2},{7,3},{8,12},{9,13},{10,... | collective-permute-start | bytes 1172 | tf_op jit(solution)/shard_map/ppermute | solution.py:52
  23.6 1.2 pack.1
  24.7 1.1 all-to-all-done.refs_0_
  25.8 5.7 %collective-permute-start.2 = (bf16[32,64,128]{2,1,0:T(8,128)(2,1)S(1)}, bf16[32,64,128]{2,1,0:T(8,128)(2,1)}, u32[]{:S(2)}, u32[]{:S(2)}) collective-permute-start(bf16[32,64,128]{2,1,0:T(8,128)(2,1)S(1)} %all-to-all-done.refs_0_), channel_id=1, source_target_pairs={{0,16},{1,17},{2,18},{3,19},{4,132},{5,133},{6,134},{7,135},{8,24}... | collective-permute-start | bytes 1572872 | tf_op jit(solution)/shard_map/ppermute | solution.py:60
  31.5 6.8 %collective-permute-start.3 = (bf16[32,64,128]{2,1,0:T(8,128)(2,1)S(1)}, bf16[32,64,128]{2,1,0:T(8,128)(2,1)}, u32[]{:S(2)}, u32[]{:S(2)}) collective-permute-start(bf16[32,64,128]{2,1,0:T(8,128)(2,1)S(1)} %all-to-all-done.refs_0_), channel_id=1, source_target_pairs={{0,48},{1,49},{2,50},{3,51},{4,388},{5,389},{6,390},{7,391},{8,56}... | collective-permute-start | bytes 1572872 | tf_op jit(solution)/shard_map/ppermute | solution.py:60
  38.3 3.1 %collective-permute-start.4 = (bf16[32,64,128]{2,1,0:T(8,128)(2,1)S(1)}, bf16[32,64,128]{2,1,0:T(8,128)(2,1)}, u32[]{:S(2)}, u32[]{:S(2)}) collective-permute-start(bf16[32,64,128]{2,1,0:T(8,128)(2,1)S(1)} %all-to-all-done.refs_0_), channel_id=1, source_target_pairs={{0,8},{1,9},{2,10},{3,11},{4,68},{5,69},{6,70},{7,71},{8,16},{9,17... | collective-permute-start | bytes 1572872 | tf_op jit(solution)/shard_map/ppermute | solution.py:60
  41.4 3.4 %collective-permute-start.5 = (bf16[32,64,128]{2,1,0:T(8,128)(2,1)S(1)}, bf16[32,64,128]{2,1,0:T(8,128)(2,1)}, u32[]{:S(2)}, u32[]{:S(2)}) collective-permute-start(bf16[32,64,128]{2,1,0:T(8,128)(2,1)S(1)} %all-to-all-done.refs_0_), channel_id=1, source_target_pairs={{0,56},{1,57},{2,58},{3,59},{4,452},{5,453},{6,454},{7,455},{8,0},... | collective-permute-start | bytes 1572872 | tf_op jit(solution)/shard_map/ppermute | solution.py:60
  44.8 3.6 %all-to-all-start.3 = ((bf16[4,320,512]{2,1,0:T(8,128)(2,1)}), bf16[4,320,512]{2,1,0:T(8,128)(2,1)S(1)}, u32[]{:S(2)}, u32[]{:S(2)}) async-start(bf16[4,320,512]{2,1,0:T(8,128)(2,1)} %pack.1), calls=%async_computation.3 | async-start | bytes 2621440 | tf_op jit(solution)/shard_map/all_to_all | solution.py:48
  48.3 2.2 %collective-permute-done.3.refs_2_ = bf16[32,64,128]{2,1,0:T(8,128)(2,1)} collective-permute-done((bf16[32,64,128]{2,1,0:T(8,128)(2,1)S(1)}, bf16[32,64,128]{2,1,0:T(8,128)(2,1)}, u32[]{:S(2)}, u32[]{:S(2)}) %collective-permute-start.3) | collective-permute-done | bytes 524320 | tf_op jit(solution)/shard_map/ppermute | solution.py:60
  50.5 4.1 %collective-permute-done.4.refs_3_ = bf16[32,64,128]{2,1,0:T(8,128)(2,1)} collective-permute-done((bf16[32,64,128]{2,1,0:T(8,128)(2,1)S(1)}, bf16[32,64,128]{2,1,0:T(8,128)(2,1)}, u32[]{:S(2)}, u32[]{:S(2)}) %collective-permute-start.4) | collective-permute-done | bytes 524320 | tf_op jit(solution)/shard_map/ppermute | solution.py:60
  54.6 2.2 %collective-permute-done.5.refs_4_ = bf16[32,64,128]{2,1,0:T(8,128)(2,1)} collective-permute-done((bf16[32,64,128]{2,1,0:T(8,128)(2,1)S(1)}, bf16[32,64,128]{2,1,0:T(8,128)(2,1)}, u32[]{:S(2)}, u32[]{:S(2)}) %collective-permute-start.5) | collective-permute-done | bytes 524320 | tf_op jit(solution)/shard_map/ppermute | solution.py:60
  56.8 3.0 %collective-permute-start.6 = (bf16[32,64,128]{2,1,0:T(8,128)(2,1)}, bf16[32,64,128]{2,1,0:T(8,128)(2,1)}, u32[]{:S(2)}, u32[]{:S(2)}) collective-permute-start(bf16[32,64,128]{2,1,0:T(8,128)(2,1)} %collective-permute-done.2.refs_1_), channel_id=1, source_target_pairs={{0,16},{1,17},{2,18},{3,19},{4,132},{5,133},{6,134},{7,135},{8,24}... | collective-permute-start | bytes 1572872 | tf_op jit(solution)/shard_map/ppermute | solution.py:60
  59.8 4.4 %collective-permute-start.7 = (bf16[32,64,128]{2,1,0:T(8,128)(2,1)}, bf16[32,64,128]{2,1,0:T(8,128)(2,1)}, u32[]{:S(2)}, u32[]{:S(2)}) collective-permute-start(bf16[32,64,128]{2,1,0:T(8,128)(2,1)} %collective-permute-done.2.refs_1_), channel_id=1, source_target_pairs={{0,8},{1,9},{2,10},{3,11},{4,68},{5,69},{6,70},{7,71},{8,16},{9,17... | collective-permute-start | bytes 1572872 | tf_op jit(solution)/shard_map/ppermute | solution.py:60
  64.3 2.1 %collective-permute-start.8 = (bf16[32,64,128]{2,1,0:T(8,128)(2,1)}, bf16[32,64,128]{2,1,0:T(8,128)(2,1)}, u32[]{:S(2)}, u32[]{:S(2)}) collective-permute-start(bf16[32,64,128]{2,1,0:T(8,128)(2,1)} %collective-permute-done.3.refs_2_), channel_id=1, source_target_pairs={{0,56},{1,57},{2,58},{3,59},{4,452},{5,453},{6,454},{7,455},{8,0},... | collective-permute-start | bytes 1572872 | tf_op jit(solution)/shard_map/ppermute | solution.py:60
  66.5 3.4 %place.1 = (bf16[28,256,128]{2,1,0:T(8,128)(2,1)S(1)}, bf16[28,256,128]{2,1,0:T(8,128)(2,1)S(1)}, s32[2,58]{1,0:T(2,128)S(1)}) custom-call(s32[18]{0:T(128)S(1)} %pad_add_fusion.where_ref, s32[97]{0:T(128)S(1)} %pad_add_fusion.1.own_n_ref, s32[97]{0:T(128)S(1)} %collective-permute-done.other_n_ref, bf16[48,128,128]{2,1,0:T(8,128)(2,1)S(1)} %bitcast.11, ...), custom_call_target="tpu_custom_call" | custom-call | flops 10000000 | bytes 7000000 | tf_op jit(solution)/shard_map/place/pallas_call | solution.py:64
  69.9 2.8 %near.1 = (f32[256,512]{1,0:T(8,128)S(1)}, f32[256,512]{1,0:T(8,128)S(1)}) custom-call(s32[2,58]{1,0:T(2,128)S(1)} %get-tuple-element.26.meta_ref, bf16[28,256,128]{2,1,0:T(8,128)(2,1)S(1)} %get-tuple-element.27.lo_ref, bf16[28,256,128]{2,1,0:T(8,128)(2,1)S(1)} %get-tuple-element.28.lt_ref, bf16[32,64,128]{2,1,0:T(8,128)(2,1)S(1)} %all-to-all-done.refs_0_, ...), custom_call_target="tpu_custom_call" | custom-call | flops 805306368 | bytes 8000000 | tf_op jit(solution)/shard_map/near/pallas_call | solution.py:64
  72.7 2.2 %collective-permute-done.6.refs_0_ = bf16[32,64,128]{2,1,0:T(8,128)(2,1)} collective-permute-done((bf16[32,64,128]{2,1,0:T(8,128)(2,1)}, bf16[32,64,128]{2,1,0:T(8,128)(2,1)}, u32[]{:S(2)}, u32[]{:S(2)}) %collective-permute-start.6) | collective-permute-done | bytes 524320 | tf_op jit(solution)/shard_map/ppermute | solution.py:60
  74.9 4.8 %collective-permute-done.7.refs_1_ = bf16[32,64,128]{2,1,0:T(8,128)(2,1)} collective-permute-done((bf16[32,64,128]{2,1,0:T(8,128)(2,1)}, bf16[32,64,128]{2,1,0:T(8,128)(2,1)}, u32[]{:S(2)}, u32[]{:S(2)}) %collective-permute-start.7) | collective-permute-done | bytes 524320 | tf_op jit(solution)/shard_map/ppermute | solution.py:60
  79.7 2.6 %far.1 = (f32[256,512]{1,0:T(8,128)S(1)}, bf16[256,512]{1,0:T(8,128)(2,1)S(1)}) custom-call(s32[2,58]{1,0:T(2,128)S(1)} %get-tuple-element.26.meta_ref, bf16[28,256,128]{2,1,0:T(8,128)(2,1)S(1)} %get-tuple-element.27.lo_ref, bf16[28,256,128]{2,1,0:T(8,128)(2,1)S(1)} %get-tuple-element.28.lt_ref, f32[256,512]{1,0:T(8,128)S(1)} %get-tuple-element.34.no_ref, ...), custom_call_target="tpu_custom_call" | custom-call | flops 402653184 | bytes 6000000 | tf_op jit(solution)/shard_map/far/pallas_call | solution.py:64
  82.3 5.9 %collective-permute-start.9 = (bf16[256,512]{1,0:T(8,128)(2,1)S(1)}, bf16[256,512]{1,0:T(8,128)(2,1)S(1)}, u32[]{:S(2)}, u32[]{:S(2)}) collective-permute-start(bf16[256,512]{1,0:T(8,128)(2,1)S(1)} %get-tuple-element.37), channel_id=1, source_target_pairs={{0,4},{1,5},{2,6},{3,7},{4,0},{5,1},{6,2},{7,3},{8,12},{9,13},{10,... | collective-permute-start | bytes 786440 | tf_op jit(solution)/shard_map/ppermute | solution.py:52
  88.2 1.1 collective-permute-done.9.came_ref
  90.3 11.5 %all_to_all.40.a_ref = bf16[4,256,256]{2,1,0:T(8,128)(2,1)S(1)} all-to-all(bf16[4,256,256]{2,1,0:T(8,128)(2,1)S(1)} %get-tuple-element.38), channel_id=1, replica_groups={{0,1,2,3},{4,5,6,7},{8,9,10,11},{12,13,14,15},{16,17,18,19},{20,21,22,2..., dimensions={0} | all-to-all | bytes 1048576 | tf_op jit(solution)/shard_map/all_to_all | solution.py:48
  101.7 3.5 %all-to-all-start.2 = ((bf16[4,256,256]{2,1,0:T(8,128)(2,1)}), bf16[4,256,256]{2,1,0:T(8,128)(2,1)S(1)}, u32[]{:S(2)}, u32[]{:S(2)}) async-start(bf16[4,256,256]{2,1,0:T(8,128)(2,1)} %get-tuple-element.39), calls=%async_computation.2 | async-start | bytes 1048576 | tf_op jit(solution)/shard_map/all_to_all | solution.py:48
  105.2 7.4 %all-to-all-done.2.b_ref = bf16[4,256,256]{2,1,0:T(8,128)(2,1)S(1)} async-done(((bf16[4,256,256]{2,1,0:T(8,128)(2,1)}), bf16[4,256,256]{2,1,0:T(8,128)(2,1)S(1)}, u32[]{:S(2)}, u32[]{:S(2)}) %all-to-all-start.2) | async-done | bytes 524320 | tf_op jit(solution)/shard_map/all_to_all | solution.py:48
  112.6 0.9 copy-done.4
  113.5 1.7 %dense.1 = (bf16[256,128]{1,0:T(8,128)(2,1)}, bf16[12,128,128]{2,1,0:T(8,128)(2,1)S(1)}) custom-call(s32[1]{0:T(128)} %bitcast.n_ref, bf16[4,256,256]{2,1,0:T(8,128)(2,1)S(1)} %all_to_all.40.a_ref, bf16[4,256,256]{2,1,0:T(8,128)(2,1)S(1)} %all-to-all-done.2.b_ref, bf16[4,320,512]{2,1,0:T(8,128)(2,1)S(1)} %all-to-all-done.3.w_ref, ...), custom_call_target="tpu_custom_call" | custom-call | flops 805306368 | bytes 5000000 | tf_op jit(solution)/shard_map/dense/pallas_call | solution.py:64
  115.2 13.5 %all_to_all.41.in_ref = bf16[8,192,128]{2,1,0:T(8,128)(2,1)S(1)} all-to-all(bf16[8,192,128]{2,1,0:T(8,128)(2,1)S(1)} %bitcast.13), channel_id=1, replica_groups={{0,4,8,12,64,68,72,76},{1,5,9,13,65,69,73,77},{2,6,10,14,66,70,74,78},{..., dimensions={0} | all-to-all | bytes 786432 | tf_op jit(solution)/shard_map/all_to_all | solution.py:48
  128.8 12.3 %all_to_all.42.in_ref = bf16[4,192,128]{2,1,0:T(8,128)(2,1)S(1)} all-to-all(bf16[4,192,128]{2,1,0:T(8,128)(2,1)S(1)} %total.3), channel_id=1, replica_groups={{0,16,32,48},{1,17,33,49},{2,18,34,50},{3,19,35,51},{4,20,36,52},{5,21,..., dimensions={0} | all-to-all | bytes 393216 | tf_op jit(solution)/shard_map/all_to_all | solution.py:48
  141.1 10.6 %all_to_all.43.in_ref = bf16[4,192,128]{2,1,0:T(8,128)(2,1)S(1)} all-to-all(bf16[4,192,128]{2,1,0:T(8,128)(2,1)S(1)} %total.4), channel_id=1, replica_groups={{0,128,256,384},{1,129,257,385},{2,130,258,386},{3,131,259,387},{4,132,..., dimensions={0} | all-to-all | bytes 393216 | tf_op jit(solution)/shard_map/all_to_all | solution.py:48
  151.7 14.2 %all_to_all.44 = bf16[8,192,128]{2,1,0:T(8,128)(2,1)S(1)} all-to-all(bf16[8,192,128]{2,1,0:T(8,128)(2,1)S(1)} %total.5), channel_id=1, replica_groups={{0,4,8,12,64,68,72,76},{1,5,9,13,65,69,73,77},{2,6,10,14,66,70,74,78},{..., dimensions={0} | all-to-all | bytes 786432 | tf_op jit(solution)/shard_map/all_to_all | solution.py:48
  (32 shorter events, 5.7 us)
Async XLA Ops:
  0.6 12.4 %copy-start = (bf16[1,1,48,128,128]{4,3,2,1,0:T(8,128)(2,1)S(1)}, bf16[1,1,48,128,128]{4,3,2,1,0:T(8,128)(2,1)}, u32[]{:S(2)}) copy-start(bf16[1,1,48,128,128]{4,3,2,1,0:T(8,128)(2,1)} %param.11) | copy-start | bytes 4718596
  0.6 1.0 copy-start.1
  1.6 18.1 %copy-start.7 = (s32[1,1,48]{2,1,0:T(1,128)S(1)}, s32[1,1,48]{2,1,0:T(1,128)}, u32[]{:S(2)}) copy-start(s32[1,1,48]{2,1,0:T(1,128)} %param.13) | copy-start | bytes 580
  1.6 18.1 %copy-start.8 = (s32[1,1,48]{2,1,0:T(1,128)S(1)}, s32[1,1,48]{2,1,0:T(1,128)}, u32[]{:S(2)}) copy-start(s32[1,1,48]{2,1,0:T(1,128)} %param.12) | copy-start | bytes 580
  1.6 20.1 %copy-start.2 = (bf16[256,128]{1,0:T(8,128)(2,1)S(1)}, bf16[256,128]{1,0:T(8,128)(2,1)}, u32[]{:S(2)}) copy-start(bf16[256,128]{1,0:T(8,128)(2,1)} %f_ref.5) | copy-start | bytes 196612
  2.5 23.3 %all-to-all-start = ((bf16[32,64,128]{2,1,0:T(8,128)(2,1)}), bf16[32,64,128]{2,1,0:T(8,128)(2,1)S(1)}, u32[]{:S(2)}, u32[]{:S(2)}) async-start(bf16[32,64,128]{2,1,0:T(8,128)(2,1)} %spread.1), calls=%async_computation | async-start | bytes 1048576 | tf_op jit(solution)/shard_map/all_to_all | solution.py:48
  13.0 53.5 %collective-permute-start.1 = (bf16[48,128,128]{2,1,0:T(8,128)(2,1)S(1)}, bf16[48,128,128]{2,1,0:T(8,128)(2,1)}, u32[]{:S(2)}, u32[]{:S(2)}) collective-permute-start(bf16[48,128,128]{2,1,0:T(8,128)(2,1)S(1)} %bitcast.10), channel_id=1, source_target_pairs={{0,4},{1,5},{2,6},{3,7},{4,0},{5,1},{6,2},{7,3},{8,12},{9,13},{10,... | collective-permute-start | bytes 4718600 | tf_op jit(solution)/shard_map/ppermute | solution.py:52
  19.8 4.9 %collective-permute-start = (s32[97]{0:T(128)S(1)}, s32[97]{0:T(128)S(1)}, u32[]{:S(2)}, u32[]{:S(2)}) collective-permute-start(s32[97]{0:T(128)S(1)} %pad_add_fusion.1.own_n_ref), channel_id=1, source_target_pairs={{0,4},{1,5},{2,6},{3,7},{4,0},{5,1},{6,2},{7,3},{8,12},{9,13},{10,... | collective-permute-start | bytes 1172 | tf_op jit(solution)/shard_map/ppermute | solution.py:52
  21.8 0.9 copy-start.5
  22.7 0.9 copy-start.6
  24.7 41.7 %copy-start.9 = (s32[16]{0:T(128)S(1)}, s32[16]{0:T(128)}, u32[]{:S(2)}) copy-start(s32[16]{0:T(128)} %constant.57.clone) | copy-start | bytes 196
  25.8 22.5 %collective-permute-start.2 = (bf16[32,64,128]{2,1,0:T(8,128)(2,1)S(1)}, bf16[32,64,128]{2,1,0:T(8,128)(2,1)}, u32[]{:S(2)}, u32[]{:S(2)}) collective-permute-start(bf16[32,64,128]{2,1,0:T(8,128)(2,1)S(1)} %all-to-all-done.refs_0_), channel_id=1, source_target_pairs={{0,16},{1,17},{2,18},{3,19},{4,132},{5,133},{6,134},{7,135},{8,24}... | collective-permute-start | bytes 1572872 | tf_op jit(solution)/shard_map/ppermute | solution.py:60
  31.5 19.0 %collective-permute-start.3 = (bf16[32,64,128]{2,1,0:T(8,128)(2,1)S(1)}, bf16[32,64,128]{2,1,0:T(8,128)(2,1)}, u32[]{:S(2)}, u32[]{:S(2)}) collective-permute-start(bf16[32,64,128]{2,1,0:T(8,128)(2,1)S(1)} %all-to-all-done.refs_0_), channel_id=1, source_target_pairs={{0,48},{1,49},{2,50},{3,51},{4,388},{5,389},{6,390},{7,391},{8,56}... | collective-permute-start | bytes 1572872 | tf_op jit(solution)/shard_map/ppermute | solution.py:60
  38.3 16.3 %collective-permute-start.4 = (bf16[32,64,128]{2,1,0:T(8,128)(2,1)S(1)}, bf16[32,64,128]{2,1,0:T(8,128)(2,1)}, u32[]{:S(2)}, u32[]{:S(2)}) collective-permute-start(bf16[32,64,128]{2,1,0:T(8,128)(2,1)S(1)} %all-to-all-done.refs_0_), channel_id=1, source_target_pairs={{0,8},{1,9},{2,10},{3,11},{4,68},{5,69},{6,70},{7,71},{8,16},{9,17... | collective-permute-start | bytes 1572872 | tf_op jit(solution)/shard_map/ppermute | solution.py:60
  41.4 15.4 %collective-permute-start.5 = (bf16[32,64,128]{2,1,0:T(8,128)(2,1)S(1)}, bf16[32,64,128]{2,1,0:T(8,128)(2,1)}, u32[]{:S(2)}, u32[]{:S(2)}) collective-permute-start(bf16[32,64,128]{2,1,0:T(8,128)(2,1)S(1)} %all-to-all-done.refs_0_), channel_id=1, source_target_pairs={{0,56},{1,57},{2,58},{3,59},{4,452},{5,453},{6,454},{7,455},{8,0},... | collective-permute-start | bytes 1572872 | tf_op jit(solution)/shard_map/ppermute | solution.py:60
  44.8 45.5 %all-to-all-start.3 = ((bf16[4,320,512]{2,1,0:T(8,128)(2,1)}), bf16[4,320,512]{2,1,0:T(8,128)(2,1)S(1)}, u32[]{:S(2)}, u32[]{:S(2)}) async-start(bf16[4,320,512]{2,1,0:T(8,128)(2,1)} %pack.1), calls=%async_computation.3 | async-start | bytes 2621440 | tf_op jit(solution)/shard_map/all_to_all | solution.py:48
  56.8 18.1 %collective-permute-start.6 = (bf16[32,64,128]{2,1,0:T(8,128)(2,1)}, bf16[32,64,128]{2,1,0:T(8,128)(2,1)}, u32[]{:S(2)}, u32[]{:S(2)}) collective-permute-start(bf16[32,64,128]{2,1,0:T(8,128)(2,1)} %collective-permute-done.2.refs_1_), channel_id=1, source_target_pairs={{0,16},{1,17},{2,18},{3,19},{4,132},{5,133},{6,134},{7,135},{8,24}... | collective-permute-start | bytes 1572872 | tf_op jit(solution)/shard_map/ppermute | solution.py:60
  59.8 19.9 %collective-permute-start.7 = (bf16[32,64,128]{2,1,0:T(8,128)(2,1)}, bf16[32,64,128]{2,1,0:T(8,128)(2,1)}, u32[]{:S(2)}, u32[]{:S(2)}) collective-permute-start(bf16[32,64,128]{2,1,0:T(8,128)(2,1)} %collective-permute-done.2.refs_1_), channel_id=1, source_target_pairs={{0,8},{1,9},{2,10},{3,11},{4,68},{5,69},{6,70},{7,71},{8,16},{9,17... | collective-permute-start | bytes 1572872 | tf_op jit(solution)/shard_map/ppermute | solution.py:60
  64.3 15.5 %collective-permute-start.8 = (bf16[32,64,128]{2,1,0:T(8,128)(2,1)}, bf16[32,64,128]{2,1,0:T(8,128)(2,1)}, u32[]{:S(2)}, u32[]{:S(2)}) collective-permute-start(bf16[32,64,128]{2,1,0:T(8,128)(2,1)} %collective-permute-done.3.refs_2_), channel_id=1, source_target_pairs={{0,56},{1,57},{2,58},{3,59},{4,452},{5,453},{6,454},{7,455},{8,0},... | collective-permute-start | bytes 1572872 | tf_op jit(solution)/shard_map/ppermute | solution.py:60
  82.3 30.3 %copy-start.3 = (bf16[512,512]{1,0:T(8,128)(2,1)S(1)}, bf16[512,512]{1,0:T(8,128)(2,1)}, u32[]{:S(2)}) copy-start(bf16[512,512]{1,0:T(8,128)(2,1)} %ow_ref.1) | copy-start | bytes 1572868
  82.3 7.1 %collective-permute-start.9 = (bf16[256,512]{1,0:T(8,128)(2,1)S(1)}, bf16[256,512]{1,0:T(8,128)(2,1)S(1)}, u32[]{:S(2)}, u32[]{:S(2)}) collective-permute-start(bf16[256,512]{1,0:T(8,128)(2,1)S(1)} %get-tuple-element.37), channel_id=1, source_target_pairs={{0,4},{1,5},{2,6},{3,7},{4,0},{5,1},{6,2},{7,3},{8,12},{9,13},{10,... | collective-permute-start | bytes 786440 | tf_op jit(solution)/shard_map/ppermute | solution.py:52
  101.7 10.8 %all-to-all-start.2 = ((bf16[4,256,256]{2,1,0:T(8,128)(2,1)}), bf16[4,256,256]{2,1,0:T(8,128)(2,1)S(1)}, u32[]{:S(2)}, u32[]{:S(2)}) async-start(bf16[4,256,256]{2,1,0:T(8,128)(2,1)} %get-tuple-element.39), calls=%async_computation.2 | async-start | bytes 1048576 | tf_op jit(solution)/shard_map/all_to_all | solution.py:48
  112.6 1.0 copy-start.4

commit v5 on v4

--- a/solution.py
+++ b/solution.py
@@ -11,6 +11,7 @@
 VMEM = pl.BlockSpec(memory_space=pltpu.VMEM)
 SMEM = pl.BlockSpec(memory_space=pltpu.SMEM)
 ANY = pl.BlockSpec(memory_space=pl.ANY)
+HBM = pl.BlockSpec(memory_space=pltpu.HBM)
 F32, BF16, I32 = jnp.float32, jnp.bfloat16, jnp.int32
 NEAR = (0, 6, 2, 7, 1)
 FAR = (4, 5, 3)
@@ -154,13 +155,27 @@
     return copies
 
 
-def spread_kernel(f_ref, out_ref):
+def fetch(sources, targets, sems):
+    copies = [
+        pltpu.make_async_copy(source, target, sems.at[k])
+        for k, (source, target) in enumerate(zip(sources, targets))
+    ]
+    for copy in copies:
+        copy.start()
+    return copies
+
+
+def spread_kernel(f_from, out_ref, f_ref, sems):
+    for copy in fetch((f_from,), (f_ref,), sems):
+        copy.wait()
     quarter = out_ref.shape[1]
     for j in range(out_ref.shape[0]):
         out_ref[j] = f_ref[j % NN * quarter:(j % NN + 1) * quarter, :]
 
 
-def pack_kernel(nw_ref, rw_ref, f_ref, w_ref):
+def pack_kernel(nw_from, rw_from, f_from, w_ref, nw_ref, rw_ref, f_ref, sems):
+    for copy in fetch((nw_from, rw_from, f_from), (nw_ref, rw_ref, f_ref), sems):
+        copy.wait()
     side = nw_ref.shape[0]
     quarter = f_ref.shape[0] // NN
     for j in range(NN):
@@ -195,12 +210,10 @@
     add_turns(meta_ref, 0, meta_ref[0, room + 1], room // STEP, lo_ref, blocks, po_ref)
 
 
-def join_kernel(own_ref, came_ref, *out_refs):
+def join_kernel(own_ref, came_ref, out_ref):
     joined = (own_ref[...] + came_ref[...].astype(F32)).astype(BF16)
-    part = joined.shape[1] // len(out_refs)
-    for k, out_ref in enumerate(out_refs):
-        for j in range(out_ref.shape[0]):
-            out_ref[j] = joined[:, k * part:(k + 1) * part]
+    for j in range(out_ref.shape[0]):
+        out_ref[j] = joined
 
 
 def total_kernel(in_ref, out_ref):
@@ -220,7 +233,7 @@
         output_ref[j * side:(j + 1) * side, :] = in_ref[2 * NN + j].astype(F32)
 
 
-def dense_kernel(n_ref, a_ref, b_ref, w_ref, f_ref, cot_ref, ow_ref, out_ref, g_ref, agg_ref):
+def dense_kernel(n_ref, a_ref, w_ref, f_ref, cot_ref, ow_ref, out_ref, g_ref, agg_ref):
     side = f_ref.shape[1]
     quarter = w_ref.shape[1] - 2 * side
     mine = pl.ds(pl.multiple_of(n_ref[0] * side, side), side)
@@ -235,19 +248,16 @@
         ],
         axis=0,
     )
-    hidden_grad = lax.dot_general(
-        cot_ref[...], ow_ref[...], (((1,), (1,)), ((), ())), preferred_element_type=F32
-    )
-    halves = []
-    for half_ref in (a_ref, b_ref):
-        half = half_ref[0].astype(F32)
-        for j in range(1, NN):
-            half = half + half_ref[j].astype(F32)
-        halves.append(half.astype(BF16))
-    agg = jnp.concatenate(halves, axis=1)
+    agg = a_ref[0].astype(F32)
+    for j in range(1, NN):
+        agg = agg + a_ref[j].astype(F32)
+    agg = agg.astype(BF16)
     agg_ref[...] = agg
     pre = jnp.dot(agg, neighbor_weight, preferred_element_type=F32) + jnp.dot(
         rows, root_weight, preferred_element_type=F32
+    )
+    hidden_grad = lax.dot_general(
+        cot_ref[...], ow_ref[...], (((1,), (1,)), ((), ())), preferred_element_type=F32
     )
     s = jax.nn.sigmoid(pre)
     hidden = (pre * s).astype(BF16)
@@ -297,10 +307,10 @@
         spread_kernel,
         "spread",
         jax.ShapeDtypeStruct((NZ * NN, quarter, side), BF16),
-        [VMEM],
+        [HBM],
         VMEM,
-        [],
-        4,
+        [pltpu.VMEM((rows, side), BF16), pltpu.SemaphoreType.DMA((1,))],
+        56,
         10**5,
         10**6,
         features,
@@ -311,10 +321,15 @@
         pack_kernel,
         "pack",
         jax.ShapeDtypeStruct((NN, 2 * side + quarter, width), BF16),
-        [VMEM, VMEM, VMEM],
+        [HBM, HBM, HBM],
         VMEM,
-        [],
-        4,
+        [
+            pltpu.VMEM((side, width), BF16),
+            pltpu.VMEM((side, width), BF16),
+            pltpu.VMEM((rows, side), BF16),
+            pltpu.SemaphoreType.DMA((3,)),
+        ],
+        56,
         10**5,
         2 * 10**6,
         neighbor_weight,
@@ -399,9 +414,9 @@
     copies = call(
         join_kernel,
         "join",
-        (jax.ShapeDtypeStruct((NN, rows, width // 2), BF16),) * 2,
+        jax.ShapeDtypeStruct((NN, rows, width), BF16),
         [VMEM, VMEM],
-        (VMEM, VMEM),
+        VMEM,
         [],
         8,
         10**6,
@@ -409,7 +424,7 @@
         part_own,
         swap_cores(part_other),
     )
-    parts = [exchange(copy, OVER_X) for copy in copies]
+    parts = exchange(copies, OVER_X)
 
     layer_output, grads = call(
         dense_kernel,
@@ -418,14 +433,14 @@
             jax.ShapeDtypeStruct((rows, side), BF16),
             jax.ShapeDtypeStruct((3 * NN, side, side), BF16),
         ),
-        [SMEM] + [VMEM] * 6,
+        [SMEM] + [VMEM] * 5,
         (VMEM, VMEM),
         [pltpu.VMEM((rows, width), BF16)],
         16,
         12 * rows * width * width,
         5 * 10**6,
         narrow[None],
-        *parts,
+        parts,
         all_weights,
         features,
         cotangent,

time: 168 us -> 161 us (0.958)
  blocking collectives: 62 us -> 48.3 us
  Pallas kernels: 14.4 us -> 20.3 us
  waiting for transfers between devices: 25.1 us -> 30.1 us
  local copies, waits for them, and re-layouts: 3.73 us -> 0.03 us
    all_to_all x5 -> x4, blocking collectives: 62 us -> 48.3 us  [exchange(): lax.all_to_all(pieces, AXES, 0, 0, axis_index_groups=groups_, tiled=True)]
    all_to_all x3, waiting for transfers between devices: 8.43 us -> 16.7 us  [exchange(): lax.all_to_all(pieces, AXES, 0, 0, axis_index_groups=groups_, tiled=True)]
    pallas_call x11, Pallas kernels: 14.4 us -> 20.3 us  [call(): pl.pallas_call(kernel, out_shape=out_shape, in_specs=in_specs, out_specs=...]
    unnamed x20 -> x14, local copies, waits for them, and re-layouts: 3.73 us -> 0.03 us
    ppermute x7, waiting for transfers between devices: 15.5 us -> 12.3 us  [pass_on(): return lax.ppermute(value, AXES, pairs)]
  transfers between devices with their start and end apart: 13 -> 13, of which waited for: 8 -> 7; matrix products, arithmetic and copies ran while one was open for 0% -> 0% of each run, Pallas kernels for 6% -> 10%
where the time goes in v5:
time: 161 us; the launch traced here: 160 us
  starting transfers between devices  59.5 us (37%)
  blocking collectives  48.3 us (30%)
  waiting for transfers between devices  30.1 us (19%)
  Pallas kernels  20.3 us (13%)
    all_to_all x4, blocking collectives, exchange(): lax.all_to_all(pieces, AXES, 0, 0, axis_index_groups=groups_, tiled=True)  48.3 us
    ppermute x7, starting transfers between devices, pass_on(): return lax.ppermute(value, AXES, pairs)  28.5 us
    pallas_call x11, Pallas kernels, call(): pl.pallas_call(kernel, out_shape=out_shape, in_specs=in_specs, out_specs=...  20.3 us
    all_to_all x3, starting transfers between devices, exchange(): lax.all_to_all(pieces, AXES, 0, 0, axis_index_groups=groups_, tiled=True)  17.6 us
    all_to_all x3, waiting for transfers between devices, exchange(): lax.all_to_all(pieces, AXES, 0, 0, axis_index_groups=groups_, tiled=True)  16.7 us
    ppermute x3, starting transfers between devices, swap_cores(): return lax.ppermute(value, AXES, OTHER_CORE)  13.5 us
    ppermute x7, waiting for transfers between devices, pass_on(): return lax.ppermute(value, AXES, pairs)  12.3 us
  transfers between devices with their start and end apart: 13, of which 7 were waited for; matrix products, arithmetic and copies ran while one was open for 0% of the time, Pallas kernels for 10%

profile of v5, /device:TPU:1, one launch (start us, length us, event | category | flops | bytes accessed | tf_op | source)
XLA Modules:
  0.0 160.0 jit_solution(11747827375746815205)
XLA Ops:
  0.7 1.9 %spread.1 = bf16[32,64,128]{2,1,0:T(8,128)(2,1)} custom-call(bf16[256,128]{1,0:T(8,128)(2,1)} %f_ref.1), custom_call_target="tpu_custom_call" | custom-call | flops 100000 | bytes 1000000 | tf_op jit(solution)/shard_map/spread/pallas_call | solution.py:65
  2.5 10.5 %all-to-all-start = ((bf16[32,64,128]{2,1,0:T(8,128)(2,1)}), bf16[32,64,128]{2,1,0:T(8,128)(2,1)S(1)}, u32[]{:S(2)}, u32[]{:S(2)}) async-start(bf16[32,64,128]{2,1,0:T(8,128)(2,1)} %spread.1), calls=%async_computation | async-start | bytes 1048576 | tf_op jit(solution)/shard_map/all_to_all | solution.py:49
  13.1 6.1 %collective-permute-start.1 = (bf16[48,128,128]{2,1,0:T(8,128)(2,1)S(1)}, bf16[48,128,128]{2,1,0:T(8,128)(2,1)}, u32[]{:S(2)}, u32[]{:S(2)}) collective-permute-start(bf16[48,128,128]{2,1,0:T(8,128)(2,1)S(1)} %bitcast.10), channel_id=1, source_target_pairs={{0,4},{1,5},{2,6},{3,7},{4,0},{5,1},{6,2},{7,3},{8,12},{9,13},{10,... | collective-permute-start | bytes 4718600 | tf_op jit(solution)/shard_map/ppermute | solution.py:53
  19.9 1.9 %collective-permute-start = (s32[97]{0:T(128)S(1)}, s32[97]{0:T(128)S(1)}, u32[]{:S(2)}, u32[]{:S(2)}) collective-permute-start(s32[97]{0:T(128)S(1)} %pad_add_fusion.1.own_n_ref), channel_id=1, source_target_pairs={{0,4},{1,5},{2,6},{3,7},{4,0},{5,1},{6,2},{7,3},{8,12},{9,13},{10,... | collective-permute-start | bytes 1172 | tf_op jit(solution)/shard_map/ppermute | solution.py:53
  21.8 2.2 %pack.1 = bf16[4,320,512]{2,1,0:T(8,128)(2,1)} custom-call(bf16[128,512]{1,0:T(8,128)(2,1)} %nw_from.1, bf16[128,512]{1,0:T(8,128)(2,1)} %rw_from.1, bf16[256,128]{1,0:T(8,128)(2,1)} %f_ref.1), custom_call_target="tpu_custom_call" | custom-call | flops 100000 | bytes 2000000 | tf_op jit(solution)/shard_map/pack/pallas_call | solution.py:65
  24.0 1.9 %all-to-all-done.refs_0_ = bf16[32,64,128]{2,1,0:T(8,128)(2,1)S(1)} async-done(((bf16[32,64,128]{2,1,0:T(8,128)(2,1)}), bf16[32,64,128]{2,1,0:T(8,128)(2,1)S(1)}, u32[]{:S(2)}, u32[]{:S(2)}) %all-to-all-start) | async-done | bytes 524320 | tf_op jit(solution)/shard_map/all_to_all | solution.py:49
  25.9 5.7 %collective-permute-start.2 = (bf16[32,64,128]{2,1,0:T(8,128)(2,1)S(1)}, bf16[32,64,128]{2,1,0:T(8,128)(2,1)}, u32[]{:S(2)}, u32[]{:S(2)}) collective-permute-start(bf16[32,64,128]{2,1,0:T(8,128)(2,1)S(1)} %all-to-all-done.refs_0_), channel_id=1, source_target_pairs={{0,16},{1,17},{2,18},{3,19},{4,132},{5,133},{6,134},{7,135},{8,24}... | collective-permute-start | bytes 1572872 | tf_op jit(solution)/shard_map/ppermute | solution.py:61
  31.5 6.8 %collective-permute-start.3 = (bf16[32,64,128]{2,1,0:T(8,128)(2,1)S(1)}, bf16[32,64,128]{2,1,0:T(8,128)(2,1)}, u32[]{:S(2)}, u32[]{:S(2)}) collective-permute-start(bf16[32,64,128]{2,1,0:T(8,128)(2,1)S(1)} %all-to-all-done.refs_0_), channel_id=1, source_target_pairs={{0,48},{1,49},{2,50},{3,51},{4,388},{5,389},{6,390},{7,391},{8,56}... | collective-permute-start | bytes 1572872 | tf_op jit(solution)/shard_map/ppermute | solution.py:61
  38.3 3.1 %collective-permute-start.4 = (bf16[32,64,128]{2,1,0:T(8,128)(2,1)S(1)}, bf16[32,64,128]{2,1,0:T(8,128)(2,1)}, u32[]{:S(2)}, u32[]{:S(2)}) collective-permute-start(bf16[32,64,128]{2,1,0:T(8,128)(2,1)S(1)} %all-to-all-done.refs_0_), channel_id=1, source_target_pairs={{0,8},{1,9},{2,10},{3,11},{4,68},{5,69},{6,70},{7,71},{8,16},{9,17... | collective-permute-start | bytes 1572872 | tf_op jit(solution)/shard_map/ppermute | solution.py:61
  41.4 3.4 %collective-permute-start.5 = (bf16[32,64,128]{2,1,0:T(8,128)(2,1)S(1)}, bf16[32,64,128]{2,1,0:T(8,128)(2,1)}, u32[]{:S(2)}, u32[]{:S(2)}) collective-permute-start(bf16[32,64,128]{2,1,0:T(8,128)(2,1)S(1)} %all-to-all-done.refs_0_), channel_id=1, source_target_pairs={{0,56},{1,57},{2,58},{3,59},{4,452},{5,453},{6,454},{7,455},{8,0},... | collective-permute-start | bytes 1572872 | tf_op jit(solution)/shard_map/ppermute | solution.py:61
  44.8 3.6 %all-to-all-start.2 = ((bf16[4,320,512]{2,1,0:T(8,128)(2,1)}), bf16[4,320,512]{2,1,0:T(8,128)(2,1)S(1)}, u32[]{:S(2)}, u32[]{:S(2)}) async-start(bf16[4,320,512]{2,1,0:T(8,128)(2,1)} %pack.1), calls=%async_computation.2 | async-start | bytes 2621440 | tf_op jit(solution)/shard_map/all_to_all | solution.py:49
  48.4 2.2 %collective-permute-done.3.refs_2_ = bf16[32,64,128]{2,1,0:T(8,128)(2,1)} collective-permute-done((bf16[32,64,128]{2,1,0:T(8,128)(2,1)S(1)}, bf16[32,64,128]{2,1,0:T(8,128)(2,1)}, u32[]{:S(2)}, u32[]{:S(2)}) %collective-permute-start.3) | collective-permute-done | bytes 524320 | tf_op jit(solution)/shard_map/ppermute | solution.py:61
  50.5 4.1 %collective-permute-done.4.refs_3_ = bf16[32,64,128]{2,1,0:T(8,128)(2,1)} collective-permute-done((bf16[32,64,128]{2,1,0:T(8,128)(2,1)S(1)}, bf16[32,64,128]{2,1,0:T(8,128)(2,1)}, u32[]{:S(2)}, u32[]{:S(2)}) %collective-permute-start.4) | collective-permute-done | bytes 524320 | tf_op jit(solution)/shard_map/ppermute | solution.py:61
  54.6 2.2 %collective-permute-done.5.refs_4_ = bf16[32,64,128]{2,1,0:T(8,128)(2,1)} collective-permute-done((bf16[32,64,128]{2,1,0:T(8,128)(2,1)S(1)}, bf16[32,64,128]{2,1,0:T(8,128)(2,1)}, u32[]{:S(2)}, u32[]{:S(2)}) %collective-permute-start.5) | collective-permute-done | bytes 524320 | tf_op jit(solution)/shard_map/ppermute | solution.py:61
  56.9 3.0 %collective-permute-start.6 = (bf16[32,64,128]{2,1,0:T(8,128)(2,1)}, bf16[32,64,128]{2,1,0:T(8,128)(2,1)}, u32[]{:S(2)}, u32[]{:S(2)}) collective-permute-start(bf16[32,64,128]{2,1,0:T(8,128)(2,1)} %collective-permute-done.2.refs_1_), channel_id=1, source_target_pairs={{0,16},{1,17},{2,18},{3,19},{4,132},{5,133},{6,134},{7,135},{8,24}... | collective-permute-start | bytes 1572872 | tf_op jit(solution)/shard_map/ppermute | solution.py:61
  59.9 4.4 %collective-permute-start.7 = (bf16[32,64,128]{2,1,0:T(8,128)(2,1)}, bf16[32,64,128]{2,1,0:T(8,128)(2,1)}, u32[]{:S(2)}, u32[]{:S(2)}) collective-permute-start(bf16[32,64,128]{2,1,0:T(8,128)(2,1)} %collective-permute-done.2.refs_1_), channel_id=1, source_target_pairs={{0,8},{1,9},{2,10},{3,11},{4,68},{5,69},{6,70},{7,71},{8,16},{9,17... | collective-permute-start | bytes 1572872 | tf_op jit(solution)/shard_map/ppermute | solution.py:61
  64.3 2.1 %collective-permute-start.8 = (bf16[32,64,128]{2,1,0:T(8,128)(2,1)}, bf16[32,64,128]{2,1,0:T(8,128)(2,1)}, u32[]{:S(2)}, u32[]{:S(2)}) collective-permute-start(bf16[32,64,128]{2,1,0:T(8,128)(2,1)} %collective-permute-done.3.refs_2_), channel_id=1, source_target_pairs={{0,56},{1,57},{2,58},{3,59},{4,452},{5,453},{6,454},{7,455},{8,0},... | collective-permute-start | bytes 1572872 | tf_op jit(solution)/shard_map/ppermute | solution.py:61
  66.5 5.7 %place.1 = (bf16[28,256,128]{2,1,0:T(8,128)(2,1)S(1)}, bf16[28,256,128]{2,1,0:T(8,128)(2,1)S(1)}, s32[2,58]{1,0:T(2,128)S(1)}) custom-call(s32[18]{0:T(128)S(1)} %pad_add_fusion.where_ref, s32[97]{0:T(128)S(1)} %pad_add_fusion.1.own_n_ref, s32[97]{0:T(128)S(1)} %collective-permute-done.other_n_ref, bf16[48,128,128]{2,1,0:T(8,128)(2,1)S(1)} %bitcast.11, ...), custom_call_target="tpu_custom_call" | custom-call | flops 10000000 | bytes 7000000 | tf_op jit(solution)/shard_map/place/pallas_call | solution.py:65
  72.3 3.7 %near.1 = (f32[256,512]{1,0:T(8,128)S(1)}, f32[256,512]{1,0:T(8,128)S(1)}) custom-call(s32[2,58]{1,0:T(2,128)S(1)} %get-tuple-element.24.meta_ref, bf16[28,256,128]{2,1,0:T(8,128)(2,1)S(1)} %get-tuple-element.25.lo_ref, bf16[28,256,128]{2,1,0:T(8,128)(2,1)S(1)} %get-tuple-element.26.lt_ref, bf16[32,64,128]{2,1,0:T(8,128)(2,1)S(1)} %all-to-all-done.refs_0_, ...), custom_call_target="tpu_custom_call" | custom-call | flops 805306368 | bytes 8000000 | tf_op jit(solution)/shard_map/near/pallas_call | solution.py:65
  76.0 3.8 %collective-permute-done.7.refs_1_ = bf16[32,64,128]{2,1,0:T(8,128)(2,1)} collective-permute-done((bf16[32,64,128]{2,1,0:T(8,128)(2,1)}, bf16[32,64,128]{2,1,0:T(8,128)(2,1)}, u32[]{:S(2)}, u32[]{:S(2)}) %collective-permute-start.7) | collective-permute-done | bytes 524320 | tf_op jit(solution)/shard_map/ppermute | solution.py:61
  79.8 3.2 %far.1 = (f32[256,512]{1,0:T(8,128)S(1)}, bf16[256,512]{1,0:T(8,128)(2,1)S(1)}) custom-call(s32[2,58]{1,0:T(2,128)S(1)} %get-tuple-element.24.meta_ref, bf16[28,256,128]{2,1,0:T(8,128)(2,1)S(1)} %get-tuple-element.25.lo_ref, bf16[28,256,128]{2,1,0:T(8,128)(2,1)S(1)} %get-tuple-element.26.lt_ref, f32[256,512]{1,0:T(8,128)S(1)} %get-tuple-element.32.no_ref, ...), custom_call_target="tpu_custom_call" | custom-call | flops 402653184 | bytes 6000000 | tf_op jit(solution)/shard_map/far/pallas_call | solution.py:65
  83.0 5.5 %collective-permute-start.9 = (bf16[256,512]{1,0:T(8,128)(2,1)S(1)}, bf16[256,512]{1,0:T(8,128)(2,1)S(1)}, u32[]{:S(2)}, u32[]{:S(2)}) collective-permute-start(bf16[256,512]{1,0:T(8,128)(2,1)S(1)} %get-tuple-element.35), channel_id=1, source_target_pairs={{0,4},{1,5},{2,6},{3,7},{4,0},{5,1},{6,2},{7,3},{8,12},{9,13},{10,... | collective-permute-start | bytes 786440 | tf_op jit(solution)/shard_map/ppermute | solution.py:53
  88.5 1.1 collective-permute-done.9.came_ref
  89.6 1.1 join.1
  90.7 3.5 %all-to-all-start.1 = ((bf16[4,256,512]{2,1,0:T(8,128)(2,1)}), bf16[4,256,512]{2,1,0:T(8,128)(2,1)S(1)}, u32[]{:S(2)}, u32[]{:S(2)}) async-start(bf16[4,256,512]{2,1,0:T(8,128)(2,1)} %join.1), calls=%async_computation.1 | async-start | bytes 2097152 | tf_op jit(solution)/shard_map/all_to_all | solution.py:49
  94.2 14.8 %all-to-all-done.1.a_ref = bf16[4,256,512]{2,1,0:T(8,128)(2,1)S(1)} async-done(((bf16[4,256,512]{2,1,0:T(8,128)(2,1)}), bf16[4,256,512]{2,1,0:T(8,128)(2,1)S(1)}, u32[]{:S(2)}, u32[]{:S(2)}) %all-to-all-start.1) | async-done | bytes 1048608 | tf_op jit(solution)/shard_map/all_to_all | solution.py:49
  109.0 1.6 dense.1
  110.6 11.1 %all_to_all.35.in_ref = bf16[8,192,128]{2,1,0:T(8,128)(2,1)S(1)} all-to-all(bf16[8,192,128]{2,1,0:T(8,128)(2,1)S(1)} %bitcast.13), channel_id=1, replica_groups={{0,4,8,12,64,68,72,76},{1,5,9,13,65,69,73,77},{2,6,10,14,66,70,74,78},{..., dimensions={0} | all-to-all | bytes 786432 | tf_op jit(solution)/shard_map/all_to_all | solution.py:49
  121.8 12.3 %all_to_all.36.in_ref = bf16[4,192,128]{2,1,0:T(8,128)(2,1)S(1)} all-to-all(bf16[4,192,128]{2,1,0:T(8,128)(2,1)S(1)} %total.3), channel_id=1, replica_groups={{0,16,32,48},{1,17,33,49},{2,18,34,50},{3,19,35,51},{4,20,36,52},{5,21,..., dimensions={0} | all-to-all | bytes 393216 | tf_op jit(solution)/shard_map/all_to_all | solution.py:49
  134.1 10.9 %all_to_all.37.in_ref = bf16[4,192,128]{2,1,0:T(8,128)(2,1)S(1)} all-to-all(bf16[4,192,128]{2,1,0:T(8,128)(2,1)S(1)} %total.4), channel_id=1, replica_groups={{0,128,256,384},{1,129,257,385},{2,130,258,386},{3,131,259,387},{4,132,..., dimensions={0} | all-to-all | bytes 393216 | tf_op jit(solution)/shard_map/all_to_all | solution.py:49
  144.9 14.1 %all_to_all.38 = bf16[8,192,128]{2,1,0:T(8,128)(2,1)S(1)} all-to-all(bf16[8,192,128]{2,1,0:T(8,128)(2,1)S(1)} %total.5), channel_id=1, replica_groups={{0,4,8,12,64,68,72,76},{1,5,9,13,65,69,73,77},{2,6,10,14,66,70,74,78},{..., dimensions={0} | all-to-all | bytes 786432 | tf_op jit(solution)/shard_map/all_to_all | solution.py:49
  159.1 0.9 last.1
  (25 shorter events, 0.3 us)
Async XLA Ops:
  0.6 12.4 %copy-start = (bf16[1,1,48,128,128]{4,3,2,1,0:T(8,128)(2,1)S(1)}, bf16[1,1,48,128,128]{4,3,2,1,0:T(8,128)(2,1)}, u32[]{:S(2)}) copy-start(bf16[1,1,48,128,128]{4,3,2,1,0:T(8,128)(2,1)} %param.11) | copy-start | bytes 4718596
  0.6 19.1 %copy-start.5 = (s32[1,1,48]{2,1,0:T(1,128)S(1)}, s32[1,1,48]{2,1,0:T(1,128)}, u32[]{:S(2)}) copy-start(s32[1,1,48]{2,1,0:T(1,128)} %param.12) | copy-start | bytes 580
  0.7 19.1 %copy-start.4 = (s32[1,1,48]{2,1,0:T(1,128)S(1)}, s32[1,1,48]{2,1,0:T(1,128)}, u32[]{:S(2)}) copy-start(s32[1,1,48]{2,1,0:T(1,128)} %param.13) | copy-start | bytes 580
  2.5 23.3 %all-to-all-start = ((bf16[32,64,128]{2,1,0:T(8,128)(2,1)}), bf16[32,64,128]{2,1,0:T(8,128)(2,1)S(1)}, u32[]{:S(2)}, u32[]{:S(2)}) async-start(bf16[32,64,128]{2,1,0:T(8,128)(2,1)} %spread.1), calls=%async_computation | async-start | bytes 1048576 | tf_op jit(solution)/shard_map/all_to_all | solution.py:49
  13.1 53.5 %collective-permute-start.1 = (bf16[48,128,128]{2,1,0:T(8,128)(2,1)S(1)}, bf16[48,128,128]{2,1,0:T(8,128)(2,1)}, u32[]{:S(2)}, u32[]{:S(2)}) collective-permute-start(bf16[48,128,128]{2,1,0:T(8,128)(2,1)S(1)} %bitcast.10), channel_id=1, source_target_pairs={{0,4},{1,5},{2,6},{3,7},{4,0},{5,1},{6,2},{7,3},{8,12},{9,13},{10,... | collective-permute-start | bytes 4718600 | tf_op jit(solution)/shard_map/ppermute | solution.py:53
  19.9 4.1 %collective-permute-start = (s32[97]{0:T(128)S(1)}, s32[97]{0:T(128)S(1)}, u32[]{:S(2)}, u32[]{:S(2)}) collective-permute-start(s32[97]{0:T(128)S(1)} %pad_add_fusion.1.own_n_ref), channel_id=1, source_target_pairs={{0,4},{1,5},{2,6},{3,7},{4,0},{5,1},{6,2},{7,3},{8,12},{9,13},{10,... | collective-permute-start | bytes 1172 | tf_op jit(solution)/shard_map/ppermute | solution.py:53
  24.0 42.5 %copy-start.6 = (s32[16]{0:T(128)S(1)}, s32[16]{0:T(128)}, u32[]{:S(2)}) copy-start(s32[16]{0:T(128)} %constant.57.clone) | copy-start | bytes 196
  25.9 22.5 %collective-permute-start.2 = (bf16[32,64,128]{2,1,0:T(8,128)(2,1)S(1)}, bf16[32,64,128]{2,1,0:T(8,128)(2,1)}, u32[]{:S(2)}, u32[]{:S(2)}) collective-permute-start(bf16[32,64,128]{2,1,0:T(8,128)(2,1)S(1)} %all-to-all-done.refs_0_), channel_id=1, source_target_pairs={{0,16},{1,17},{2,18},{3,19},{4,132},{5,133},{6,134},{7,135},{8,24}... | collective-permute-start | bytes 1572872 | tf_op jit(solution)/shard_map/ppermute | solution.py:61
  31.5 19.0 %collective-permute-start.3 = (bf16[32,64,128]{2,1,0:T(8,128)(2,1)S(1)}, bf16[32,64,128]{2,1,0:T(8,128)(2,1)}, u32[]{:S(2)}, u32[]{:S(2)}) collective-permute-start(bf16[32,64,128]{2,1,0:T(8,128)(2,1)S(1)} %all-to-all-done.refs_0_), channel_id=1, source_target_pairs={{0,48},{1,49},{2,50},{3,51},{4,388},{5,389},{6,390},{7,391},{8,56}... | collective-permute-start | bytes 1572872 | tf_op jit(solution)/shard_map/ppermute | solution.py:61
  38.3 16.3 %collective-permute-start.4 = (bf16[32,64,128]{2,1,0:T(8,128)(2,1)S(1)}, bf16[32,64,128]{2,1,0:T(8,128)(2,1)}, u32[]{:S(2)}, u32[]{:S(2)}) collective-permute-start(bf16[32,64,128]{2,1,0:T(8,128)(2,1)S(1)} %all-to-all-done.refs_0_), channel_id=1, source_target_pairs={{0,8},{1,9},{2,10},{3,11},{4,68},{5,69},{6,70},{7,71},{8,16},{9,17... | collective-permute-start | bytes 1572872 | tf_op jit(solution)/shard_map/ppermute | solution.py:61
  41.4 15.4 %collective-permute-start.5 = (bf16[32,64,128]{2,1,0:T(8,128)(2,1)S(1)}, bf16[32,64,128]{2,1,0:T(8,128)(2,1)}, u32[]{:S(2)}, u32[]{:S(2)}) collective-permute-start(bf16[32,64,128]{2,1,0:T(8,128)(2,1)S(1)} %all-to-all-done.refs_0_), channel_id=1, source_target_pairs={{0,56},{1,57},{2,58},{3,59},{4,452},{5,453},{6,454},{7,455},{8,0},... | collective-permute-start | bytes 1572872 | tf_op jit(solution)/shard_map/ppermute | solution.py:61
  44.8 45.9 %all-to-all-start.2 = ((bf16[4,320,512]{2,1,0:T(8,128)(2,1)}), bf16[4,320,512]{2,1,0:T(8,128)(2,1)S(1)}, u32[]{:S(2)}, u32[]{:S(2)}) async-start(bf16[4,320,512]{2,1,0:T(8,128)(2,1)} %pack.1), calls=%async_computation.2 | async-start | bytes 2621440 | tf_op jit(solution)/shard_map/all_to_all | solution.py:49
  56.9 19.1 %collective-permute-start.6 = (bf16[32,64,128]{2,1,0:T(8,128)(2,1)}, bf16[32,64,128]{2,1,0:T(8,128)(2,1)}, u32[]{:S(2)}, u32[]{:S(2)}) collective-permute-start(bf16[32,64,128]{2,1,0:T(8,128)(2,1)} %collective-permute-done.2.refs_1_), channel_id=1, source_target_pairs={{0,16},{1,17},{2,18},{3,19},{4,132},{5,133},{6,134},{7,135},{8,24}... | collective-permute-start | bytes 1572872 | tf_op jit(solution)/shard_map/ppermute | solution.py:61
  59.9 19.9 %collective-permute-start.7 = (bf16[32,64,128]{2,1,0:T(8,128)(2,1)}, bf16[32,64,128]{2,1,0:T(8,128)(2,1)}, u32[]{:S(2)}, u32[]{:S(2)}) collective-permute-start(bf16[32,64,128]{2,1,0:T(8,128)(2,1)} %collective-permute-done.2.refs_1_), channel_id=1, source_target_pairs={{0,8},{1,9},{2,10},{3,11},{4,68},{5,69},{6,70},{7,71},{8,16},{9,17... | collective-permute-start | bytes 1572872 | tf_op jit(solution)/shard_map/ppermute | solution.py:61
  64.3 15.5 %collective-permute-start.8 = (bf16[32,64,128]{2,1,0:T(8,128)(2,1)}, bf16[32,64,128]{2,1,0:T(8,128)(2,1)}, u32[]{:S(2)}, u32[]{:S(2)}) collective-permute-start(bf16[32,64,128]{2,1,0:T(8,128)(2,1)} %collective-permute-done.3.refs_2_), channel_id=1, source_target_pairs={{0,56},{1,57},{2,58},{3,59},{4,452},{5,453},{6,454},{7,455},{8,0},... | collective-permute-start | bytes 1572872 | tf_op jit(solution)/shard_map/ppermute | solution.py:61
  83.0 6.6 %collective-permute-start.9 = (bf16[256,512]{1,0:T(8,128)(2,1)S(1)}, bf16[256,512]{1,0:T(8,128)(2,1)S(1)}, u32[]{:S(2)}, u32[]{:S(2)}) collective-permute-start(bf16[256,512]{1,0:T(8,128)(2,1)S(1)} %get-tuple-element.35), channel_id=1, source_target_pairs={{0,4},{1,5},{2,6},{3,7},{4,0},{5,1},{6,2},{7,3},{8,12},{9,13},{10,... | collective-permute-start | bytes 786440 | tf_op jit(solution)/shard_map/ppermute | solution.py:53
  89.6 19.4 %copy-start.1 = (bf16[256,128]{1,0:T(8,128)(2,1)S(1)}, bf16[256,128]{1,0:T(8,128)(2,1)}, u32[]{:S(2)}) copy-start(bf16[256,128]{1,0:T(8,128)(2,1)} %f_ref.1) | copy-start | bytes 196612
  89.6 19.4 %copy-start.2 = (bf16[512,512]{1,0:T(8,128)(2,1)S(1)}, bf16[512,512]{1,0:T(8,128)(2,1)}, u32[]{:S(2)}) copy-start(bf16[512,512]{1,0:T(8,128)(2,1)} %ow_ref.1) | copy-start | bytes 1572868
  89.6 19.4 %copy-start.3 = (bf16[256,512]{1,0:T(8,128)(2,1)S(1)}, bf16[256,512]{1,0:T(8,128)(2,1)}, u32[]{:S(2)}) copy-start(bf16[256,512]{1,0:T(8,128)(2,1)} %cot_ref.1) | copy-start | bytes 786436
  90.7 18.3 %all-to-all-start.1 = ((bf16[4,256,512]{2,1,0:T(8,128)(2,1)}), bf16[4,256,512]{2,1,0:T(8,128)(2,1)S(1)}, u32[]{:S(2)}, u32[]{:S(2)}) async-start(bf16[4,256,512]{2,1,0:T(8,128)(2,1)} %join.1), calls=%async_computation.1 | async-start | bytes 2097152 | tf_op jit(solution)/shard_map/all_to_all | solution.py:49

commit v6 on v5

--- a/solution.py
+++ b/solution.py
@@ -53,9 +53,10 @@
     return lax.ppermute(value, AXES, OTHER_CORE)
 
 
-def pass_on(value, hops):
+def pass_on(value, even_hops, odd_hops):
     pairs = []
     for z, y, c, n in places():
+        hops = odd_hops if (z if c else y) % 2 else even_hops
         to = (z, (y + hops) % NY, c, n) if c == 0 else ((z + hops) % NZ, y, c, n)
         pairs.append((device(z, y, c, n), device(*to)))
     return lax.ppermute(value, AXES, pairs)
@@ -340,12 +341,13 @@
     all_weights = exchange(weights, OVER_X)
     by_distance = {0: line}
     for hops in (2, -2, 1, -1):
-        by_distance[-hops % NY] = pass_on(line, hops)
-    arrived = lax.optimization_barrier([by_distance[d] for d in NEAR[1:]])
+        by_distance[-hops % NY] = pass_on(line, hops, hops)
+    across = jnp.where(here % 2 == 0, by_distance[2], by_distance[6])
+    arrived, across = lax.optimization_barrier(([by_distance[d] for d in NEAR[1:]], across))
     by_distance.update(zip(NEAR[1:], arrived))
     for hops in (1, -1):
-        by_distance[-3 * hops % NY] = pass_on(by_distance[-2 * hops % NY], hops)
-    by_distance[4] = pass_on(by_distance[6], 2)
+        by_distance[-3 * hops % NY] = pass_on(by_distance[-2 * hops % NY], hops, hops)
+    by_distance[4] = pass_on(across, -2, 2)
     turns = (slots + 2 * STEP - 2) // STEP
     placed = jax.ShapeDtypeStruct((turns * STEP // 2, rows, side), BF16)
     left_own, left_other, meta = call(

time: 161 us -> 158 us (0.981)
  waiting for transfers between devices: 30.1 us -> 25.9 us
  Pallas kernels: 20.3 us -> 17.4 us
  starting transfers between devices: 59.5 us -> 61.8 us
    ppermute x7, waiting for transfers between devices: 12.3 us -> 8.34 us  [pass_on(): return lax.ppermute(value, AXES, pairs)]
    pallas_call x11, Pallas kernels: 20.3 us -> 17.4 us  [call(): pl.pallas_call(kernel, out_shape=out_shape, in_specs=in_specs, out_specs=...]
    ppermute x7, starting transfers between devices: 28.5 us -> 30.5 us  [pass_on(): return lax.ppermute(value, AXES, pairs)]
  transfers between devices with their start and end apart: 13 -> 13, of which waited for: 7 -> 6; matrix products, arithmetic and copies ran while one was open for 0% -> 0% of each run, Pallas kernels for 10% -> 8%
where the time goes in v6:
time: 158 us; the launch traced here: 157 us
  starting transfers between devices  61.8 us (39%)
  blocking collectives  49.8 us (32%)
  waiting for transfers between devices  25.9 us (16%)
  Pallas kernels  17.4 us (11%)
  between operations  1.59 us (1%)
    all_to_all x4, blocking collectives, exchange(): lax.all_to_all(pieces, AXES, 0, 0, axis_index_groups=groups_, tiled=True)  49.8 us
    ppermute x7, starting transfers between devices, pass_on(): return lax.ppermute(value, AXES, pairs)  30.5 us
    all_to_all x3, starting transfers between devices, exchange(): lax.all_to_all(pieces, AXES, 0, 0, axis_index_groups=groups_, tiled=True)  18.6 us
    pallas_call x11, Pallas kernels, call(): pl.pallas_call(kernel, out_shape=out_shape, in_specs=in_specs, out_specs=...  17.4 us
    all_to_all x3, waiting for transfers between devices, exchange(): lax.all_to_all(pieces, AXES, 0, 0, axis_index_groups=groups_, tiled=True)  16.4 us
    ppermute x3, starting transfers between devices, swap_cores(): return lax.ppermute(value, AXES, OTHER_CORE)  12.7 us
    ppermute x7, waiting for transfers between devices, pass_on(): return lax.ppermute(value, AXES, pairs)  8.34 us
  transfers between devices with their start and end apart: 13, of which 6 were waited for; matrix products, arithmetic and copies ran while one was open for 0% of the time, Pallas kernels for 8%

profile of v6, /device:TPU:1, one launch (start us, length us, event | category | flops | bytes accessed | tf_op | source)
XLA Modules:
  0.0 156.7 jit_solution(9870302818551484543)
XLA Ops:
  0.7 1.7 %spread.1 = bf16[32,64,128]{2,1,0:T(8,128)(2,1)} custom-call(bf16[256,128]{1,0:T(8,128)(2,1)} %f_ref.1), custom_call_target="tpu_custom_call" | custom-call | flops 100000 | bytes 1000000 | tf_op jit(solution)/shard_map/spread/pallas_call | solution.py:66
  2.4 10.5 %all-to-all-start = ((bf16[32,64,128]{2,1,0:T(8,128)(2,1)}), bf16[32,64,128]{2,1,0:T(8,128)(2,1)S(1)}, u32[]{:S(2)}, u32[]{:S(2)}) async-start(bf16[32,64,128]{2,1,0:T(8,128)(2,1)} %spread.1), calls=%async_computation | async-start | bytes 1048576 | tf_op jit(solution)/shard_map/all_to_all | solution.py:49
  12.9 6.1 %collective-permute-start.1 = (bf16[48,128,128]{2,1,0:T(8,128)(2,1)}, bf16[48,128,128]{2,1,0:T(8,128)(2,1)}, u32[]{:S(2)}, u32[]{:S(2)}) collective-permute-start(bf16[48,128,128]{2,1,0:T(8,128)(2,1)} %bitcast.6.own_ref), channel_id=1, source_target_pairs={{0,4},{1,5},{2,6},{3,7},{4,0},{5,1},{6,2},{7,3},{8,12},{9,13},{10,... | collective-permute-start | bytes 4718600 | tf_op jit(solution)/shard_map/ppermute | solution.py:53
  19.7 0.1 pad_add_fusion.1.own_n_ref
  19.7 1.9 %collective-permute-start = (s32[97]{0:T(128)S(1)}, s32[97]{0:T(128)S(1)}, u32[]{:S(2)}, u32[]{:S(2)}) collective-permute-start(s32[97]{0:T(128)S(1)} %pad_add_fusion.1.own_n_ref), channel_id=1, source_target_pairs={{0,4},{1,5},{2,6},{3,7},{4,0},{5,1},{6,2},{7,3},{8,12},{9,13},{10,... | collective-permute-start | bytes 1172 | tf_op jit(solution)/shard_map/ppermute | solution.py:53
  21.7 2.2 %pack.1 = bf16[4,320,512]{2,1,0:T(8,128)(2,1)} custom-call(bf16[128,512]{1,0:T(8,128)(2,1)} %nw_from.1, bf16[128,512]{1,0:T(8,128)(2,1)} %rw_from.1, bf16[256,128]{1,0:T(8,128)(2,1)} %f_ref.1), custom_call_target="tpu_custom_call" | custom-call | flops 100000 | bytes 2000000 | tf_op jit(solution)/shard_map/pack/pallas_call | solution.py:66
  23.9 1.9 %all-to-all-done.refs_0_ = bf16[32,64,128]{2,1,0:T(8,128)(2,1)S(1)} async-done(((bf16[32,64,128]{2,1,0:T(8,128)(2,1)}), bf16[32,64,128]{2,1,0:T(8,128)(2,1)S(1)}, u32[]{:S(2)}, u32[]{:S(2)}) %all-to-all-start) | async-done | bytes 524320 | tf_op jit(solution)/shard_map/all_to_all | solution.py:49
  25.7 5.7 %collective-permute-start.2 = (bf16[32,64,128]{2,1,0:T(8,128)(2,1)S(1)}, bf16[32,64,128]{2,1,0:T(8,128)(2,1)S(1)}, u32[]{:S(2)}, u32[]{:S(2)}) collective-permute-start(bf16[32,64,128]{2,1,0:T(8,128)(2,1)S(1)} %all-to-all-done.refs_0_), channel_id=1, source_target_pairs={{0,16},{1,17},{2,18},{3,19},{4,132},{5,133},{6,134},{7,135},{8,24}... | collective-permute-start | bytes 1572872 | tf_op jit(solution)/shard_map/ppermute | solution.py:62
  31.4 6.8 %collective-permute-start.3 = (bf16[32,64,128]{2,1,0:T(8,128)(2,1)S(1)}, bf16[32,64,128]{2,1,0:T(8,128)(2,1)S(1)}, u32[]{:S(2)}, u32[]{:S(2)}) collective-permute-start(bf16[32,64,128]{2,1,0:T(8,128)(2,1)S(1)} %all-to-all-done.refs_0_), channel_id=1, source_target_pairs={{0,48},{1,49},{2,50},{3,51},{4,388},{5,389},{6,390},{7,391},{8,56}... | collective-permute-start | bytes 1572872 | tf_op jit(solution)/shard_map/ppermute | solution.py:62
  38.2 3.1 %collective-permute-start.4 = (bf16[32,64,128]{2,1,0:T(8,128)(2,1)S(1)}, bf16[32,64,128]{2,1,0:T(8,128)(2,1)S(1)}, u32[]{:S(2)}, u32[]{:S(2)}) collective-permute-start(bf16[32,64,128]{2,1,0:T(8,128)(2,1)S(1)} %all-to-all-done.refs_0_), channel_id=1, source_target_pairs={{0,8},{1,9},{2,10},{3,11},{4,68},{5,69},{6,70},{7,71},{8,16},{9,17... | collective-permute-start | bytes 1572872 | tf_op jit(solution)/shard_map/ppermute | solution.py:62
  41.3 3.4 %collective-permute-start.5 = (bf16[32,64,128]{2,1,0:T(8,128)(2,1)S(1)}, bf16[32,64,128]{2,1,0:T(8,128)(2,1)}, u32[]{:S(2)}, u32[]{:S(2)}) collective-permute-start(bf16[32,64,128]{2,1,0:T(8,128)(2,1)S(1)} %all-to-all-done.refs_0_), channel_id=1, source_target_pairs={{0,56},{1,57},{2,58},{3,59},{4,452},{5,453},{6,454},{7,455},{8,0},... | collective-permute-start | bytes 1572872 | tf_op jit(solution)/shard_map/ppermute | solution.py:62
  44.8 3.6 %all-to-all-start.2 = ((bf16[4,320,512]{2,1,0:T(8,128)(2,1)}), bf16[4,320,512]{2,1,0:T(8,128)(2,1)S(1)}, u32[]{:S(2)}, u32[]{:S(2)}) async-start(bf16[4,320,512]{2,1,0:T(8,128)(2,1)} %pack.1), calls=%async_computation.2 | async-start | bytes 2621440 | tf_op jit(solution)/shard_map/all_to_all | solution.py:49
  48.3 2.0 %collective-permute-done.3.refs_2_ = bf16[32,64,128]{2,1,0:T(8,128)(2,1)S(1)} collective-permute-done((bf16[32,64,128]{2,1,0:T(8,128)(2,1)S(1)}, bf16[32,64,128]{2,1,0:T(8,128)(2,1)S(1)}, u32[]{:S(2)}, u32[]{:S(2)}) %collective-permute-start.3) | collective-permute-done | bytes 524320 | tf_op jit(solution)/shard_map/ppermute | solution.py:62
  50.4 4.0 %collective-permute-done.4.refs_3_ = bf16[32,64,128]{2,1,0:T(8,128)(2,1)S(1)} collective-permute-done((bf16[32,64,128]{2,1,0:T(8,128)(2,1)S(1)}, bf16[32,64,128]{2,1,0:T(8,128)(2,1)S(1)}, u32[]{:S(2)}, u32[]{:S(2)}) %collective-permute-start.4) | collective-permute-done | bytes 524320 | tf_op jit(solution)/shard_map/ppermute | solution.py:62
  54.4 2.3 %collective-permute-done.5.refs_4_ = bf16[32,64,128]{2,1,0:T(8,128)(2,1)} collective-permute-done((bf16[32,64,128]{2,1,0:T(8,128)(2,1)S(1)}, bf16[32,64,128]{2,1,0:T(8,128)(2,1)}, u32[]{:S(2)}, u32[]{:S(2)}) %collective-permute-start.5) | collective-permute-done | bytes 524320 | tf_op jit(solution)/shard_map/ppermute | solution.py:62
  56.7 5.1 %collective-permute-start.6 = (bf16[32,64,128]{2,1,0:T(8,128)(2,1)S(1)}, bf16[32,64,128]{2,1,0:T(8,128)(2,1)S(1)}, u32[]{:S(2)}, u32[]{:S(2)}) collective-permute-start(bf16[32,64,128]{2,1,0:T(8,128)(2,1)S(1)} %broadcast_select_fusion), channel_id=1, source_target_pairs={{0,48},{1,49},{2,50},{3,51},{4,388},{5,389},{6,390},{7,391},{8,24}... | collective-permute-start | bytes 1572872 | tf_op jit(solution)/shard_map/ppermute | solution.py:62
  61.8 2.4 %collective-permute-start.7 = (bf16[32,64,128]{2,1,0:T(8,128)(2,1)S(1)}, bf16[32,64,128]{2,1,0:T(8,128)(2,1)S(1)}, u32[]{:S(2)}, u32[]{:S(2)}) collective-permute-start(bf16[32,64,128]{2,1,0:T(8,128)(2,1)S(1)} %collective-permute-done.2.refs_1_), channel_id=1, source_target_pairs={{0,8},{1,9},{2,10},{3,11},{4,68},{5,69},{6,70},{7,71},{8,16},{9,17... | collective-permute-start | bytes 1572872 | tf_op jit(solution)/shard_map/ppermute | solution.py:62
  64.2 4.1 %collective-permute-start.8 = (bf16[32,64,128]{2,1,0:T(8,128)(2,1)S(1)}, bf16[32,64,128]{2,1,0:T(8,128)(2,1)S(1)}, u32[]{:S(2)}, u32[]{:S(2)}) collective-permute-start(bf16[32,64,128]{2,1,0:T(8,128)(2,1)S(1)} %collective-permute-done.3.refs_2_), channel_id=1, source_target_pairs={{0,56},{1,57},{2,58},{3,59},{4,452},{5,453},{6,454},{7,455},{8,0},... | collective-permute-start | bytes 1572872 | tf_op jit(solution)/shard_map/ppermute | solution.py:62
  68.4 5.4 %place.1 = (bf16[28,256,128]{2,1,0:T(8,128)(2,1)S(1)}, bf16[28,256,128]{2,1,0:T(8,128)(2,1)S(1)}, s32[2,58]{1,0:T(2,128)S(1)}) custom-call(s32[18]{0:T(128)S(1)} %pad_add_fusion.where_ref, s32[97]{0:T(128)S(1)} %pad_add_fusion.1.own_n_ref, s32[97]{0:T(128)S(1)} %collective-permute-done.other_n_ref, bf16[48,128,128]{2,1,0:T(8,128)(2,1)} %bitcast.6.own_ref, ...), custom_call_target="tpu_custom_call" | custom-call | flops 10000000 | bytes 7000000 | tf_op jit(solution)/shard_map/place/pallas_call | solution.py:66
  73.8 2.7 %near.1 = (f32[256,512]{1,0:T(8,128)S(1)}, f32[256,512]{1,0:T(8,128)S(1)}) custom-call(s32[2,58]{1,0:T(2,128)S(1)} %get-tuple-element.25.meta_ref, bf16[28,256,128]{2,1,0:T(8,128)(2,1)S(1)} %get-tuple-element.26.lo_ref, bf16[28,256,128]{2,1,0:T(8,128)(2,1)S(1)} %get-tuple-element.27.lt_ref, bf16[32,64,128]{2,1,0:T(8,128)(2,1)S(1)} %all-to-all-done.refs_0_, ...), custom_call_target="tpu_custom_call" | custom-call | flops 805306368 | bytes 8000000 | tf_op jit(solution)/shard_map/near/pallas_call | solution.py:66
  76.5 1.7 %far.1 = (f32[256,512]{1,0:T(8,128)S(1)}, bf16[256,512]{1,0:T(8,128)(2,1)S(1)}) custom-call(s32[2,58]{1,0:T(2,128)S(1)} %get-tuple-element.25.meta_ref, bf16[28,256,128]{2,1,0:T(8,128)(2,1)S(1)} %get-tuple-element.26.lo_ref, bf16[28,256,128]{2,1,0:T(8,128)(2,1)S(1)} %get-tuple-element.27.lt_ref, f32[256,512]{1,0:T(8,128)S(1)} %get-tuple-element.33.no_ref, ...), custom_call_target="tpu_custom_call" | custom-call | flops 402653184 | bytes 6000000 | tf_op jit(solution)/shard_map/far/pallas_call | solution.py:66
  78.2 4.7 %collective-permute-start.9 = (bf16[256,512]{1,0:T(8,128)(2,1)S(1)}, bf16[256,512]{1,0:T(8,128)(2,1)S(1)}, u32[]{:S(2)}, u32[]{:S(2)}) collective-permute-start(bf16[256,512]{1,0:T(8,128)(2,1)S(1)} %get-tuple-element.37), channel_id=1, source_target_pairs={{0,4},{1,5},{2,6},{3,7},{4,0},{5,1},{6,2},{7,3},{8,12},{9,13},{10,... | collective-permute-start | bytes 786440 | tf_op jit(solution)/shard_map/ppermute | solution.py:53
  82.9 1.1 collective-permute-done.9.came_ref
  84.1 1.1 join.1
  85.2 4.5 %all-to-all-start.1 = ((bf16[4,256,512]{2,1,0:T(8,128)(2,1)}), bf16[4,256,512]{2,1,0:T(8,128)(2,1)S(1)}, u32[]{:S(2)}, u32[]{:S(2)}) async-start(bf16[4,256,512]{2,1,0:T(8,128)(2,1)} %join.1), calls=%async_computation.1 | async-start | bytes 2097152 | tf_op jit(solution)/shard_map/all_to_all | solution.py:49
  89.7 14.5 %all-to-all-done.1.a_ref = bf16[4,256,512]{2,1,0:T(8,128)(2,1)S(1)} async-done(((bf16[4,256,512]{2,1,0:T(8,128)(2,1)}), bf16[4,256,512]{2,1,0:T(8,128)(2,1)S(1)}, u32[]{:S(2)}, u32[]{:S(2)}) %all-to-all-start.1) | async-done | bytes 1048608 | tf_op jit(solution)/shard_map/all_to_all | solution.py:49
  104.2 1.6 %dense.1 = (bf16[256,128]{1,0:T(8,128)(2,1)}, bf16[12,128,128]{2,1,0:T(8,128)(2,1)S(1)}) custom-call(s32[1]{0:T(128)} %bitcast.n_ref, bf16[4,256,512]{2,1,0:T(8,128)(2,1)S(1)} %all-to-all-done.1.a_ref, bf16[4,320,512]{2,1,0:T(8,128)(2,1)S(1)} %all-to-all-done.2.w_ref, bf16[256,128]{1,0:T(8,128)(2,1)S(1)} %copy-done, bf16[256,512]{1,0:T(8,128)(2,1)S(1)} %copy-done.2, ...), custom_call_target="tpu_custom_call" | custom-call | flops 805306368 | bytes 5000000 | tf_op jit(solution)/shard_map/dense/pallas_call | solution.py:66
  105.8 14.1 %all_to_all.35.in_ref = bf16[8,192,128]{2,1,0:T(8,128)(2,1)S(1)} all-to-all(bf16[8,192,128]{2,1,0:T(8,128)(2,1)S(1)} %bitcast.11), channel_id=1, replica_groups={{0,4,8,12,64,68,72,76},{1,5,9,13,65,69,73,77},{2,6,10,14,66,70,74,78},{..., dimensions={0} | all-to-all | bytes 786432 | tf_op jit(solution)/shard_map/all_to_all | solution.py:49
  119.9 10.7 %all_to_all.36.in_ref = bf16[4,192,128]{2,1,0:T(8,128)(2,1)S(1)} all-to-all(bf16[4,192,128]{2,1,0:T(8,128)(2,1)S(1)} %total.3), channel_id=1, replica_groups={{0,16,32,48},{1,17,33,49},{2,18,34,50},{3,19,35,51},{4,20,36,52},{5,21,..., dimensions={0} | all-to-all | bytes 393216 | tf_op jit(solution)/shard_map/all_to_all | solution.py:49
  130.7 10.9 %all_to_all.37.in_ref = bf16[4,192,128]{2,1,0:T(8,128)(2,1)S(1)} all-to-all(bf16[4,192,128]{2,1,0:T(8,128)(2,1)S(1)} %total.4), channel_id=1, replica_groups={{0,128,256,384},{1,129,257,385},{2,130,258,386},{3,131,259,387},{4,132,..., dimensions={0} | all-to-all | bytes 393216 | tf_op jit(solution)/shard_map/all_to_all | solution.py:49
  141.6 14.1 %all_to_all.38 = bf16[8,192,128]{2,1,0:T(8,128)(2,1)S(1)} all-to-all(bf16[8,192,128]{2,1,0:T(8,128)(2,1)S(1)} %total.5), channel_id=1, replica_groups={{0,4,8,12,64,68,72,76},{1,5,9,13,65,69,73,77},{2,6,10,14,66,70,74,78},{..., dimensions={0} | all-to-all | bytes 786432 | tf_op jit(solution)/shard_map/all_to_all | solution.py:49
  155.8 0.9 last.1
  (24 shorter events, 0.3 us)
Async XLA Ops:
  0.6 19.0 %copy-start.3 = (s32[1,1,48]{2,1,0:T(1,128)S(1)}, s32[1,1,48]{2,1,0:T(1,128)}, u32[]{:S(2)}) copy-start(s32[1,1,48]{2,1,0:T(1,128)} %param.13) | copy-start | bytes 580
  0.6 19.0 %copy-start.4 = (s32[1,1,48]{2,1,0:T(1,128)S(1)}, s32[1,1,48]{2,1,0:T(1,128)}, u32[]{:S(2)}) copy-start(s32[1,1,48]{2,1,0:T(1,128)} %param.12) | copy-start | bytes 580
  2.4 23.3 %all-to-all-start = ((bf16[32,64,128]{2,1,0:T(8,128)(2,1)}), bf16[32,64,128]{2,1,0:T(8,128)(2,1)S(1)}, u32[]{:S(2)}, u32[]{:S(2)}) async-start(bf16[32,64,128]{2,1,0:T(8,128)(2,1)} %spread.1), calls=%async_computation | async-start | bytes 1048576 | tf_op jit(solution)/shard_map/all_to_all | solution.py:49
  12.9 55.5 %collective-permute-start.1 = (bf16[48,128,128]{2,1,0:T(8,128)(2,1)}, bf16[48,128,128]{2,1,0:T(8,128)(2,1)}, u32[]{:S(2)}, u32[]{:S(2)}) collective-permute-start(bf16[48,128,128]{2,1,0:T(8,128)(2,1)} %bitcast.6.own_ref), channel_id=1, source_target_pairs={{0,4},{1,5},{2,6},{3,7},{4,0},{5,1},{6,2},{7,3},{8,12},{9,13},{10,... | collective-permute-start | bytes 4718600 | tf_op jit(solution)/shard_map/ppermute | solution.py:53
  19.7 4.1 %collective-permute-start = (s32[97]{0:T(128)S(1)}, s32[97]{0:T(128)S(1)}, u32[]{:S(2)}, u32[]{:S(2)}) collective-permute-start(s32[97]{0:T(128)S(1)} %pad_add_fusion.1.own_n_ref), channel_id=1, source_target_pairs={{0,4},{1,5},{2,6},{3,7},{4,0},{5,1},{6,2},{7,3},{8,12},{9,13},{10,... | collective-permute-start | bytes 1172 | tf_op jit(solution)/shard_map/ppermute | solution.py:53
  25.7 22.6 %collective-permute-start.2 = (bf16[32,64,128]{2,1,0:T(8,128)(2,1)S(1)}, bf16[32,64,128]{2,1,0:T(8,128)(2,1)S(1)}, u32[]{:S(2)}, u32[]{:S(2)}) collective-permute-start(bf16[32,64,128]{2,1,0:T(8,128)(2,1)S(1)} %all-to-all-done.refs_0_), channel_id=1, source_target_pairs={{0,16},{1,17},{2,18},{3,19},{4,132},{5,133},{6,134},{7,135},{8,24}... | collective-permute-start | bytes 1572872 | tf_op jit(solution)/shard_map/ppermute | solution.py:62
  31.4 18.9 %collective-permute-start.3 = (bf16[32,64,128]{2,1,0:T(8,128)(2,1)S(1)}, bf16[32,64,128]{2,1,0:T(8,128)(2,1)S(1)}, u32[]{:S(2)}, u32[]{:S(2)}) collective-permute-start(bf16[32,64,128]{2,1,0:T(8,128)(2,1)S(1)} %all-to-all-done.refs_0_), channel_id=1, source_target_pairs={{0,48},{1,49},{2,50},{3,51},{4,388},{5,389},{6,390},{7,391},{8,56}... | collective-permute-start | bytes 1572872 | tf_op jit(solution)/shard_map/ppermute | solution.py:62
  38.2 16.2 %collective-permute-start.4 = (bf16[32,64,128]{2,1,0:T(8,128)(2,1)S(1)}, bf16[32,64,128]{2,1,0:T(8,128)(2,1)S(1)}, u32[]{:S(2)}, u32[]{:S(2)}) collective-permute-start(bf16[32,64,128]{2,1,0:T(8,128)(2,1)S(1)} %all-to-all-done.refs_0_), channel_id=1, source_target_pairs={{0,8},{1,9},{2,10},{3,11},{4,68},{5,69},{6,70},{7,71},{8,16},{9,17... | collective-permute-start | bytes 1572872 | tf_op jit(solution)/shard_map/ppermute | solution.py:62
  41.3 15.4 %collective-permute-start.5 = (bf16[32,64,128]{2,1,0:T(8,128)(2,1)S(1)}, bf16[32,64,128]{2,1,0:T(8,128)(2,1)}, u32[]{:S(2)}, u32[]{:S(2)}) collective-permute-start(bf16[32,64,128]{2,1,0:T(8,128)(2,1)S(1)} %all-to-all-done.refs_0_), channel_id=1, source_target_pairs={{0,56},{1,57},{2,58},{3,59},{4,452},{5,453},{6,454},{7,455},{8,0},... | collective-permute-start | bytes 1572872 | tf_op jit(solution)/shard_map/ppermute | solution.py:62
  44.8 23.5 %copy-start.5 = (s32[16]{0:T(128)S(1)}, s32[16]{0:T(128)}, u32[]{:S(2)}) copy-start(s32[16]{0:T(128)} %constant.61.clone) | copy-start | bytes 196
  44.8 40.4 %all-to-all-start.2 = ((bf16[4,320,512]{2,1,0:T(8,128)(2,1)}), bf16[4,320,512]{2,1,0:T(8,128)(2,1)S(1)}, u32[]{:S(2)}, u32[]{:S(2)}) async-start(bf16[4,320,512]{2,1,0:T(8,128)(2,1)} %pack.1), calls=%async_computation.2 | async-start | bytes 2621440 | tf_op jit(solution)/shard_map/all_to_all | solution.py:49
  56.7 19.7 %collective-permute-start.6 = (bf16[32,64,128]{2,1,0:T(8,128)(2,1)S(1)}, bf16[32,64,128]{2,1,0:T(8,128)(2,1)S(1)}, u32[]{:S(2)}, u32[]{:S(2)}) collective-permute-start(bf16[32,64,128]{2,1,0:T(8,128)(2,1)S(1)} %broadcast_select_fusion), channel_id=1, source_target_pairs={{0,48},{1,49},{2,50},{3,51},{4,388},{5,389},{6,390},{7,391},{8,24}... | collective-permute-start | bytes 1572872 | tf_op jit(solution)/shard_map/ppermute | solution.py:62
  61.8 14.7 %collective-permute-start.7 = (bf16[32,64,128]{2,1,0:T(8,128)(2,1)S(1)}, bf16[32,64,128]{2,1,0:T(8,128)(2,1)S(1)}, u32[]{:S(2)}, u32[]{:S(2)}) collective-permute-start(bf16[32,64,128]{2,1,0:T(8,128)(2,1)S(1)} %collective-permute-done.2.refs_1_), channel_id=1, source_target_pairs={{0,8},{1,9},{2,10},{3,11},{4,68},{5,69},{6,70},{7,71},{8,16},{9,17... | collective-permute-start | bytes 1572872 | tf_op jit(solution)/shard_map/ppermute | solution.py:62
  64.2 12.3 %collective-permute-start.8 = (bf16[32,64,128]{2,1,0:T(8,128)(2,1)S(1)}, bf16[32,64,128]{2,1,0:T(8,128)(2,1)S(1)}, u32[]{:S(2)}, u32[]{:S(2)}) collective-permute-start(bf16[32,64,128]{2,1,0:T(8,128)(2,1)S(1)} %collective-permute-done.3.refs_2_), channel_id=1, source_target_pairs={{0,56},{1,57},{2,58},{3,59},{4,452},{5,453},{6,454},{7,455},{8,0},... | collective-permute-start | bytes 1572872 | tf_op jit(solution)/shard_map/ppermute | solution.py:62
  78.2 5.9 %collective-permute-start.9 = (bf16[256,512]{1,0:T(8,128)(2,1)S(1)}, bf16[256,512]{1,0:T(8,128)(2,1)S(1)}, u32[]{:S(2)}, u32[]{:S(2)}) collective-permute-start(bf16[256,512]{1,0:T(8,128)(2,1)S(1)} %get-tuple-element.37), channel_id=1, source_target_pairs={{0,4},{1,5},{2,6},{3,7},{4,0},{5,1},{6,2},{7,3},{8,12},{9,13},{10,... | collective-permute-start | bytes 786440 | tf_op jit(solution)/shard_map/ppermute | solution.py:53
  84.1 20.1 %copy-start = (bf16[256,128]{1,0:T(8,128)(2,1)S(1)}, bf16[256,128]{1,0:T(8,128)(2,1)}, u32[]{:S(2)}) copy-start(bf16[256,128]{1,0:T(8,128)(2,1)} %f_ref.1) | copy-start | bytes 196612
  84.1 20.1 %copy-start.1 = (bf16[512,512]{1,0:T(8,128)(2,1)S(1)}, bf16[512,512]{1,0:T(8,128)(2,1)}, u32[]{:S(2)}) copy-start(bf16[512,512]{1,0:T(8,128)(2,1)} %ow_ref.1) | copy-start | bytes 1572868
  84.1 20.1 %copy-start.2 = (bf16[256,512]{1,0:T(8,128)(2,1)S(1)}, bf16[256,512]{1,0:T(8,128)(2,1)}, u32[]{:S(2)}) copy-start(bf16[256,512]{1,0:T(8,128)(2,1)} %cot_ref.1) | copy-start | bytes 786436
  85.2 19.0 %all-to-all-start.1 = ((bf16[4,256,512]{2,1,0:T(8,128)(2,1)}), bf16[4,256,512]{2,1,0:T(8,128)(2,1)S(1)}, u32[]{:S(2)}, u32[]{:S(2)}) async-start(bf16[4,256,512]{2,1,0:T(8,128)(2,1)} %join.1), calls=%async_computation.1 | async-start | bytes 2097152 | tf_op jit(solution)/shard_map/all_to_all | solution.py:49

commit v7 on v6

--- a/solution.py
+++ b/solution.py
@@ -342,12 +342,6 @@
     by_distance = {0: line}
     for hops in (2, -2, 1, -1):
         by_distance[-hops % NY] = pass_on(line, hops, hops)
-    across = jnp.where(here % 2 == 0, by_distance[2], by_distance[6])
-    arrived, across = lax.optimization_barrier(([by_distance[d] for d in NEAR[1:]], across))
-    by_distance.update(zip(NEAR[1:], arrived))
-    for hops in (1, -1):
-        by_distance[-3 * hops % NY] = pass_on(by_distance[-2 * hops % NY], hops, hops)
-    by_distance[4] = pass_on(across, -2, 2)
     turns = (slots + 2 * STEP - 2) // STEP
     placed = jax.ShapeDtypeStruct((turns * STEP // 2, rows, side), BF16)
     left_own, left_other, meta = call(
@@ -371,6 +365,12 @@
         other_tiles,
     )
 
+    across = jnp.where(here % 2 == 0, by_distance[2], by_distance[6])
+    arrived, across, meta = lax.optimization_barrier(([by_distance[d] for d in NEAR[1:]], across, meta))
+    by_distance.update(zip(NEAR[1:], arrived))
+    for hops in (1, -1):
+        by_distance[-3 * hops % NY] = pass_on(by_distance[-2 * hops % NY], hops, hops)
+    by_distance[4] = pass_on(across, -2, 2)
     whole = jax.ShapeDtypeStruct((rows, width), F32)
     flops = 2 * slots * rows * quarter * width
     line_size = NZ * NN

time: 158 us -> 158 us (level)
    ppermute x3, starting transfers between devices: 12.7 us -> 14.5 us  [swap_cores(): return lax.ppermute(value, AXES, OTHER_CORE)]
  transfers between devices with their start and end apart: 13 -> 13, of which waited for: 6 -> 7; matrix products, arithmetic and copies ran while one was open for 0% -> 0% of each run, Pallas kernels for 8% -> 8%
where the time goes in v7:
time: 158 us; the launch traced here: 157 us
  starting transfers between devices  63 us (40%)
  blocking collectives  49.3 us (31%)
  waiting for transfers between devices  25.5 us (16%)
  Pallas kernels  17.3 us (11%)
  between operations  1.59 us (1%)
    all_to_all x4, blocking collectives, exchange(): lax.all_to_all(pieces, AXES, 0, 0, axis_index_groups=groups_, tiled=True)  49.3 us
    ppermute x7, starting transfers between devices, pass_on(): return lax.ppermute(value, AXES, pairs)  30.5 us
    all_to_all x3, starting transfers between devices, exchange(): lax.all_to_all(pieces, AXES, 0, 0, axis_index_groups=groups_, tiled=True)  18 us
    pallas_call x11, Pallas kernels, call(): pl.pallas_call(kernel, out_shape=out_shape, in_specs=in_specs, out_specs=...  17.3 us
    all_to_all x3, waiting for transfers between devices, exchange(): lax.all_to_all(pieces, AXES, 0, 0, axis_index_groups=groups_, tiled=True)  16.4 us
    ppermute x3, starting transfers between devices, swap_cores(): return lax.ppermute(value, AXES, OTHER_CORE)  14.5 us
    ppermute x7, waiting for transfers between devices, pass_on(): return lax.ppermute(value, AXES, pairs)  7.94 us
  transfers between devices with their start and end apart: 13, of which 7 were waited for; matrix products, arithmetic and copies ran while one was open for 0% of the time, Pallas kernels for 8%

profile of v7, /device:TPU:1, one launch (start us, length us, event | category | flops | bytes accessed | tf_op | source)
XLA Modules:
  0.0 156.9 jit_solution(2180997210146729202)
XLA Ops:
  0.7 1.7 %spread.1 = bf16[32,64,128]{2,1,0:T(8,128)(2,1)} custom-call(bf16[256,128]{1,0:T(8,128)(2,1)} %f_ref.1), custom_call_target="tpu_custom_call" | custom-call | flops 100000 | bytes 1000000 | tf_op jit(solution)/shard_map/spread/pallas_call | solution.py:66
  2.4 10.5 %all-to-all-start = ((bf16[32,64,128]{2,1,0:T(8,128)(2,1)}), bf16[32,64,128]{2,1,0:T(8,128)(2,1)S(1)}, u32[]{:S(2)}, u32[]{:S(2)}) async-start(bf16[32,64,128]{2,1,0:T(8,128)(2,1)} %spread.1), calls=%async_computation | async-start | bytes 1048576 | tf_op jit(solution)/shard_map/all_to_all | solution.py:49
  12.9 6.1 %collective-permute-start.5 = (bf16[48,128,128]{2,1,0:T(8,128)(2,1)}, bf16[48,128,128]{2,1,0:T(8,128)(2,1)}, u32[]{:S(2)}, u32[]{:S(2)}) collective-permute-start(bf16[48,128,128]{2,1,0:T(8,128)(2,1)} %bitcast.6.own_ref), channel_id=1, source_target_pairs={{0,4},{1,5},{2,6},{3,7},{4,0},{5,1},{6,2},{7,3},{8,12},{9,13},{10,... | collective-permute-start | bytes 4718600 | tf_op jit(solution)/shard_map/ppermute | solution.py:53
  19.8 1.9 %collective-permute-start = (s32[97]{0:T(128)S(1)}, s32[97]{0:T(128)S(1)}, u32[]{:S(2)}, u32[]{:S(2)}) collective-permute-start(s32[97]{0:T(128)S(1)} %pad_add_fusion.own_n_ref), channel_id=1, source_target_pairs={{0,4},{1,5},{2,6},{3,7},{4,0},{5,1},{6,2},{7,3},{8,12},{9,13},{10,... | collective-permute-start | bytes 1172 | tf_op jit(solution)/shard_map/ppermute | solution.py:53
  21.7 2.2 %pack.1 = bf16[4,320,512]{2,1,0:T(8,128)(2,1)} custom-call(bf16[128,512]{1,0:T(8,128)(2,1)} %nw_from.1, bf16[128,512]{1,0:T(8,128)(2,1)} %rw_from.1, bf16[256,128]{1,0:T(8,128)(2,1)} %f_ref.1), custom_call_target="tpu_custom_call" | custom-call | flops 100000 | bytes 2000000 | tf_op jit(solution)/shard_map/pack/pallas_call | solution.py:66
  23.9 1.9 %all-to-all-done.refs_0_ = bf16[32,64,128]{2,1,0:T(8,128)(2,1)S(1)} async-done(((bf16[32,64,128]{2,1,0:T(8,128)(2,1)}), bf16[32,64,128]{2,1,0:T(8,128)(2,1)S(1)}, u32[]{:S(2)}, u32[]{:S(2)}) %all-to-all-start) | async-done | bytes 524320 | tf_op jit(solution)/shard_map/all_to_all | solution.py:49
  25.8 5.7 %collective-permute-start.1 = (bf16[32,64,128]{2,1,0:T(8,128)(2,1)S(1)}, bf16[32,64,128]{2,1,0:T(8,128)(2,1)S(1)}, u32[]{:S(2)}, u32[]{:S(2)}) collective-permute-start(bf16[32,64,128]{2,1,0:T(8,128)(2,1)S(1)} %all-to-all-done.refs_0_), channel_id=1, source_target_pairs={{0,16},{1,17},{2,18},{3,19},{4,132},{5,133},{6,134},{7,135},{8,24}... | collective-permute-start | bytes 1572872 | tf_op jit(solution)/shard_map/ppermute | solution.py:62
  31.4 6.8 %collective-permute-start.2 = (bf16[32,64,128]{2,1,0:T(8,128)(2,1)S(1)}, bf16[32,64,128]{2,1,0:T(8,128)(2,1)S(1)}, u32[]{:S(2)}, u32[]{:S(2)}) collective-permute-start(bf16[32,64,128]{2,1,0:T(8,128)(2,1)S(1)} %all-to-all-done.refs_0_), channel_id=1, source_target_pairs={{0,48},{1,49},{2,50},{3,51},{4,388},{5,389},{6,390},{7,391},{8,56}... | collective-permute-start | bytes 1572872 | tf_op jit(solution)/shard_map/ppermute | solution.py:62
  38.2 3.1 %collective-permute-start.3 = (bf16[32,64,128]{2,1,0:T(8,128)(2,1)S(1)}, bf16[32,64,128]{2,1,0:T(8,128)(2,1)S(1)}, u32[]{:S(2)}, u32[]{:S(2)}) collective-permute-start(bf16[32,64,128]{2,1,0:T(8,128)(2,1)S(1)} %all-to-all-done.refs_0_), channel_id=1, source_target_pairs={{0,8},{1,9},{2,10},{3,11},{4,68},{5,69},{6,70},{7,71},{8,16},{9,17... | collective-permute-start | bytes 1572872 | tf_op jit(solution)/shard_map/ppermute | solution.py:62
  41.3 3.4 %collective-permute-start.4 = (bf16[32,64,128]{2,1,0:T(8,128)(2,1)S(1)}, bf16[32,64,128]{2,1,0:T(8,128)(2,1)}, u32[]{:S(2)}, u32[]{:S(2)}) collective-permute-start(bf16[32,64,128]{2,1,0:T(8,128)(2,1)S(1)} %all-to-all-done.refs_0_), channel_id=1, source_target_pairs={{0,56},{1,57},{2,58},{3,59},{4,452},{5,453},{6,454},{7,455},{8,0},... | collective-permute-start | bytes 1572872 | tf_op jit(solution)/shard_map/ppermute | solution.py:62
  44.9 3.5 %all-to-all-start.2 = ((bf16[4,320,512]{2,1,0:T(8,128)(2,1)}), bf16[4,320,512]{2,1,0:T(8,128)(2,1)S(1)}, u32[]{:S(2)}, u32[]{:S(2)}) async-start(bf16[4,320,512]{2,1,0:T(8,128)(2,1)} %pack.1), calls=%async_computation.2 | async-start | bytes 2621440 | tf_op jit(solution)/shard_map/all_to_all | solution.py:49
  48.4 1.9 %collective-permute-done.2.refs_2_ = bf16[32,64,128]{2,1,0:T(8,128)(2,1)S(1)} collective-permute-done((bf16[32,64,128]{2,1,0:T(8,128)(2,1)S(1)}, bf16[32,64,128]{2,1,0:T(8,128)(2,1)S(1)}, u32[]{:S(2)}, u32[]{:S(2)}) %collective-permute-start.2) | collective-permute-done | bytes 524320 | tf_op jit(solution)/shard_map/ppermute | solution.py:62
  50.4 5.2 %place.1 = (bf16[28,256,128]{2,1,0:T(8,128)(2,1)S(1)}, bf16[28,256,128]{2,1,0:T(8,128)(2,1)S(1)}, s32[2,58]{1,0:T(2,128)S(1)}) custom-call(s32[18]{0:T(128)S(1)} %pad_add_fusion.1.where_ref, s32[97]{0:T(128)S(1)} %pad_add_fusion.own_n_ref, s32[97]{0:T(128)S(1)} %collective-permute-done.other_n_ref, bf16[48,128,128]{2,1,0:T(8,128)(2,1)} %bitcast.6.own_ref, ...), custom_call_target="tpu_custom_call" | custom-call | flops 10000000 | bytes 7000000 | tf_op jit(solution)/shard_map/place/pallas_call | solution.py:66
  55.7 1.1 collective-permute-done.4.refs_4_
  56.7 5.1 %collective-permute-start.6 = (bf16[32,64,128]{2,1,0:T(8,128)(2,1)S(1)}, bf16[32,64,128]{2,1,0:T(8,128)(2,1)S(1)}, u32[]{:S(2)}, u32[]{:S(2)}) collective-permute-start(bf16[32,64,128]{2,1,0:T(8,128)(2,1)S(1)} %broadcast_select_fusion), channel_id=1, source_target_pairs={{0,48},{1,49},{2,50},{3,51},{4,388},{5,389},{6,390},{7,391},{8,24}... | collective-permute-start | bytes 1572872 | tf_op jit(solution)/shard_map/ppermute | solution.py:62
  61.8 2.4 %collective-permute-start.7 = (bf16[32,64,128]{2,1,0:T(8,128)(2,1)S(1)}, bf16[32,64,128]{2,1,0:T(8,128)(2,1)S(1)}, u32[]{:S(2)}, u32[]{:S(2)}) collective-permute-start(bf16[32,64,128]{2,1,0:T(8,128)(2,1)S(1)} %collective-permute-done.1.refs_1_), channel_id=1, source_target_pairs={{0,8},{1,9},{2,10},{3,11},{4,68},{5,69},{6,70},{7,71},{8,16},{9,17... | collective-permute-start | bytes 1572872 | tf_op jit(solution)/shard_map/ppermute | solution.py:62
  64.2 4.1 %collective-permute-start.8 = (bf16[32,64,128]{2,1,0:T(8,128)(2,1)S(1)}, bf16[32,64,128]{2,1,0:T(8,128)(2,1)S(1)}, u32[]{:S(2)}, u32[]{:S(2)}) collective-permute-start(bf16[32,64,128]{2,1,0:T(8,128)(2,1)S(1)} %collective-permute-done.2.refs_2_), channel_id=1, source_target_pairs={{0,56},{1,57},{2,58},{3,59},{4,452},{5,453},{6,454},{7,455},{8,0},... | collective-permute-start | bytes 1572872 | tf_op jit(solution)/shard_map/ppermute | solution.py:62
  68.3 2.7 %near.1 = (f32[256,512]{1,0:T(8,128)S(1)}, f32[256,512]{1,0:T(8,128)S(1)}) custom-call(s32[2,58]{1,0:T(2,128)S(1)} %get-tuple-element.28.meta_ref, bf16[28,256,128]{2,1,0:T(8,128)(2,1)S(1)} %get-tuple-element.29.lo_ref, bf16[28,256,128]{2,1,0:T(8,128)(2,1)S(1)} %get-tuple-element.30.lt_ref, bf16[32,64,128]{2,1,0:T(8,128)(2,1)S(1)} %all-to-all-done.refs_0_, ...), custom_call_target="tpu_custom_call" | custom-call | flops 805306368 | bytes 8000000 | tf_op jit(solution)/shard_map/near/pallas_call | solution.py:66
  71.0 4.1 %collective-permute-done.7.refs_1_ = bf16[32,64,128]{2,1,0:T(8,128)(2,1)S(1)} collective-permute-done((bf16[32,64,128]{2,1,0:T(8,128)(2,1)S(1)}, bf16[32,64,128]{2,1,0:T(8,128)(2,1)S(1)}, u32[]{:S(2)}, u32[]{:S(2)}) %collective-permute-start.7) | collective-permute-done | bytes 524320 | tf_op jit(solution)/shard_map/ppermute | solution.py:62
  75.2 0.8 collective-permute-done.8.refs_2_
  76.0 1.7 %far.1 = (f32[256,512]{1,0:T(8,128)S(1)}, bf16[256,512]{1,0:T(8,128)(2,1)S(1)}) custom-call(s32[2,58]{1,0:T(2,128)S(1)} %get-tuple-element.28.meta_ref, bf16[28,256,128]{2,1,0:T(8,128)(2,1)S(1)} %get-tuple-element.29.lo_ref, bf16[28,256,128]{2,1,0:T(8,128)(2,1)S(1)} %get-tuple-element.30.lt_ref, f32[256,512]{1,0:T(8,128)S(1)} %get-tuple-element.35.no_ref, ...), custom_call_target="tpu_custom_call" | custom-call | flops 402653184 | bytes 6000000 | tf_op jit(solution)/shard_map/far/pallas_call | solution.py:66
  77.7 6.5 %collective-permute-start.9 = (bf16[256,512]{1,0:T(8,128)(2,1)S(1)}, bf16[256,512]{1,0:T(8,128)(2,1)S(1)}, u32[]{:S(2)}, u32[]{:S(2)}) collective-permute-start(bf16[256,512]{1,0:T(8,128)(2,1)S(1)} %get-tuple-element.39), channel_id=1, source_target_pairs={{0,4},{1,5},{2,6},{3,7},{4,0},{5,1},{6,2},{7,3},{8,12},{9,13},{10,... | collective-permute-start | bytes 786440 | tf_op jit(solution)/shard_map/ppermute | solution.py:53
  84.2 1.1 collective-permute-done.9.came_ref
  85.4 1.1 join.1
  86.5 3.9 %all-to-all-start.1 = ((bf16[4,256,512]{2,1,0:T(8,128)(2,1)}), bf16[4,256,512]{2,1,0:T(8,128)(2,1)S(1)}, u32[]{:S(2)}, u32[]{:S(2)}) async-start(bf16[4,256,512]{2,1,0:T(8,128)(2,1)} %join.1), calls=%async_computation.1 | async-start | bytes 2097152 | tf_op jit(solution)/shard_map/all_to_all | solution.py:49
  90.4 14.5 %all-to-all-done.1.a_ref = bf16[4,256,512]{2,1,0:T(8,128)(2,1)S(1)} async-done(((bf16[4,256,512]{2,1,0:T(8,128)(2,1)}), bf16[4,256,512]{2,1,0:T(8,128)(2,1)S(1)}, u32[]{:S(2)}, u32[]{:S(2)}) %all-to-all-start.1) | async-done | bytes 1048608 | tf_op jit(solution)/shard_map/all_to_all | solution.py:49
  105.0 1.6 %dense.1 = (bf16[256,128]{1,0:T(8,128)(2,1)}, bf16[12,128,128]{2,1,0:T(8,128)(2,1)S(1)}) custom-call(s32[1]{0:T(128)} %bitcast.n_ref, bf16[4,256,512]{2,1,0:T(8,128)(2,1)S(1)} %all-to-all-done.1.a_ref, bf16[4,320,512]{2,1,0:T(8,128)(2,1)S(1)} %all-to-all-done.2.w_ref, bf16[256,128]{1,0:T(8,128)(2,1)S(1)} %copy-done, bf16[256,512]{1,0:T(8,128)(2,1)S(1)} %copy-done.2, ...), custom_call_target="tpu_custom_call" | custom-call | flops 805306368 | bytes 5000000 | tf_op jit(solution)/shard_map/dense/pallas_call | solution.py:66
  106.6 11.4 %all_to_all.35.in_ref = bf16[8,192,128]{2,1,0:T(8,128)(2,1)S(1)} all-to-all(bf16[8,192,128]{2,1,0:T(8,128)(2,1)S(1)} %bitcast.11), channel_id=1, replica_groups={{0,4,8,12,64,68,72,76},{1,5,9,13,65,69,73,77},{2,6,10,14,66,70,74,78},{..., dimensions={0} | all-to-all | bytes 786432 | tf_op jit(solution)/shard_map/all_to_all | solution.py:49
  118.0 12.6 %all_to_all.36.in_ref = bf16[4,192,128]{2,1,0:T(8,128)(2,1)S(1)} all-to-all(bf16[4,192,128]{2,1,0:T(8,128)(2,1)S(1)} %total.3), channel_id=1, replica_groups={{0,16,32,48},{1,17,33,49},{2,18,34,50},{3,19,35,51},{4,20,36,52},{5,21,..., dimensions={0} | all-to-all | bytes 393216 | tf_op jit(solution)/shard_map/all_to_all | solution.py:49
  130.6 11.2 %all_to_all.37.in_ref = bf16[4,192,128]{2,1,0:T(8,128)(2,1)S(1)} all-to-all(bf16[4,192,128]{2,1,0:T(8,128)(2,1)S(1)} %total.4), channel_id=1, replica_groups={{0,128,256,384},{1,129,257,385},{2,130,258,386},{3,131,259,387},{4,132,..., dimensions={0} | all-to-all | bytes 393216 | tf_op jit(solution)/shard_map/all_to_all | solution.py:49
  141.8 14.2 %all_to_all.38 = bf16[8,192,128]{2,1,0:T(8,128)(2,1)S(1)} all-to-all(bf16[8,192,128]{2,1,0:T(8,128)(2,1)S(1)} %total.5), channel_id=1, replica_groups={{0,4,8,12,64,68,72,76},{1,5,9,13,65,69,73,77},{2,6,10,14,66,70,74,78},{..., dimensions={0} | all-to-all | bytes 786432 | tf_op jit(solution)/shard_map/all_to_all | solution.py:49
  156.0 0.9 last.1
  (24 shorter events, 0.4 us)
Async XLA Ops:
  0.6 44.1 %copy-start.5 = (s32[16]{0:T(128)S(1)}, s32[16]{0:T(128)}, u32[]{:S(2)}) copy-start(s32[16]{0:T(128)} %constant.61.clone) | copy-start | bytes 196
  0.6 19.0 %copy-start.4 = (s32[1,1,48]{2,1,0:T(1,128)S(1)}, s32[1,1,48]{2,1,0:T(1,128)}, u32[]{:S(2)}) copy-start(s32[1,1,48]{2,1,0:T(1,128)} %param.12) | copy-start | bytes 580
  0.7 19.0 %copy-start.3 = (s32[1,1,48]{2,1,0:T(1,128)S(1)}, s32[1,1,48]{2,1,0:T(1,128)}, u32[]{:S(2)}) copy-start(s32[1,1,48]{2,1,0:T(1,128)} %param.13) | copy-start | bytes 580
  2.4 23.3 %all-to-all-start = ((bf16[32,64,128]{2,1,0:T(8,128)(2,1)}), bf16[32,64,128]{2,1,0:T(8,128)(2,1)S(1)}, u32[]{:S(2)}, u32[]{:S(2)}) async-start(bf16[32,64,128]{2,1,0:T(8,128)(2,1)} %spread.1), calls=%async_computation | async-start | bytes 1048576 | tf_op jit(solution)/shard_map/all_to_all | solution.py:49
  12.9 37.5 %collective-permute-start.5 = (bf16[48,128,128]{2,1,0:T(8,128)(2,1)}, bf16[48,128,128]{2,1,0:T(8,128)(2,1)}, u32[]{:S(2)}, u32[]{:S(2)}) collective-permute-start(bf16[48,128,128]{2,1,0:T(8,128)(2,1)} %bitcast.6.own_ref), channel_id=1, source_target_pairs={{0,4},{1,5},{2,6},{3,7},{4,0},{5,1},{6,2},{7,3},{8,12},{9,13},{10,... | collective-permute-start | bytes 4718600 | tf_op jit(solution)/shard_map/ppermute | solution.py:53
  19.8 4.1 %collective-permute-start = (s32[97]{0:T(128)S(1)}, s32[97]{0:T(128)S(1)}, u32[]{:S(2)}, u32[]{:S(2)}) collective-permute-start(s32[97]{0:T(128)S(1)} %pad_add_fusion.own_n_ref), channel_id=1, source_target_pairs={{0,4},{1,5},{2,6},{3,7},{4,0},{5,1},{6,2},{7,3},{8,12},{9,13},{10,... | collective-permute-start | bytes 1172 | tf_op jit(solution)/shard_map/ppermute | solution.py:53
  25.8 22.7 %collective-permute-start.1 = (bf16[32,64,128]{2,1,0:T(8,128)(2,1)S(1)}, bf16[32,64,128]{2,1,0:T(8,128)(2,1)S(1)}, u32[]{:S(2)}, u32[]{:S(2)}) collective-permute-start(bf16[32,64,128]{2,1,0:T(8,128)(2,1)S(1)} %all-to-all-done.refs_0_), channel_id=1, source_target_pairs={{0,16},{1,17},{2,18},{3,19},{4,132},{5,133},{6,134},{7,135},{8,24}... | collective-permute-start | bytes 1572872 | tf_op jit(solution)/shard_map/ppermute | solution.py:62
  31.4 18.9 %collective-permute-start.2 = (bf16[32,64,128]{2,1,0:T(8,128)(2,1)S(1)}, bf16[32,64,128]{2,1,0:T(8,128)(2,1)S(1)}, u32[]{:S(2)}, u32[]{:S(2)}) collective-permute-start(bf16[32,64,128]{2,1,0:T(8,128)(2,1)S(1)} %all-to-all-done.refs_0_), channel_id=1, source_target_pairs={{0,48},{1,49},{2,50},{3,51},{4,388},{5,389},{6,390},{7,391},{8,56}... | collective-permute-start | bytes 1572872 | tf_op jit(solution)/shard_map/ppermute | solution.py:62
  38.2 17.5 %collective-permute-start.3 = (bf16[32,64,128]{2,1,0:T(8,128)(2,1)S(1)}, bf16[32,64,128]{2,1,0:T(8,128)(2,1)S(1)}, u32[]{:S(2)}, u32[]{:S(2)}) collective-permute-start(bf16[32,64,128]{2,1,0:T(8,128)(2,1)S(1)} %all-to-all-done.refs_0_), channel_id=1, source_target_pairs={{0,8},{1,9},{2,10},{3,11},{4,68},{5,69},{6,70},{7,71},{8,16},{9,17... | collective-permute-start | bytes 1572872 | tf_op jit(solution)/shard_map/ppermute | solution.py:62
  41.3 15.4 %collective-permute-start.4 = (bf16[32,64,128]{2,1,0:T(8,128)(2,1)S(1)}, bf16[32,64,128]{2,1,0:T(8,128)(2,1)}, u32[]{:S(2)}, u32[]{:S(2)}) collective-permute-start(bf16[32,64,128]{2,1,0:T(8,128)(2,1)S(1)} %all-to-all-done.refs_0_), channel_id=1, source_target_pairs={{0,56},{1,57},{2,58},{3,59},{4,452},{5,453},{6,454},{7,455},{8,0},... | collective-permute-start | bytes 1572872 | tf_op jit(solution)/shard_map/ppermute | solution.py:62
  44.9 41.6 %all-to-all-start.2 = ((bf16[4,320,512]{2,1,0:T(8,128)(2,1)}), bf16[4,320,512]{2,1,0:T(8,128)(2,1)S(1)}, u32[]{:S(2)}, u32[]{:S(2)}) async-start(bf16[4,320,512]{2,1,0:T(8,128)(2,1)} %pack.1), calls=%async_computation.2 | async-start | bytes 2621440 | tf_op jit(solution)/shard_map/all_to_all | solution.py:49
  56.7 14.3 %collective-permute-start.6 = (bf16[32,64,128]{2,1,0:T(8,128)(2,1)S(1)}, bf16[32,64,128]{2,1,0:T(8,128)(2,1)S(1)}, u32[]{:S(2)}, u32[]{:S(2)}) collective-permute-start(bf16[32,64,128]{2,1,0:T(8,128)(2,1)S(1)} %broadcast_select_fusion), channel_id=1, source_target_pairs={{0,48},{1,49},{2,50},{3,51},{4,388},{5,389},{6,390},{7,391},{8,24}... | collective-permute-start | bytes 1572872 | tf_op jit(solution)/shard_map/ppermute | solution.py:62
  61.8 13.4 %collective-permute-start.7 = (bf16[32,64,128]{2,1,0:T(8,128)(2,1)S(1)}, bf16[32,64,128]{2,1,0:T(8,128)(2,1)S(1)}, u32[]{:S(2)}, u32[]{:S(2)}) collective-permute-start(bf16[32,64,128]{2,1,0:T(8,128)(2,1)S(1)} %collective-permute-done.1.refs_1_), channel_id=1, source_target_pairs={{0,8},{1,9},{2,10},{3,11},{4,68},{5,69},{6,70},{7,71},{8,16},{9,17... | collective-permute-start | bytes 1572872 | tf_op jit(solution)/shard_map/ppermute | solution.py:62
  64.2 11.8 %collective-permute-start.8 = (bf16[32,64,128]{2,1,0:T(8,128)(2,1)S(1)}, bf16[32,64,128]{2,1,0:T(8,128)(2,1)S(1)}, u32[]{:S(2)}, u32[]{:S(2)}) collective-permute-start(bf16[32,64,128]{2,1,0:T(8,128)(2,1)S(1)} %collective-permute-done.2.refs_2_), channel_id=1, source_target_pairs={{0,56},{1,57},{2,58},{3,59},{4,452},{5,453},{6,454},{7,455},{8,0},... | collective-permute-start | bytes 1572872 | tf_op jit(solution)/shard_map/ppermute | solution.py:62
  77.7 7.7 %collective-permute-start.9 = (bf16[256,512]{1,0:T(8,128)(2,1)S(1)}, bf16[256,512]{1,0:T(8,128)(2,1)S(1)}, u32[]{:S(2)}, u32[]{:S(2)}) collective-permute-start(bf16[256,512]{1,0:T(8,128)(2,1)S(1)} %get-tuple-element.39), channel_id=1, source_target_pairs={{0,4},{1,5},{2,6},{3,7},{4,0},{5,1},{6,2},{7,3},{8,12},{9,13},{10,... | collective-permute-start | bytes 786440 | tf_op jit(solution)/shard_map/ppermute | solution.py:53
  85.4 19.6 %copy-start = (bf16[256,128]{1,0:T(8,128)(2,1)S(1)}, bf16[256,128]{1,0:T(8,128)(2,1)}, u32[]{:S(2)}) copy-start(bf16[256,128]{1,0:T(8,128)(2,1)} %f_ref.1) | copy-start | bytes 196612
  85.4 19.6 %copy-start.1 = (bf16[512,512]{1,0:T(8,128)(2,1)S(1)}, bf16[512,512]{1,0:T(8,128)(2,1)}, u32[]{:S(2)}) copy-start(bf16[512,512]{1,0:T(8,128)(2,1)} %ow_ref.1) | copy-start | bytes 1572868
  85.4 19.6 %copy-start.2 = (bf16[256,512]{1,0:T(8,128)(2,1)S(1)}, bf16[256,512]{1,0:T(8,128)(2,1)}, u32[]{:S(2)}) copy-start(bf16[256,512]{1,0:T(8,128)(2,1)} %cot_ref.1) | copy-start | bytes 786436
  86.5 18.5 %all-to-all-start.1 = ((bf16[4,256,512]{2,1,0:T(8,128)(2,1)}), bf16[4,256,512]{2,1,0:T(8,128)(2,1)S(1)}, u32[]{:S(2)}, u32[]{:S(2)}) async-start(bf16[4,256,512]{2,1,0:T(8,128)(2,1)} %join.1), calls=%async_computation.1 | async-start | bytes 2097152 | tf_op jit(solution)/shard_map/all_to_all | solution.py:49

commit v8 on v7

--- a/solution.py
+++ b/solution.py
@@ -366,8 +366,8 @@
     )
 
     across = jnp.where(here % 2 == 0, by_distance[2], by_distance[6])
-    arrived, across, meta = lax.optimization_barrier(([by_distance[d] for d in NEAR[1:]], across, meta))
-    by_distance.update(zip(NEAR[1:], arrived))
+    arrived, across = lax.optimization_barrier(([by_distance[d] for d in NEAR[1:3]], across))
+    by_distance.update(zip(NEAR[1:3], arrived))
     for hops in (1, -1):
         by_distance[-3 * hops % NY] = pass_on(by_distance[-2 * hops % NY], hops, hops)
     by_distance[4] = pass_on(across, -2, 2)

time: 158 us -> 154 us (0.975)
  waiting for transfers between devices: 25.5 us -> 19.8 us
  Pallas kernels: 17.3 us -> 21.6 us
  starting transfers between devices: 63 us -> 61.3 us
    ppermute x7, waiting for transfers between devices: 7.94 us -> 1.99 us  [pass_on(): return lax.ppermute(value, AXES, pairs)]
    pallas_call x11, Pallas kernels: 17.3 us -> 21.6 us  [call(): pl.pallas_call(kernel, out_shape=out_shape, in_specs=in_specs, out_specs=...]
  transfers between devices with their start and end apart: 13 -> 13, of which waited for: 7 -> 4; matrix products, arithmetic and copies ran while one was open for 0% -> 0% of each run, Pallas kernels for 8% -> 11%
where the time goes in v8:
time: 154 us; the launch traced here: 153 us
  starting transfers between devices  61.3 us (40%)
  blocking collectives  48 us (31%)
  Pallas kernels  21.6 us (14%)
  waiting for transfers between devices  19.8 us (13%)
  between operations  1.62 us (1%)
    all_to_all x4, blocking collectives, exchange(): lax.all_to_all(pieces, AXES, 0, 0, axis_index_groups=groups_, tiled=True)  48 us
    ppermute x7, starting transfers between devices, pass_on(): return lax.ppermute(value, AXES, pairs)  30.4 us
    pallas_call x11, Pallas kernels, call(): pl.pallas_call(kernel, out_shape=out_shape, in_specs=in_specs, out_specs=...  21.6 us
    all_to_all x3, starting transfers between devices, exchange(): lax.all_to_all(pieces, AXES, 0, 0, axis_index_groups=groups_, tiled=True)  17.6 us
    all_to_all x3, waiting for transfers between devices, exchange(): lax.all_to_all(pieces, AXES, 0, 0, axis_index_groups=groups_, tiled=True)  16.7 us
    ppermute x3, starting transfers between devices, swap_cores(): return lax.ppermute(value, AXES, OTHER_CORE)  13.3 us
  transfers between devices with their start and end apart: 13, of which 4 were waited for; matrix products, arithmetic and copies ran while one was open for 0% of the time, Pallas kernels for 11%

profile of v8, /device:TPU:1, one launch (start us, length us, event | category | flops | bytes accessed | tf_op | source)
XLA Modules:
  0.0 152.6 jit_solution(1194341463148000999)
XLA Ops:
  0.7 1.7 %spread.1 = bf16[32,64,128]{2,1,0:T(8,128)(2,1)} custom-call(bf16[256,128]{1,0:T(8,128)(2,1)} %f_ref.1), custom_call_target="tpu_custom_call" | custom-call | flops 100000 | bytes 1000000 | tf_op jit(solution)/shard_map/spread/pallas_call | solution.py:66
  2.4 10.5 %all-to-all-start = ((bf16[32,64,128]{2,1,0:T(8,128)(2,1)}), bf16[32,64,128]{2,1,0:T(8,128)(2,1)S(1)}, u32[]{:S(2)}, u32[]{:S(2)}) async-start(bf16[32,64,128]{2,1,0:T(8,128)(2,1)} %spread.1), calls=%async_computation | async-start | bytes 1048576 | tf_op jit(solution)/shard_map/all_to_all | solution.py:49
  12.9 6.1 %collective-permute-start.1 = (bf16[48,128,128]{2,1,0:T(8,128)(2,1)}, bf16[48,128,128]{2,1,0:T(8,128)(2,1)}, u32[]{:S(2)}, u32[]{:S(2)}) collective-permute-start(bf16[48,128,128]{2,1,0:T(8,128)(2,1)} %bitcast.6.own_ref), channel_id=1, source_target_pairs={{0,4},{1,5},{2,6},{3,7},{4,0},{5,1},{6,2},{7,3},{8,12},{9,13},{10,... | collective-permute-start | bytes 4718600 | tf_op jit(solution)/shard_map/ppermute | solution.py:53
  19.7 0.1 pad_add_fusion.1.own_n_ref
  19.7 1.9 %collective-permute-start = (s32[97]{0:T(128)S(1)}, s32[97]{0:T(128)S(1)}, u32[]{:S(2)}, u32[]{:S(2)}) collective-permute-start(s32[97]{0:T(128)S(1)} %pad_add_fusion.1.own_n_ref), channel_id=1, source_target_pairs={{0,4},{1,5},{2,6},{3,7},{4,0},{5,1},{6,2},{7,3},{8,12},{9,13},{10,... | collective-permute-start | bytes 1172 | tf_op jit(solution)/shard_map/ppermute | solution.py:53
  21.7 2.2 %pack.1 = bf16[4,320,512]{2,1,0:T(8,128)(2,1)} custom-call(bf16[128,512]{1,0:T(8,128)(2,1)} %nw_from.1, bf16[128,512]{1,0:T(8,128)(2,1)} %rw_from.1, bf16[256,128]{1,0:T(8,128)(2,1)} %f_ref.1), custom_call_target="tpu_custom_call" | custom-call | flops 100000 | bytes 2000000 | tf_op jit(solution)/shard_map/pack/pallas_call | solution.py:66
  23.9 1.9 %all-to-all-done.refs_0_ = bf16[32,64,128]{2,1,0:T(8,128)(2,1)S(1)} async-done(((bf16[32,64,128]{2,1,0:T(8,128)(2,1)}), bf16[32,64,128]{2,1,0:T(8,128)(2,1)S(1)}, u32[]{:S(2)}, u32[]{:S(2)}) %all-to-all-start) | async-done | bytes 524320 | tf_op jit(solution)/shard_map/all_to_all | solution.py:49
  25.7 5.7 %collective-permute-start.2 = (bf16[32,64,128]{2,1,0:T(8,128)(2,1)S(1)}, bf16[32,64,128]{2,1,0:T(8,128)(2,1)S(1)}, u32[]{:S(2)}, u32[]{:S(2)}) collective-permute-start(bf16[32,64,128]{2,1,0:T(8,128)(2,1)S(1)} %all-to-all-done.refs_0_), channel_id=1, source_target_pairs={{0,16},{1,17},{2,18},{3,19},{4,132},{5,133},{6,134},{7,135},{8,24}... | collective-permute-start | bytes 1572872 | tf_op jit(solution)/shard_map/ppermute | solution.py:62
  31.4 6.8 %collective-permute-start.3 = (bf16[32,64,128]{2,1,0:T(8,128)(2,1)S(1)}, bf16[32,64,128]{2,1,0:T(8,128)(2,1)S(1)}, u32[]{:S(2)}, u32[]{:S(2)}) collective-permute-start(bf16[32,64,128]{2,1,0:T(8,128)(2,1)S(1)} %all-to-all-done.refs_0_), channel_id=1, source_target_pairs={{0,48},{1,49},{2,50},{3,51},{4,388},{5,389},{6,390},{7,391},{8,56}... | collective-permute-start | bytes 1572872 | tf_op jit(solution)/shard_map/ppermute | solution.py:62
  38.3 3.1 %collective-permute-start.4 = (bf16[32,64,128]{2,1,0:T(8,128)(2,1)S(1)}, bf16[32,64,128]{2,1,0:T(8,128)(2,1)S(1)}, u32[]{:S(2)}, u32[]{:S(2)}) collective-permute-start(bf16[32,64,128]{2,1,0:T(8,128)(2,1)S(1)} %all-to-all-done.refs_0_), channel_id=1, source_target_pairs={{0,8},{1,9},{2,10},{3,11},{4,68},{5,69},{6,70},{7,71},{8,16},{9,17... | collective-permute-start | bytes 1572872 | tf_op jit(solution)/shard_map/ppermute | solution.py:62
  41.4 3.4 %collective-permute-start.5 = (bf16[32,64,128]{2,1,0:T(8,128)(2,1)S(1)}, bf16[32,64,128]{2,1,0:T(8,128)(2,1)}, u32[]{:S(2)}, u32[]{:S(2)}) collective-permute-start(bf16[32,64,128]{2,1,0:T(8,128)(2,1)S(1)} %all-to-all-done.refs_0_), channel_id=1, source_target_pairs={{0,56},{1,57},{2,58},{3,59},{4,452},{5,453},{6,454},{7,455},{8,0},... | collective-permute-start | bytes 1572872 | tf_op jit(solution)/shard_map/ppermute | solution.py:62
  44.8 3.6 %all-to-all-start.2 = ((bf16[4,320,512]{2,1,0:T(8,128)(2,1)}), bf16[4,320,512]{2,1,0:T(8,128)(2,1)S(1)}, u32[]{:S(2)}, u32[]{:S(2)}) async-start(bf16[4,320,512]{2,1,0:T(8,128)(2,1)} %pack.1), calls=%async_computation.2 | async-start | bytes 2621440 | tf_op jit(solution)/shard_map/all_to_all | solution.py:49
  48.3 2.0 %collective-permute-done.3.refs_2_ = bf16[32,64,128]{2,1,0:T(8,128)(2,1)S(1)} collective-permute-done((bf16[32,64,128]{2,1,0:T(8,128)(2,1)S(1)}, bf16[32,64,128]{2,1,0:T(8,128)(2,1)S(1)}, u32[]{:S(2)}, u32[]{:S(2)}) %collective-permute-start.3) | collective-permute-done | bytes 524320 | tf_op jit(solution)/shard_map/ppermute | solution.py:62
  50.3 0.1 broadcast_select_fusion
  50.4 5.0 %collective-permute-start.6 = (bf16[32,64,128]{2,1,0:T(8,128)(2,1)S(1)}, bf16[32,64,128]{2,1,0:T(8,128)(2,1)S(1)}, u32[]{:S(2)}, u32[]{:S(2)}) collective-permute-start(bf16[32,64,128]{2,1,0:T(8,128)(2,1)S(1)} %broadcast_select_fusion), channel_id=1, source_target_pairs={{0,48},{1,49},{2,50},{3,51},{4,388},{5,389},{6,390},{7,391},{8,24}... | collective-permute-start | bytes 1572872 | tf_op jit(solution)/shard_map/ppermute | solution.py:62
  55.3 3.7 %collective-permute-start.7 = (bf16[32,64,128]{2,1,0:T(8,128)(2,1)S(1)}, bf16[32,64,128]{2,1,0:T(8,128)(2,1)S(1)}, u32[]{:S(2)}, u32[]{:S(2)}) collective-permute-start(bf16[32,64,128]{2,1,0:T(8,128)(2,1)S(1)} %collective-permute-done.2.refs_1_), channel_id=1, source_target_pairs={{0,8},{1,9},{2,10},{3,11},{4,68},{5,69},{6,70},{7,71},{8,16},{9,17... | collective-permute-start | bytes 1572872 | tf_op jit(solution)/shard_map/ppermute | solution.py:62
  59.1 2.8 %collective-permute-start.8 = (bf16[32,64,128]{2,1,0:T(8,128)(2,1)S(1)}, bf16[32,64,128]{2,1,0:T(8,128)(2,1)S(1)}, u32[]{:S(2)}, u32[]{:S(2)}) collective-permute-start(bf16[32,64,128]{2,1,0:T(8,128)(2,1)S(1)} %collective-permute-done.3.refs_2_), channel_id=1, source_target_pairs={{0,56},{1,57},{2,58},{3,59},{4,452},{5,453},{6,454},{7,455},{8,0},... | collective-permute-start | bytes 1572872 | tf_op jit(solution)/shard_map/ppermute | solution.py:62
  61.9 0.1 pad_add_fusion.where_ref
  62.0 7.6 %place.1 = (bf16[28,256,128]{2,1,0:T(8,128)(2,1)S(1)}, bf16[28,256,128]{2,1,0:T(8,128)(2,1)S(1)}, s32[2,58]{1,0:T(2,128)S(1)}) custom-call(s32[18]{0:T(128)S(1)} %pad_add_fusion.where_ref, s32[97]{0:T(128)S(1)} %pad_add_fusion.1.own_n_ref, s32[97]{0:T(128)S(1)} %collective-permute-done.other_n_ref, bf16[48,128,128]{2,1,0:T(8,128)(2,1)} %bitcast.6.own_ref, ...), custom_call_target="tpu_custom_call" | custom-call | flops 10000000 | bytes 7000000 | tf_op jit(solution)/shard_map/place/pallas_call | solution.py:66
  69.6 3.9 %near.1 = (f32[256,512]{1,0:T(8,128)S(1)}, f32[256,512]{1,0:T(8,128)S(1)}) custom-call(s32[2,58]{1,0:T(2,128)S(1)} %get-tuple-element.23.meta_ref, bf16[28,256,128]{2,1,0:T(8,128)(2,1)S(1)} %get-tuple-element.24.lo_ref, bf16[28,256,128]{2,1,0:T(8,128)(2,1)S(1)} %get-tuple-element.25.lt_ref, bf16[32,64,128]{2,1,0:T(8,128)(2,1)S(1)} %all-to-all-done.refs_0_, ...), custom_call_target="tpu_custom_call" | custom-call | flops 805306368 | bytes 8000000 | tf_op jit(solution)/shard_map/near/pallas_call | solution.py:66
  73.6 2.3 %far.1 = (f32[256,512]{1,0:T(8,128)S(1)}, bf16[256,512]{1,0:T(8,128)(2,1)S(1)}) custom-call(s32[2,58]{1,0:T(2,128)S(1)} %get-tuple-element.23.meta_ref, bf16[28,256,128]{2,1,0:T(8,128)(2,1)S(1)} %get-tuple-element.24.lo_ref, bf16[28,256,128]{2,1,0:T(8,128)(2,1)S(1)} %get-tuple-element.25.lt_ref, f32[256,512]{1,0:T(8,128)S(1)} %get-tuple-element.29.no_ref, ...), custom_call_target="tpu_custom_call" | custom-call | flops 402653184 | bytes 6000000 | tf_op jit(solution)/shard_map/far/pallas_call | solution.py:66
  75.9 5.3 %collective-permute-start.9 = (bf16[256,512]{1,0:T(8,128)(2,1)S(1)}, bf16[256,512]{1,0:T(8,128)(2,1)S(1)}, u32[]{:S(2)}, u32[]{:S(2)}) collective-permute-start(bf16[256,512]{1,0:T(8,128)(2,1)S(1)} %get-tuple-element.33), channel_id=1, source_target_pairs={{0,4},{1,5},{2,6},{3,7},{4,0},{5,1},{6,2},{7,3},{8,12},{9,13},{10,... | collective-permute-start | bytes 786440 | tf_op jit(solution)/shard_map/ppermute | solution.py:53
  81.3 1.1 collective-permute-done.9.came_ref
  82.4 1.1 join.1
  83.5 3.5 %all-to-all-start.1 = ((bf16[4,256,512]{2,1,0:T(8,128)(2,1)}), bf16[4,256,512]{2,1,0:T(8,128)(2,1)S(1)}, u32[]{:S(2)}, u32[]{:S(2)}) async-start(bf16[4,256,512]{2,1,0:T(8,128)(2,1)} %join.1), calls=%async_computation.1 | async-start | bytes 2097152 | tf_op jit(solution)/shard_map/all_to_all | solution.py:49
  87.0 14.8 %all-to-all-done.1.a_ref = bf16[4,256,512]{2,1,0:T(8,128)(2,1)S(1)} async-done(((bf16[4,256,512]{2,1,0:T(8,128)(2,1)}), bf16[4,256,512]{2,1,0:T(8,128)(2,1)S(1)}, u32[]{:S(2)}, u32[]{:S(2)}) %all-to-all-start.1) | async-done | bytes 1048608 | tf_op jit(solution)/shard_map/all_to_all | solution.py:49
  101.9 1.6 %dense.1 = (bf16[256,128]{1,0:T(8,128)(2,1)}, bf16[12,128,128]{2,1,0:T(8,128)(2,1)S(1)}) custom-call(s32[1]{0:T(128)} %bitcast.n_ref, bf16[4,256,512]{2,1,0:T(8,128)(2,1)S(1)} %all-to-all-done.1.a_ref, bf16[4,320,512]{2,1,0:T(8,128)(2,1)S(1)} %all-to-all-done.2.w_ref, bf16[256,128]{1,0:T(8,128)(2,1)S(1)} %copy-done, bf16[256,512]{1,0:T(8,128)(2,1)S(1)} %copy-done.2, ...), custom_call_target="tpu_custom_call" | custom-call | flops 805306368 | bytes 5000000 | tf_op jit(solution)/shard_map/dense/pallas_call | solution.py:66
  103.5 11.0 %all_to_all.35.in_ref = bf16[8,192,128]{2,1,0:T(8,128)(2,1)S(1)} all-to-all(bf16[8,192,128]{2,1,0:T(8,128)(2,1)S(1)} %bitcast.11), channel_id=1, replica_groups={{0,4,8,12,64,68,72,76},{1,5,9,13,65,69,73,77},{2,6,10,14,66,70,74,78},{..., dimensions={0} | all-to-all | bytes 786432 | tf_op jit(solution)/shard_map/all_to_all | solution.py:49
  114.6 12.6 %all_to_all.36.in_ref = bf16[4,192,128]{2,1,0:T(8,128)(2,1)S(1)} all-to-all(bf16[4,192,128]{2,1,0:T(8,128)(2,1)S(1)} %total.3), channel_id=1, replica_groups={{0,16,32,48},{1,17,33,49},{2,18,34,50},{3,19,35,51},{4,20,36,52},{5,21,..., dimensions={0} | all-to-all | bytes 393216 | tf_op jit(solution)/shard_map/all_to_all | solution.py:49
  127.2 10.3 %all_to_all.37.in_ref = bf16[4,192,128]{2,1,0:T(8,128)(2,1)S(1)} all-to-all(bf16[4,192,128]{2,1,0:T(8,128)(2,1)S(1)} %total.4), channel_id=1, replica_groups={{0,128,256,384},{1,129,257,385},{2,130,258,386},{3,131,259,387},{4,132,..., dimensions={0} | all-to-all | bytes 393216 | tf_op jit(solution)/shard_map/all_to_all | solution.py:49
  137.5 14.1 %all_to_all.38 = bf16[8,192,128]{2,1,0:T(8,128)(2,1)S(1)} all-to-all(bf16[8,192,128]{2,1,0:T(8,128)(2,1)S(1)} %total.5), channel_id=1, replica_groups={{0,4,8,12,64,68,72,76},{1,5,9,13,65,69,73,77},{2,6,10,14,66,70,74,78},{..., dimensions={0} | all-to-all | bytes 786432 | tf_op jit(solution)/shard_map/all_to_all | solution.py:49
  151.6 0.9 last.1
  (24 shorter events, 0.2 us)
Async XLA Ops:
  0.6 19.0 %copy-start.4 = (s32[1,1,48]{2,1,0:T(1,128)S(1)}, s32[1,1,48]{2,1,0:T(1,128)}, u32[]{:S(2)}) copy-start(s32[1,1,48]{2,1,0:T(1,128)} %param.12) | copy-start | bytes 580
  0.6 19.0 %copy-start.3 = (s32[1,1,48]{2,1,0:T(1,128)S(1)}, s32[1,1,48]{2,1,0:T(1,128)}, u32[]{:S(2)}) copy-start(s32[1,1,48]{2,1,0:T(1,128)} %param.13) | copy-start | bytes 580
  2.4 23.3 %all-to-all-start = ((bf16[32,64,128]{2,1,0:T(8,128)(2,1)}), bf16[32,64,128]{2,1,0:T(8,128)(2,1)S(1)}, u32[]{:S(2)}, u32[]{:S(2)}) async-start(bf16[32,64,128]{2,1,0:T(8,128)(2,1)} %spread.1), calls=%async_computation | async-start | bytes 1048576 | tf_op jit(solution)/shard_map/all_to_all | solution.py:49
  12.9 46.1 %collective-permute-start.1 = (bf16[48,128,128]{2,1,0:T(8,128)(2,1)}, bf16[48,128,128]{2,1,0:T(8,128)(2,1)}, u32[]{:S(2)}, u32[]{:S(2)}) collective-permute-start(bf16[48,128,128]{2,1,0:T(8,128)(2,1)} %bitcast.6.own_ref), channel_id=1, source_target_pairs={{0,4},{1,5},{2,6},{3,7},{4,0},{5,1},{6,2},{7,3},{8,12},{9,13},{10,... | collective-permute-start | bytes 4718600 | tf_op jit(solution)/shard_map/ppermute | solution.py:53
  19.7 4.1 %collective-permute-start = (s32[97]{0:T(128)S(1)}, s32[97]{0:T(128)S(1)}, u32[]{:S(2)}, u32[]{:S(2)}) collective-permute-start(s32[97]{0:T(128)S(1)} %pad_add_fusion.1.own_n_ref), channel_id=1, source_target_pairs={{0,4},{1,5},{2,6},{3,7},{4,0},{5,1},{6,2},{7,3},{8,12},{9,13},{10,... | collective-permute-start | bytes 1172 | tf_op jit(solution)/shard_map/ppermute | solution.py:53
  25.7 22.6 %collective-permute-start.2 = (bf16[32,64,128]{2,1,0:T(8,128)(2,1)S(1)}, bf16[32,64,128]{2,1,0:T(8,128)(2,1)S(1)}, u32[]{:S(2)}, u32[]{:S(2)}) collective-permute-start(bf16[32,64,128]{2,1,0:T(8,128)(2,1)S(1)} %all-to-all-done.refs_0_), channel_id=1, source_target_pairs={{0,16},{1,17},{2,18},{3,19},{4,132},{5,133},{6,134},{7,135},{8,24}... | collective-permute-start | bytes 1572872 | tf_op jit(solution)/shard_map/ppermute | solution.py:62
  31.4 18.9 %collective-permute-start.3 = (bf16[32,64,128]{2,1,0:T(8,128)(2,1)S(1)}, bf16[32,64,128]{2,1,0:T(8,128)(2,1)S(1)}, u32[]{:S(2)}, u32[]{:S(2)}) collective-permute-start(bf16[32,64,128]{2,1,0:T(8,128)(2,1)S(1)} %all-to-all-done.refs_0_), channel_id=1, source_target_pairs={{0,48},{1,49},{2,50},{3,51},{4,388},{5,389},{6,390},{7,391},{8,56}... | collective-permute-start | bytes 1572872 | tf_op jit(solution)/shard_map/ppermute | solution.py:62
  38.2 23.6 %copy-start.5 = (s32[16]{0:T(128)S(1)}, s32[16]{0:T(128)}, u32[]{:S(2)}) copy-start(s32[16]{0:T(128)} %constant.61.clone) | copy-start | bytes 196
  38.3 31.3 %collective-permute-start.4 = (bf16[32,64,128]{2,1,0:T(8,128)(2,1)S(1)}, bf16[32,64,128]{2,1,0:T(8,128)(2,1)S(1)}, u32[]{:S(2)}, u32[]{:S(2)}) collective-permute-start(bf16[32,64,128]{2,1,0:T(8,128)(2,1)S(1)} %all-to-all-done.refs_0_), channel_id=1, source_target_pairs={{0,8},{1,9},{2,10},{3,11},{4,68},{5,69},{6,70},{7,71},{8,16},{9,17... | collective-permute-start | bytes 1572872 | tf_op jit(solution)/shard_map/ppermute | solution.py:62
  41.4 28.2 %collective-permute-start.5 = (bf16[32,64,128]{2,1,0:T(8,128)(2,1)S(1)}, bf16[32,64,128]{2,1,0:T(8,128)(2,1)}, u32[]{:S(2)}, u32[]{:S(2)}) collective-permute-start(bf16[32,64,128]{2,1,0:T(8,128)(2,1)S(1)} %all-to-all-done.refs_0_), channel_id=1, source_target_pairs={{0,56},{1,57},{2,58},{3,59},{4,452},{5,453},{6,454},{7,455},{8,0},... | collective-permute-start | bytes 1572872 | tf_op jit(solution)/shard_map/ppermute | solution.py:62
  44.8 38.7 %all-to-all-start.2 = ((bf16[4,320,512]{2,1,0:T(8,128)(2,1)}), bf16[4,320,512]{2,1,0:T(8,128)(2,1)S(1)}, u32[]{:S(2)}, u32[]{:S(2)}) async-start(bf16[4,320,512]{2,1,0:T(8,128)(2,1)} %pack.1), calls=%async_computation.2 | async-start | bytes 2621440 | tf_op jit(solution)/shard_map/all_to_all | solution.py:49
  50.4 23.2 %collective-permute-start.6 = (bf16[32,64,128]{2,1,0:T(8,128)(2,1)S(1)}, bf16[32,64,128]{2,1,0:T(8,128)(2,1)S(1)}, u32[]{:S(2)}, u32[]{:S(2)}) collective-permute-start(bf16[32,64,128]{2,1,0:T(8,128)(2,1)S(1)} %broadcast_select_fusion), channel_id=1, source_target_pairs={{0,48},{1,49},{2,50},{3,51},{4,388},{5,389},{6,390},{7,391},{8,24}... | collective-permute-start | bytes 1572872 | tf_op jit(solution)/shard_map/ppermute | solution.py:62
  55.3 18.2 %collective-permute-start.7 = (bf16[32,64,128]{2,1,0:T(8,128)(2,1)S(1)}, bf16[32,64,128]{2,1,0:T(8,128)(2,1)S(1)}, u32[]{:S(2)}, u32[]{:S(2)}) collective-permute-start(bf16[32,64,128]{2,1,0:T(8,128)(2,1)S(1)} %collective-permute-done.2.refs_1_), channel_id=1, source_target_pairs={{0,8},{1,9},{2,10},{3,11},{4,68},{5,69},{6,70},{7,71},{8,16},{9,17... | collective-permute-start | bytes 1572872 | tf_op jit(solution)/shard_map/ppermute | solution.py:62
  59.1 14.5 %collective-permute-start.8 = (bf16[32,64,128]{2,1,0:T(8,128)(2,1)S(1)}, bf16[32,64,128]{2,1,0:T(8,128)(2,1)S(1)}, u32[]{:S(2)}, u32[]{:S(2)}) collective-permute-start(bf16[32,64,128]{2,1,0:T(8,128)(2,1)S(1)} %collective-permute-done.3.refs_2_), channel_id=1, source_target_pairs={{0,56},{1,57},{2,58},{3,59},{4,452},{5,453},{6,454},{7,455},{8,0},... | collective-permute-start | bytes 1572872 | tf_op jit(solution)/shard_map/ppermute | solution.py:62
  75.9 6.5 %collective-permute-start.9 = (bf16[256,512]{1,0:T(8,128)(2,1)S(1)}, bf16[256,512]{1,0:T(8,128)(2,1)S(1)}, u32[]{:S(2)}, u32[]{:S(2)}) collective-permute-start(bf16[256,512]{1,0:T(8,128)(2,1)S(1)} %get-tuple-element.33), channel_id=1, source_target_pairs={{0,4},{1,5},{2,6},{3,7},{4,0},{5,1},{6,2},{7,3},{8,12},{9,13},{10,... | collective-permute-start | bytes 786440 | tf_op jit(solution)/shard_map/ppermute | solution.py:53
  82.4 19.4 %copy-start = (bf16[256,128]{1,0:T(8,128)(2,1)S(1)}, bf16[256,128]{1,0:T(8,128)(2,1)}, u32[]{:S(2)}) copy-start(bf16[256,128]{1,0:T(8,128)(2,1)} %f_ref.1) | copy-start | bytes 196612
  82.4 19.4 %copy-start.1 = (bf16[512,512]{1,0:T(8,128)(2,1)S(1)}, bf16[512,512]{1,0:T(8,128)(2,1)}, u32[]{:S(2)}) copy-start(bf16[512,512]{1,0:T(8,128)(2,1)} %ow_ref.1) | copy-start | bytes 1572868
  82.4 19.4 %copy-start.2 = (bf16[256,512]{1,0:T(8,128)(2,1)S(1)}, bf16[256,512]{1,0:T(8,128)(2,1)}, u32[]{:S(2)}) copy-start(bf16[256,512]{1,0:T(8,128)(2,1)} %cot_ref.1) | copy-start | bytes 786436
  83.5 18.3 %all-to-all-start.1 = ((bf16[4,256,512]{2,1,0:T(8,128)(2,1)}), bf16[4,256,512]{2,1,0:T(8,128)(2,1)S(1)}, u32[]{:S(2)}, u32[]{:S(2)}) async-start(bf16[4,256,512]{2,1,0:T(8,128)(2,1)} %join.1), calls=%async_computation.1 | async-start | bytes 2097152 | tf_op jit(solution)/shard_map/all_to_all | solution.py:49

commit v9 on v8

--- a/solution.py
+++ b/solution.py
@@ -75,11 +75,11 @@
     )(*args)
 
 
-def place_kernel(where_ref, own_n_ref, other_n_ref, own_ref, other_ref, lo_ref, lt_ref, meta_ref, order, tiles, sems):
+def place_kernel(where_ref, one_n_ref, own_ref, one_l_ref, meta_ref, order, tiles, sems):
     slots, half = own_ref.shape[0], own_ref.shape[2] // 2
     side = own_ref.shape[1]
     copies = [
-        pltpu.make_async_copy(ref, tiles.at[k], sems.at[k]) for k, ref in enumerate((own_ref, other_ref))
+        pltpu.make_async_copy(ref, tiles.at[k], sems.at[k]) for k, ref in enumerate((own_ref,))
     ]
     for copy in copies:
         copy.start()
@@ -87,7 +87,7 @@
     first = where_ref[0] == 0
     here = where_ref[1]
     low = lax.broadcasted_iota(I32, own_ref.shape[1:], 1) < half
-    for block, (n_ref, l_ref) in enumerate(((own_n_ref, lo_ref), (other_n_ref, lt_ref))):
+    for block, (n_ref, l_ref) in enumerate(((one_n_ref, one_l_ref),)):
         count = n_ref[2 * slots]
         for k in range(room):
             order[k] = -1
@@ -186,29 +186,29 @@
             w_ref[j, 2 * side:, q * side:(q + 1) * side] = f_ref[q * quarter:(q + 1) * quarter, :]
 
 
-def near_kernel(meta_ref, lo_ref, lt_ref, *refs):
+def near_kernel(mo_ref, mt_ref, lo_ref, lt_ref, *refs):
     *given, po_ref, pt_ref, blocks, sems = refs
-    room = meta_ref.shape[1] - 2
+    room = mo_ref.shape[1] - 2
     copies = bring(given, blocks, sems)
     po_ref[...] = jnp.zeros_like(po_ref)
     pt_ref[...] = jnp.zeros_like(pt_ref)
     for copy in copies:
         copy.wait()
-    add_turns(meta_ref, 1, 0, meta_ref[1, room], lt_ref, blocks, pt_ref)
-    add_turns(meta_ref, 0, 0, meta_ref[0, room], lo_ref, blocks, po_ref)
-
-
-def far_kernel(meta_ref, lo_ref, lt_ref, no_ref, nt_ref, *refs):
+    add_turns(mt_ref, 0, 0, mt_ref[0, room], lt_ref, blocks, pt_ref)
+    add_turns(mo_ref, 0, 0, mo_ref[0, room], lo_ref, blocks, po_ref)
+
+
+def far_kernel(mo_ref, mt_ref, lo_ref, lt_ref, no_ref, nt_ref, *refs):
     *given, po_ref, pt_ref, acc, blocks, sems = refs
-    room = meta_ref.shape[1] - 2
+    room = mo_ref.shape[1] - 2
     copies = bring(given, blocks, sems)
     acc[...] = nt_ref[...]
     po_ref[...] = no_ref[...]
     for copy in copies:
         copy.wait()
-    add_turns(meta_ref, 1, meta_ref[1, room + 1], room // STEP, lt_ref, blocks, acc)
+    add_turns(mt_ref, 0, mt_ref[0, room + 1], room // STEP, lt_ref, blocks, acc)
     pt_ref[...] = acc[...].astype(BF16)
-    add_turns(meta_ref, 0, meta_ref[0, room + 1], room // STEP, lo_ref, blocks, po_ref)
+    add_turns(mo_ref, 0, mo_ref[0, room + 1], room // STEP, lo_ref, blocks, po_ref)
 
 
 def join_kernel(own_ref, came_ref, out_ref):
@@ -342,29 +342,35 @@
     by_distance = {0: line}
     for hops in (2, -2, 1, -1):
         by_distance[-hops % NY] = pass_on(line, hops, hops)
+    where = jnp.concatenate([jnp.stack([core, here]).astype(I32), jnp.array(RING, I32)])
     turns = (slots + 2 * STEP - 2) // STEP
     placed = jax.ShapeDtypeStruct((turns * STEP // 2, rows, side), BF16)
-    left_own, left_other, meta = call(
-        place_kernel,
-        "place",
-        (placed, placed, jax.ShapeDtypeStruct((2, turns * STEP + 2), I32)),
-        [SMEM, SMEM, SMEM, ANY, ANY],
-        (VMEM, VMEM, SMEM),
-        [
-            pltpu.SMEM((turns * STEP,), I32),
-            pltpu.VMEM((2, *tiles.shape), BF16),
-            pltpu.SemaphoreType.DMA((2,)),
-        ],
-        10,
-        10**7,
-        7 * 10**6,
-        jnp.concatenate([jnp.stack([core, here]).astype(I32), jnp.array(RING, I32)]),
-        numbers,
-        other_numbers,
-        tiles,
-        other_tiles,
-    )
-
+
+    def place(of_numbers, of_tiles):
+        return call(
+            place_kernel,
+            "place",
+            (placed, jax.ShapeDtypeStruct((1, turns * STEP + 2), I32)),
+            [SMEM, SMEM, ANY],
+            (VMEM, SMEM),
+            [
+                pltpu.SMEM((turns * STEP,), I32),
+                pltpu.VMEM((1, *tiles.shape), BF16),
+                pltpu.SemaphoreType.DMA((1,)),
+            ],
+            8,
+            10**7,
+            4 * 10**6,
+            where,
+            of_numbers,
+            of_tiles,
+        )
+
+    left_own, meta_own = place(numbers, tiles)
+    left_other, meta_other = place(other_numbers, other_tiles)
+    by_distance[2], by_distance[6], meta_own = lax.optimization_barrier(
+        (by_distance[2], by_distance[6], meta_own)
+    )
     across = jnp.where(here % 2 == 0, by_distance[2], by_distance[6])
     arrived, across = lax.optimization_barrier(([by_distance[d] for d in NEAR[1:3]], across))
     by_distance.update(zip(NEAR[1:3], arrived))
@@ -378,7 +384,7 @@
         near_kernel,
         "near",
         (whole, whole),
-        [SMEM, VMEM, VMEM] + [ANY] * len(NEAR),
+        [SMEM, SMEM, VMEM, VMEM] + [ANY] * len(NEAR),
         (VMEM, VMEM),
         [
             pltpu.VMEM((len(NEAR) * line_size, quarter, side), BF16),
@@ -387,7 +393,8 @@
         20,
         flops,
         8 * 10**6,
-        meta,
+        meta_own,
+        meta_other,
         left_own,
         left_other,
         *[by_distance[d] for d in NEAR],
@@ -396,7 +403,7 @@
         far_kernel,
         "far",
         (whole, jax.ShapeDtypeStruct((rows, width), BF16)),
-        [SMEM, VMEM, VMEM, VMEM, VMEM] + [ANY] * len(FAR),
+        [SMEM, SMEM, VMEM, VMEM, VMEM, VMEM] + [ANY] * len(FAR),
         (VMEM, VMEM),
         [
             pltpu.VMEM((rows, width), F32),
@@ -406,7 +413,8 @@
         20,
         flops // 2,
         6 * 10**6,
-        meta,
+        meta_own,
+        meta_other,
         left_own,
         left_other,
         near_own,

time: 154 us -> 154 us (level)
  blocking collectives: 48 us -> 49.9 us
  waiting for transfers between devices: 19.8 us -> 18 us
    ppermute x7, starting transfers between devices: 30.4 us -> 27.9 us  [pass_on(): return lax.ppermute(value, AXES, pairs)]
    all_to_all x4, blocking collectives: 48 us -> 49.9 us  [exchange(): lax.all_to_all(pieces, AXES, 0, 0, axis_index_groups=groups_, tiled=True)]
    pallas_call x11 -> x12, Pallas kernels: 21.6 us -> 21.1 us  [call(): pl.pallas_call(kernel, out_shape=out_shape, in_specs=in_specs, out_specs=...]
  transfers between devices with their start and end apart: 13 -> 13, of which waited for: 4 -> 5; matrix products, arithmetic and copies ran while one was open for 0% -> 1% of each run, Pallas kernels for 11% -> 11%
where the time goes in v9:
time: 154 us; the launch traced here: 153 us
  starting transfers between devices  60.6 us (39%)
  blocking collectives  49.9 us (32%)
  Pallas kernels  21.1 us (14%)
  waiting for transfers between devices  18 us (12%)
  between operations  1.61 us (1%)
    all_to_all x4, blocking collectives, exchange(): lax.all_to_all(pieces, AXES, 0, 0, axis_index_groups=groups_, tiled=True)  49.9 us
    ppermute x7, starting transfers between devices, pass_on(): return lax.ppermute(value, AXES, pairs)  27.9 us
    pallas_call x12, Pallas kernels, call(): pl.pallas_call(kernel, out_shape=out_shape, in_specs=in_specs, out_specs=...  21.1 us
    all_to_all x3, starting transfers between devices, exchange(): lax.all_to_all(pieces, AXES, 0, 0, axis_index_groups=groups_, tiled=True)  18.4 us
    all_to_all x3, waiting for transfers between devices, exchange(): lax.all_to_all(pieces, AXES, 0, 0, axis_index_groups=groups_, tiled=True)  16.4 us
    ppermute x3, starting transfers between devices, swap_cores(): return lax.ppermute(value, AXES, OTHER_CORE)  14.4 us
  transfers between devices with their start and end apart: 13, of which 5 were waited for; matrix products, arithmetic and copies ran while one was open for 1% of the time, Pallas kernels for 11%

profile of v9, /device:TPU:1, one launch (start us, length us, event | category | flops | bytes accessed | tf_op | source)
XLA Modules:
  0.0 152.6 jit_solution(3282614462034922093)
XLA Ops:
  0.7 1.7 %spread.1 = bf16[32,64,128]{2,1,0:T(8,128)(2,1)} custom-call(bf16[256,128]{1,0:T(8,128)(2,1)} %f_ref.1), custom_call_target="tpu_custom_call" | custom-call | flops 100000 | bytes 1000000 | tf_op jit(solution)/shard_map/spread/pallas_call | solution.py:66
  2.4 10.6 %all-to-all-start = ((bf16[32,64,128]{2,1,0:T(8,128)(2,1)}), bf16[32,64,128]{2,1,0:T(8,128)(2,1)}, u32[]{:S(2)}, u32[]{:S(2)}) async-start(bf16[32,64,128]{2,1,0:T(8,128)(2,1)} %spread.1), calls=%async_computation | async-start | bytes 1048576 | tf_op jit(solution)/shard_map/all_to_all | solution.py:49
  13.1 6.1 %collective-permute-start.3 = (bf16[48,128,128]{2,1,0:T(8,128)(2,1)}, bf16[48,128,128]{2,1,0:T(8,128)(2,1)}, u32[]{:S(2)}, u32[]{:S(2)}) collective-permute-start(bf16[48,128,128]{2,1,0:T(8,128)(2,1)} %bitcast.6.own_ref), channel_id=1, source_target_pairs={{0,4},{1,5},{2,6},{3,7},{4,0},{5,1},{6,2},{7,3},{8,12},{9,13},{10,... | collective-permute-start | bytes 4718600 | tf_op jit(solution)/shard_map/ppermute | solution.py:53
  19.9 1.9 %collective-permute-start = (s32[97]{0:T(128)S(1)}, s32[97]{0:T(128)S(1)}, u32[]{:S(2)}, u32[]{:S(2)}) collective-permute-start(s32[97]{0:T(128)S(1)} %pad_add_fusion.one_n_ref), channel_id=1, source_target_pairs={{0,4},{1,5},{2,6},{3,7},{4,0},{5,1},{6,2},{7,3},{8,12},{9,13},{10,... | collective-permute-start | bytes 1172 | tf_op jit(solution)/shard_map/ppermute | solution.py:53
  21.8 2.2 %pack.1 = bf16[4,320,512]{2,1,0:T(8,128)(2,1)} custom-call(bf16[128,512]{1,0:T(8,128)(2,1)} %nw_from.1, bf16[128,512]{1,0:T(8,128)(2,1)} %rw_from.1, bf16[256,128]{1,0:T(8,128)(2,1)} %f_ref.1), custom_call_target="tpu_custom_call" | custom-call | flops 100000 | bytes 2000000 | tf_op jit(solution)/shard_map/pack/pallas_call | solution.py:66
  24.0 1.9 %all-to-all-done.refs_0_ = bf16[32,64,128]{2,1,0:T(8,128)(2,1)} async-done(((bf16[32,64,128]{2,1,0:T(8,128)(2,1)}), bf16[32,64,128]{2,1,0:T(8,128)(2,1)}, u32[]{:S(2)}, u32[]{:S(2)}) %all-to-all-start) | async-done | bytes 524320 | tf_op jit(solution)/shard_map/all_to_all | solution.py:49
  25.8 5.7 %collective-permute-start.2 = (bf16[32,64,128]{2,1,0:T(8,128)(2,1)}, bf16[32,64,128]{2,1,0:T(8,128)(2,1)}, u32[]{:S(2)}, u32[]{:S(2)}) collective-permute-start(bf16[32,64,128]{2,1,0:T(8,128)(2,1)} %all-to-all-done.refs_0_), channel_id=1, source_target_pairs={{0,16},{1,17},{2,18},{3,19},{4,132},{5,133},{6,134},{7,135},{8,24}... | collective-permute-start | bytes 1572872 | tf_op jit(solution)/shard_map/ppermute | solution.py:62
  31.5 6.8 %collective-permute-start.1 = (bf16[32,64,128]{2,1,0:T(8,128)(2,1)}, bf16[32,64,128]{2,1,0:T(8,128)(2,1)}, u32[]{:S(2)}, u32[]{:S(2)}) collective-permute-start(bf16[32,64,128]{2,1,0:T(8,128)(2,1)} %all-to-all-done.refs_0_), channel_id=1, source_target_pairs={{0,48},{1,49},{2,50},{3,51},{4,388},{5,389},{6,390},{7,391},{8,56}... | collective-permute-start | bytes 1572872 | tf_op jit(solution)/shard_map/ppermute | solution.py:62
  38.4 4.7 %place.2 = (bf16[28,256,128]{2,1,0:T(8,128)(2,1)S(1)}, s32[1,58]{1,0:T(1,128)S(1)}) custom-call(s32[18]{0:T(128)S(1)} %pad_add_fusion.1.where_ref, s32[97]{0:T(128)S(1)} %pad_add_fusion.one_n_ref, bf16[48,128,128]{2,1,0:T(8,128)(2,1)} %bitcast.6.own_ref), custom_call_target="tpu_custom_call" | custom-call | flops 10000000 | bytes 4000000 | tf_op jit(solution)/shard_map/place/pallas_call | solution.py:66
  43.2 3.2 %collective-permute-start.5 = (bf16[32,64,128]{2,1,0:T(8,128)(2,1)}, bf16[32,64,128]{2,1,0:T(8,128)(2,1)}, u32[]{:S(2)}, u32[]{:S(2)}) collective-permute-start(bf16[32,64,128]{2,1,0:T(8,128)(2,1)} %all-to-all-done.refs_0_), channel_id=1, source_target_pairs={{0,56},{1,57},{2,58},{3,59},{4,452},{5,453},{6,454},{7,455},{8,0},... | collective-permute-start | bytes 1572872 | tf_op jit(solution)/shard_map/ppermute | solution.py:62
  46.4 2.1 %collective-permute-start.4 = (bf16[32,64,128]{2,1,0:T(8,128)(2,1)}, bf16[32,64,128]{2,1,0:T(8,128)(2,1)}, u32[]{:S(2)}, u32[]{:S(2)}) collective-permute-start(bf16[32,64,128]{2,1,0:T(8,128)(2,1)} %all-to-all-done.refs_0_), channel_id=1, source_target_pairs={{0,8},{1,9},{2,10},{3,11},{4,68},{5,69},{6,70},{7,71},{8,16},{9,17... | collective-permute-start | bytes 1572872 | tf_op jit(solution)/shard_map/ppermute | solution.py:62
  48.5 3.6 %all-to-all-start.2 = ((bf16[4,320,512]{2,1,0:T(8,128)(2,1)}), bf16[4,320,512]{2,1,0:T(8,128)(2,1)S(1)}, u32[]{:S(2)}, u32[]{:S(2)}) async-start(bf16[4,320,512]{2,1,0:T(8,128)(2,1)} %pack.1), calls=%async_computation.2 | async-start | bytes 2621440 | tf_op jit(solution)/shard_map/all_to_all | solution.py:49
  52.1 1.1 broadcast_select_fusion
  53.2 3.6 %collective-permute-start.6 = (bf16[32,64,128]{2,1,0:T(8,128)(2,1)S(1)}, bf16[32,64,128]{2,1,0:T(8,128)(2,1)S(1)}, u32[]{:S(2)}, u32[]{:S(2)}) collective-permute-start(bf16[32,64,128]{2,1,0:T(8,128)(2,1)S(1)} %broadcast_select_fusion), channel_id=1, source_target_pairs={{0,48},{1,49},{2,50},{3,51},{4,388},{5,389},{6,390},{7,391},{8,24}... | collective-permute-start | bytes 1572872 | tf_op jit(solution)/shard_map/ppermute | solution.py:62
  56.8 3.7 %collective-permute-start.7 = (bf16[32,64,128]{2,1,0:T(8,128)(2,1)}, bf16[32,64,128]{2,1,0:T(8,128)(2,1)S(1)}, u32[]{:S(2)}, u32[]{:S(2)}) collective-permute-start(bf16[32,64,128]{2,1,0:T(8,128)(2,1)} %collective-permute-done.2.refs_1_), channel_id=1, source_target_pairs={{0,8},{1,9},{2,10},{3,11},{4,68},{5,69},{6,70},{7,71},{8,16},{9,17... | collective-permute-start | bytes 1572872 | tf_op jit(solution)/shard_map/ppermute | solution.py:62
  60.5 2.8 %collective-permute-start.8 = (bf16[32,64,128]{2,1,0:T(8,128)(2,1)}, bf16[32,64,128]{2,1,0:T(8,128)(2,1)S(1)}, u32[]{:S(2)}, u32[]{:S(2)}) collective-permute-start(bf16[32,64,128]{2,1,0:T(8,128)(2,1)} %collective-permute-done.1.refs_2_), channel_id=1, source_target_pairs={{0,56},{1,57},{2,58},{3,59},{4,452},{5,453},{6,454},{7,455},{8,0},... | collective-permute-start | bytes 1572872 | tf_op jit(solution)/shard_map/ppermute | solution.py:62
  63.3 3.3 %place.3 = (bf16[28,256,128]{2,1,0:T(8,128)(2,1)S(1)}, s32[1,58]{1,0:T(1,128)S(1)}) custom-call(s32[18]{0:T(128)S(1)} %pad_add_fusion.1.where_ref, s32[97]{0:T(128)S(1)} %collective-permute-done.one_n_ref, bf16[48,128,128]{2,1,0:T(8,128)(2,1)} %collective-permute-done.3.own_ref), custom_call_target="tpu_custom_call" | custom-call | flops 10000000 | bytes 4000000 | tf_op jit(solution)/shard_map/place/pallas_call | solution.py:66
  66.6 3.8 %near.1 = (f32[256,512]{1,0:T(8,128)S(1)}, f32[256,512]{1,0:T(8,128)S(1)}) custom-call(s32[1,58]{1,0:T(1,128)S(1)} %get-tuple-element.28.mo_ref, s32[1,58]{1,0:T(1,128)S(1)} %get-tuple-element.30.mt_ref, bf16[28,256,128]{2,1,0:T(8,128)(2,1)S(1)} %get-tuple-element.31.lo_ref, bf16[28,256,128]{2,1,0:T(8,128)(2,1)S(1)} %get-tuple-element.32.lt_ref, ...), custom_call_target="tpu_custom_call" | custom-call | flops 805306368 | bytes 8000000 | tf_op jit(solution)/shard_map/near/pallas_call | solution.py:66
  70.5 0.3 collective-permute-done.7.refs_1_
  70.8 0.2 collective-permute-done.8.refs_2_
  71.0 1.7 %far.1 = (f32[256,512]{1,0:T(8,128)S(1)}, bf16[256,512]{1,0:T(8,128)(2,1)S(1)}) custom-call(s32[1,58]{1,0:T(1,128)S(1)} %get-tuple-element.28.mo_ref, s32[1,58]{1,0:T(1,128)S(1)} %get-tuple-element.30.mt_ref, bf16[28,256,128]{2,1,0:T(8,128)(2,1)S(1)} %get-tuple-element.31.lo_ref, bf16[28,256,128]{2,1,0:T(8,128)(2,1)S(1)} %get-tuple-element.32.lt_ref, ...), custom_call_target="tpu_custom_call" | custom-call | flops 402653184 | bytes 6000000 | tf_op jit(solution)/shard_map/far/pallas_call | solution.py:66
  72.7 6.4 %collective-permute-start.9 = (bf16[256,512]{1,0:T(8,128)(2,1)S(1)}, bf16[256,512]{1,0:T(8,128)(2,1)S(1)}, u32[]{:S(2)}, u32[]{:S(2)}) collective-permute-start(bf16[256,512]{1,0:T(8,128)(2,1)S(1)} %get-tuple-element.41), channel_id=1, source_target_pairs={{0,4},{1,5},{2,6},{3,7},{4,0},{5,1},{6,2},{7,3},{8,12},{9,13},{10,... | collective-permute-start | bytes 786440 | tf_op jit(solution)/shard_map/ppermute | solution.py:53
  79.1 1.1 collective-permute-done.9.came_ref
  80.2 1.1 join.1
  81.3 4.2 %all-to-all-start.1 = ((bf16[4,256,512]{2,1,0:T(8,128)(2,1)}), bf16[4,256,512]{2,1,0:T(8,128)(2,1)S(1)}, u32[]{:S(2)}, u32[]{:S(2)}) async-start(bf16[4,256,512]{2,1,0:T(8,128)(2,1)} %join.1), calls=%async_computation.1 | async-start | bytes 2097152 | tf_op jit(solution)/shard_map/all_to_all | solution.py:49
  85.5 14.5 %all-to-all-done.1.a_ref = bf16[4,256,512]{2,1,0:T(8,128)(2,1)S(1)} async-done(((bf16[4,256,512]{2,1,0:T(8,128)(2,1)}), bf16[4,256,512]{2,1,0:T(8,128)(2,1)S(1)}, u32[]{:S(2)}, u32[]{:S(2)}) %all-to-all-start.1) | async-done | bytes 1048608 | tf_op jit(solution)/shard_map/all_to_all | solution.py:49
  100.0 1.6 %dense.1 = (bf16[256,128]{1,0:T(8,128)(2,1)}, bf16[12,128,128]{2,1,0:T(8,128)(2,1)S(1)}) custom-call(s32[1]{0:T(128)} %bitcast.n_ref, bf16[4,256,512]{2,1,0:T(8,128)(2,1)S(1)} %all-to-all-done.1.a_ref, bf16[4,320,512]{2,1,0:T(8,128)(2,1)S(1)} %all-to-all-done.2.w_ref, bf16[256,128]{1,0:T(8,128)(2,1)S(1)} %copy-done, bf16[256,512]{1,0:T(8,128)(2,1)S(1)} %copy-done.2, ...), custom_call_target="tpu_custom_call" | custom-call | flops 805306368 | bytes 5000000 | tf_op jit(solution)/shard_map/dense/pallas_call | solution.py:66
  101.6 12.5 %all_to_all.35.in_ref = bf16[8,192,128]{2,1,0:T(8,128)(2,1)S(1)} all-to-all(bf16[8,192,128]{2,1,0:T(8,128)(2,1)S(1)} %bitcast.11), channel_id=1, replica_groups={{0,4,8,12,64,68,72,76},{1,5,9,13,65,69,73,77},{2,6,10,14,66,70,74,78},{..., dimensions={0} | all-to-all | bytes 786432 | tf_op jit(solution)/shard_map/all_to_all | solution.py:49
  114.2 11.8 %all_to_all.36.in_ref = bf16[4,192,128]{2,1,0:T(8,128)(2,1)S(1)} all-to-all(bf16[4,192,128]{2,1,0:T(8,128)(2,1)S(1)} %total.3), channel_id=1, replica_groups={{0,16,32,48},{1,17,33,49},{2,18,34,50},{3,19,35,51},{4,20,36,52},{5,21,..., dimensions={0} | all-to-all | bytes 393216 | tf_op jit(solution)/shard_map/all_to_all | solution.py:49
  126.1 11.4 %all_to_all.37.in_ref = bf16[4,192,128]{2,1,0:T(8,128)(2,1)S(1)} all-to-all(bf16[4,192,128]{2,1,0:T(8,128)(2,1)S(1)} %total.4), channel_id=1, replica_groups={{0,128,256,384},{1,129,257,385},{2,130,258,386},{3,131,259,387},{4,132,..., dimensions={0} | all-to-all | bytes 393216 | tf_op jit(solution)/shard_map/all_to_all | solution.py:49
  137.5 14.2 %all_to_all.38 = bf16[8,192,128]{2,1,0:T(8,128)(2,1)S(1)} all-to-all(bf16[8,192,128]{2,1,0:T(8,128)(2,1)S(1)} %total.5), channel_id=1, replica_groups={{0,4,8,12,64,68,72,76},{1,5,9,13,65,69,73,77},{2,6,10,14,66,70,74,78},{..., dimensions={0} | all-to-all | bytes 786432 | tf_op jit(solution)/shard_map/all_to_all | solution.py:49
  151.7 0.9 last.1
  (25 shorter events, 0.3 us)
Async XLA Ops:
  0.6 37.7 %copy-start.5 = (s32[16]{0:T(128)S(1)}, s32[16]{0:T(128)}, u32[]{:S(2)}) copy-start(s32[16]{0:T(128)} %constant.61.clone) | copy-start | bytes 196
  0.6 19.1 %copy-start.3 = (s32[1,1,48]{2,1,0:T(1,128)S(1)}, s32[1,1,48]{2,1,0:T(1,128)}, u32[]{:S(2)}) copy-start(s32[1,1,48]{2,1,0:T(1,128)} %param.13) | copy-start | bytes 580
  0.7 19.1 %copy-start.4 = (s32[1,1,48]{2,1,0:T(1,128)S(1)}, s32[1,1,48]{2,1,0:T(1,128)}, u32[]{:S(2)}) copy-start(s32[1,1,48]{2,1,0:T(1,128)} %param.12) | copy-start | bytes 580
  2.4 23.4 %all-to-all-start = ((bf16[32,64,128]{2,1,0:T(8,128)(2,1)}), bf16[32,64,128]{2,1,0:T(8,128)(2,1)}, u32[]{:S(2)}, u32[]{:S(2)}) async-start(bf16[32,64,128]{2,1,0:T(8,128)(2,1)} %spread.1), calls=%async_computation | async-start | bytes 1048576 | tf_op jit(solution)/shard_map/all_to_all | solution.py:49
  13.1 47.5 %collective-permute-start.3 = (bf16[48,128,128]{2,1,0:T(8,128)(2,1)}, bf16[48,128,128]{2,1,0:T(8,128)(2,1)}, u32[]{:S(2)}, u32[]{:S(2)}) collective-permute-start(bf16[48,128,128]{2,1,0:T(8,128)(2,1)} %bitcast.6.own_ref), channel_id=1, source_target_pairs={{0,4},{1,5},{2,6},{3,7},{4,0},{5,1},{6,2},{7,3},{8,12},{9,13},{10,... | collective-permute-start | bytes 4718600 | tf_op jit(solution)/shard_map/ppermute | solution.py:53
  19.9 4.1 %collective-permute-start = (s32[97]{0:T(128)S(1)}, s32[97]{0:T(128)S(1)}, u32[]{:S(2)}, u32[]{:S(2)}) collective-permute-start(s32[97]{0:T(128)S(1)} %pad_add_fusion.one_n_ref), channel_id=1, source_target_pairs={{0,4},{1,5},{2,6},{3,7},{4,0},{5,1},{6,2},{7,3},{8,12},{9,13},{10,... | collective-permute-start | bytes 1172 | tf_op jit(solution)/shard_map/ppermute | solution.py:53
  25.8 26.2 %collective-permute-start.2 = (bf16[32,64,128]{2,1,0:T(8,128)(2,1)}, bf16[32,64,128]{2,1,0:T(8,128)(2,1)}, u32[]{:S(2)}, u32[]{:S(2)}) collective-permute-start(bf16[32,64,128]{2,1,0:T(8,128)(2,1)} %all-to-all-done.refs_0_), channel_id=1, source_target_pairs={{0,16},{1,17},{2,18},{3,19},{4,132},{5,133},{6,134},{7,135},{8,24}... | collective-permute-start | bytes 1572872 | tf_op jit(solution)/shard_map/ppermute | solution.py:62
  31.5 20.5 %collective-permute-start.1 = (bf16[32,64,128]{2,1,0:T(8,128)(2,1)}, bf16[32,64,128]{2,1,0:T(8,128)(2,1)}, u32[]{:S(2)}, u32[]{:S(2)}) collective-permute-start(bf16[32,64,128]{2,1,0:T(8,128)(2,1)} %all-to-all-done.refs_0_), channel_id=1, source_target_pairs={{0,48},{1,49},{2,50},{3,51},{4,388},{5,389},{6,390},{7,391},{8,56}... | collective-permute-start | bytes 1572872 | tf_op jit(solution)/shard_map/ppermute | solution.py:62
  43.2 23.5 %collective-permute-start.5 = (bf16[32,64,128]{2,1,0:T(8,128)(2,1)}, bf16[32,64,128]{2,1,0:T(8,128)(2,1)}, u32[]{:S(2)}, u32[]{:S(2)}) collective-permute-start(bf16[32,64,128]{2,1,0:T(8,128)(2,1)} %all-to-all-done.refs_0_), channel_id=1, source_target_pairs={{0,56},{1,57},{2,58},{3,59},{4,452},{5,453},{6,454},{7,455},{8,0},... | collective-permute-start | bytes 1572872 | tf_op jit(solution)/shard_map/ppermute | solution.py:62
  46.4 20.3 %collective-permute-start.4 = (bf16[32,64,128]{2,1,0:T(8,128)(2,1)}, bf16[32,64,128]{2,1,0:T(8,128)(2,1)}, u32[]{:S(2)}, u32[]{:S(2)}) collective-permute-start(bf16[32,64,128]{2,1,0:T(8,128)(2,1)} %all-to-all-done.refs_0_), channel_id=1, source_target_pairs={{0,8},{1,9},{2,10},{3,11},{4,68},{5,69},{6,70},{7,71},{8,16},{9,17... | collective-permute-start | bytes 1572872 | tf_op jit(solution)/shard_map/ppermute | solution.py:62
  48.5 32.8 %all-to-all-start.2 = ((bf16[4,320,512]{2,1,0:T(8,128)(2,1)}), bf16[4,320,512]{2,1,0:T(8,128)(2,1)S(1)}, u32[]{:S(2)}, u32[]{:S(2)}) async-start(bf16[4,320,512]{2,1,0:T(8,128)(2,1)} %pack.1), calls=%async_computation.2 | async-start | bytes 2621440 | tf_op jit(solution)/shard_map/all_to_all | solution.py:49
  53.2 17.3 %collective-permute-start.6 = (bf16[32,64,128]{2,1,0:T(8,128)(2,1)S(1)}, bf16[32,64,128]{2,1,0:T(8,128)(2,1)S(1)}, u32[]{:S(2)}, u32[]{:S(2)}) collective-permute-start(bf16[32,64,128]{2,1,0:T(8,128)(2,1)S(1)} %broadcast_select_fusion), channel_id=1, source_target_pairs={{0,48},{1,49},{2,50},{3,51},{4,388},{5,389},{6,390},{7,391},{8,24}... | collective-permute-start | bytes 1572872 | tf_op jit(solution)/shard_map/ppermute | solution.py:62
  56.8 14.0 %collective-permute-start.7 = (bf16[32,64,128]{2,1,0:T(8,128)(2,1)}, bf16[32,64,128]{2,1,0:T(8,128)(2,1)S(1)}, u32[]{:S(2)}, u32[]{:S(2)}) collective-permute-start(bf16[32,64,128]{2,1,0:T(8,128)(2,1)} %collective-permute-done.2.refs_1_), channel_id=1, source_target_pairs={{0,8},{1,9},{2,10},{3,11},{4,68},{5,69},{6,70},{7,71},{8,16},{9,17... | collective-permute-start | bytes 1572872 | tf_op jit(solution)/shard_map/ppermute | solution.py:62
  60.5 10.4 %collective-permute-start.8 = (bf16[32,64,128]{2,1,0:T(8,128)(2,1)}, bf16[32,64,128]{2,1,0:T(8,128)(2,1)S(1)}, u32[]{:S(2)}, u32[]{:S(2)}) collective-permute-start(bf16[32,64,128]{2,1,0:T(8,128)(2,1)} %collective-permute-done.1.refs_2_), channel_id=1, source_target_pairs={{0,56},{1,57},{2,58},{3,59},{4,452},{5,453},{6,454},{7,455},{8,0},... | collective-permute-start | bytes 1572872 | tf_op jit(solution)/shard_map/ppermute | solution.py:62
  72.7 7.5 %collective-permute-start.9 = (bf16[256,512]{1,0:T(8,128)(2,1)S(1)}, bf16[256,512]{1,0:T(8,128)(2,1)S(1)}, u32[]{:S(2)}, u32[]{:S(2)}) collective-permute-start(bf16[256,512]{1,0:T(8,128)(2,1)S(1)} %get-tuple-element.41), channel_id=1, source_target_pairs={{0,4},{1,5},{2,6},{3,7},{4,0},{5,1},{6,2},{7,3},{8,12},{9,13},{10,... | collective-permute-start | bytes 786440 | tf_op jit(solution)/shard_map/ppermute | solution.py:53
  80.2 19.8 %copy-start = (bf16[256,128]{1,0:T(8,128)(2,1)S(1)}, bf16[256,128]{1,0:T(8,128)(2,1)}, u32[]{:S(2)}) copy-start(bf16[256,128]{1,0:T(8,128)(2,1)} %f_ref.1) | copy-start | bytes 196612
  80.2 19.8 %copy-start.1 = (bf16[512,512]{1,0:T(8,128)(2,1)S(1)}, bf16[512,512]{1,0:T(8,128)(2,1)}, u32[]{:S(2)}) copy-start(bf16[512,512]{1,0:T(8,128)(2,1)} %ow_ref.1) | copy-start | bytes 1572868
  80.2 19.8 %copy-start.2 = (bf16[256,512]{1,0:T(8,128)(2,1)S(1)}, bf16[256,512]{1,0:T(8,128)(2,1)}, u32[]{:S(2)}) copy-start(bf16[256,512]{1,0:T(8,128)(2,1)} %cot_ref.1) | copy-start | bytes 786436
  81.3 18.7 %all-to-all-start.1 = ((bf16[4,256,512]{2,1,0:T(8,128)(2,1)}), bf16[4,256,512]{2,1,0:T(8,128)(2,1)S(1)}, u32[]{:S(2)}, u32[]{:S(2)}) async-start(bf16[4,256,512]{2,1,0:T(8,128)(2,1)} %join.1), calls=%async_computation.1 | async-start | bytes 2097152 | tf_op jit(solution)/shard_map/all_to_all | solution.py:49
